TPU v7x, 32 devices: a whole 2x2x4 slice. The times are simulated.
32 devices in a mesh: group: 2 (over y), batch: 8 (over z, x), tensor: 2 (over core).
Axes of the slice: x: 2, y: 2, z: 4, core: 2. Of those that a mesh axis runs over, the one named last changes fastest.
Arguments:
- features: bfloat16 [32, 8192], P(('group', 'batch'), 'tensor'), parts along dimension 0, may hold values from -6 to 6
- up_weight: bfloat16 [8192, 32768], P('tensor', 'batch'), may hold values from -0.0625 to 0.0625
- adapter_down_weight: bfloat16 [64, 8192, 16], P(('group', 'batch'), 'tensor'), parts along dimension 0, may hold values from -0.0625 to 0.0625
- adapter_up_weight: bfloat16 [64, 16, 32768], P(('group', 'batch'), 'tensor'), parts along dimension 0, may hold values from -1.5 to 1.5
- request_adapter: int32 [32], P('group'), parts along dimension 0, may hold values from 0 to 31, as said below
- adapter_storage_row: int32 [64], P('group'), parts along dimension 0, may hold values from 0 to 31, as said below
Outputs:
- hidden: bfloat16 [32, 32768], P('group', ('batch', 'tensor')), parts along dimension 0
There are 2 independent parts, one for each index of `group`. A program takes and returns all parts, laid end to end along the dimension named above; an argument that names none is the same for every part. Nothing has to cross between parts.
Inputs may be any that keep to these rules, and one draw needn't show every extreme that they name: `request_adapter`: the requests whose adapters have storage rows in [o * 4, (o + 1) * 4) number at most 8 for every o, and exactly 8 for one o. A permutation: adapter a is stored in row adapter_storage_row[a] of adapter_down_weight and adapter_up_weight.
All inputs are finite; a program needn't handle non-finite values.
Results may differ from a plain program's by a relative error of at most 0.0049.
Values may be sent and summed in bfloat16 or wider, within the bound.
No kernel may reach another device: no remote copies, remote signals or barrier semaphores. Data moves between devices by JAX's collectives and lax.ppermute only.
A program may use at most 128 MiB of HBM per device.

v0:
```python
import jax
import jax.numpy as jnp
from jax import lax
from jax.sharding import PartitionSpec as P

OWN_MOST = 8


def per_device(
    features,
    up_weight,
    adapter_down_weight,
    adapter_up_weight,
    request_adapter,
    adapter_storage_row,
):
    batches = lax.axis_size("batch")
    own_batch = lax.axis_index("batch")
    adapters_here = adapter_down_weight.shape[0]
    rank_half = adapter_up_weight.shape[1]
    requests = request_adapter.shape[0]
    slot_of = adapter_storage_row[request_adapter]
    owner_of = slot_of // adapters_here
    local_pick = slot_of - owner_of * adapters_here
    gathered = lax.all_gather(features, "batch", axis=0, tiled=True)
    plain_output = jnp.dot(gathered, up_weight, preferred_element_type=jnp.float32)
    adapter_range = jnp.arange(adapters_here, dtype=jnp.int32)
    owner_hits = (owner_of[:, None] == jnp.arange(batches, dtype=jnp.int32)[None, :]).astype(
        jnp.int32
    )
    before = jnp.cumsum(owner_hits, axis=0) - owner_hits
    rank_of = jnp.sum(before * owner_hits, axis=1)
    is_mine = owner_of == own_batch
    target = jnp.where(is_mine, rank_of, OWN_MOST)
    chosen = (
        jnp.zeros((OWN_MOST,), jnp.int32)
        .at[target]
        .set(jnp.arange(requests, dtype=jnp.int32), mode="drop")
    )
    filled = jnp.zeros((OWN_MOST,), jnp.float32).at[target].set(1.0, mode="drop")
    selected_rows = gathered[chosen]
    selector = (local_pick[chosen][:, None] == adapter_range[None, :]).astype(jnp.float32) * filled[
        :, None
    ]
    shrink_parts = jnp.einsum(
        "et,hts->ehs", selected_rows, adapter_down_weight, preferred_element_type=jnp.float32
    )
    shrink_term = jnp.sum(shrink_parts * selector[:, :, None], axis=1)
    shrunk_half = lax.psum_scatter(shrink_term, "tensor", scatter_dimension=1, tiled=True).astype(
        jnp.bfloat16
    )
    broadcast_rows = (selector[:, :, None] * shrunk_half.astype(jnp.float32)[:, None, :]).astype(
        jnp.bfloat16
    )
    broadcast_rows = broadcast_rows.reshape(OWN_MOST, adapters_here * rank_half)
    flattened_up_rows = adapter_up_weight.reshape(
        adapters_here * rank_half, adapter_up_weight.shape[2]
    )
    adapter_update = jnp.dot(broadcast_rows, flattened_up_rows, preferred_element_type=jnp.float32)
    received_rows = lax.all_to_all(adapter_update, "batch", split_axis=1, concat_axis=0, tiled=True)
    storage_index = owner_of * OWN_MOST + rank_of
    adapter_output = received_rows[storage_index]
    total_output = lax.psum_scatter(
        plain_output + adapter_output, "tensor", scatter_dimension=1, tiled=True
    )
    return jnp.square(jnp.maximum(total_output, 0.0)).astype(jnp.bfloat16)


def solution(mesh):
    in_specs = (
        P(("group", "batch"), "tensor"),
        P("tensor", "batch"),
        P(("group", "batch"), "tensor", None),
        P(("group", "batch"), "tensor", None),
        P("group"),
        P("group"),
    )
    out_specs = P("group", ("batch", "tensor"))
    return jax.shard_map(
        per_device, mesh=mesh, in_specs=in_specs, out_specs=out_specs, check_vma=False
    )
```

profile of v0, /device:TPU:0, one launch (start us, length us, event | category | flops | bytes accessed | tf_op | source)
XLA Modules:
  0.0 111.3 jit_solution(1248414503346950429)
XLA Ops:
  6.5 0.0 copy-start
  6.5 0.0 copy-start.2
  6.5 0.0 copy-start.1
  6.5 0.8 compare_select_fusion.3
  7.4 1.3 %gather_fusion = s32[16]{0:T(128)S(1)} fusion(s32[32]{0:T(128)} %param.11, s32[1024]{0:T(1024)S(1)} %pad_clamp_fusion.2), kind=kCustom, calls=%fused_computation | custom fusion | bytes 192 | tf_op jit(solution)/shard_map/gather | solution.py:22
  8.7 0.1 fusion.5
  8.8 0.2 select_reduce_fusion
  9.0 0.6 scatter_custom_fusion
  9.7 32.5 %all-gather = bf16[8,2,4096]{2,1,0:T(2,128)(2,1)S(1)} all-gather(bf16[1,2,4096]{2,1,0:T(2,128)(2,1)} %bitcast.46), channel_id=1, replica_groups=mesh['group'=2,'batch'=8,'tensor'=2] {'batch'}, dimensions={0}, use_global_device_ids=true | all-gather | bytes 147456 | tf_op jit(solution)/shard_map/all_gather | solution.py:25
  42.2 0.1 reshape.204
  42.2 0.6 gather_fusion.1
  42.9 0.6 gather_fusion.2
  43.5 0.6 scatter_custom_fusion.1
  44.1 0.1 copy.10
  44.2 0.0 copy-done
  44.2 0.7 fusion.3
  44.9 2.5 %all-reduce = bf16[8,16]{1,0:T(8,128)(2,1)S(1)} all-reduce(f32[8,16]{1,0:T(8,128)S(1)} %fusion.3), channel_id=2, replica_groups=mesh['group'=2,'batch'=8,'tensor'=2] {'tensor'}, use_global_device_ids=true, to_apply=%region_5.6.clone | all-reduce | flops 128 | bytes 768
  47.4 0.0 copy-done.2
  47.4 0.6 dynamic-slice
  48.6 0.1 fusion.6
  48.7 0.1 multiply_convert_fusion.1
  48.8 0.1 reshape.206
  48.9 0.0 copy-done.1
  48.9 1.4 %fusion = f32[8,8,4096]{2,0,1:T(8,128)} fusion(bf16[8,32,1]{1,0,2:T(8,128)(2,1)S(1)} %reshape.206, bf16[4,8,8,4096]{3,2,1,0:T(8,128)(2,1)S(1)} %bitcast.45), kind=kOutput, calls=%fused_computation.7 | convolution fusion | flops 16777216 | bytes 3146240 | tf_op jit(solution)/shard_map/dot_general | solution.py:59
  50.3 5.5 %all-to-all-start = ((f32[8,8,4096]{2,0,1:T(8,128)}), f32[8,8,4096]{2,0,1:T(8,128)S(1)}, u32[]{:S(2)}, u32[]{:S(2)}) async-start(f32[8,8,4096]{2,0,1:T(8,128)} %fusion), calls=%async_computation | async-start | bytes 2097152 | tf_op jit(solution)/shard_map/all_to_all | solution.py:60
  55.7 0.0 reduce-scatter.3.cloned.1.call-start
  55.8 26.0 %all-to-all-done = f32[8,8,4096]{2,0,1:T(8,128)S(1)} async-done(((f32[8,8,4096]{2,0,1:T(8,128)}), f32[8,8,4096]{2,0,1:T(8,128)S(1)}, u32[]{:S(2)}, u32[]{:S(2)}) %all-to-all-start) | async-done | bytes 1048608 | tf_op jit(solution)/shard_map/all_to_all | solution.py:60
  81.8 0.6 gather_fusion.3
  82.5 13.5 %convolution_add_fusion = f32[16,4096]{1,0:T(8,128)} fusion(f32[16,4096]{1,0:T(8,128)S(1)} %gather_fusion.3, bf16[16,4096]{1,0:T(8,128)(2,1)S(1)} %reshape.204, bf16[4096,4096]{1,0:T(8,128)(2,1)} %param.7), kind=kOutput, calls=%fused_computation.6 | convolution fusion | flops 536936448 | bytes 34209792 | tf_op jit(solution)/shard_map/dot_general | solution.py:26
  96.0 0.0 reduce-scatter.3.cloned.1.call-update
  96.0 6.9 %reduce-scatter.3.cloned.1.call-done = f32[16,2048]{1,0:T(8,128)} async-done(((f32[16,4096]{1,0:T(8,128)}), f32[16,2048]{1,0:T(8,128)}) %reduce-scatter.3.cloned.1.call-update) | async-done | bytes 131088 | tf_op jit(solution)/shard_map/reduce_scatter | solution.py:63
  102.9 1.5 %multiply_convert_fusion = bf16[16,2048]{1,0:T(8,128)(2,1)} fusion(f32[16,2048]{1,0:T(8,128)} %reduce-scatter.3.cloned.1.call-done), kind=kLoop, calls=%fused_computation.12 | loop fusion | flops 98304 | bytes 196608 | tf_op jit(solution)/shard_map/convert_element_type | solution.py:66
  (10 shorter events, 0.1 us)
Async XLA Ops:
  6.5 37.7 %copy-start = (bf16[4,4096,16]{1,2,0:T(8,128)(2,1)S(1)}, bf16[4,4096,16]{1,2,0:T(8,128)(2,1)}, u32[]{:S(2)}) copy-start(bf16[4,4096,16]{1,2,0:T(8,128)(2,1)} %param.8) | copy-start | bytes 1572868
  6.5 40.9 %copy-start.2 = (u32[32]{0:T(128)S(1)}, u32[32]{0:T(128)}, u32[]{:S(2)}) copy-start(u32[32]{0:T(128)} %constant.52) | copy-start | bytes 388
  6.5 42.3 %copy-start.1 = (bf16[4,8,32768]{2,1,0:T(8,128)(2,1)S(1)}, bf16[4,8,32768]{2,1,0:T(8,128)(2,1)}, u32[]{:S(2)}) copy-start(bf16[4,8,32768]{2,1,0:T(8,128)(2,1)} %param.9) | copy-start | bytes 6291460
  50.3 31.6 %all-to-all-start = ((f32[8,8,4096]{2,0,1:T(8,128)}), f32[8,8,4096]{2,0,1:T(8,128)S(1)}, u32[]{:S(2)}, u32[]{:S(2)}) async-start(f32[8,8,4096]{2,0,1:T(8,128)} %fusion), calls=%async_computation | async-start | bytes 2097152 | tf_op jit(solution)/shard_map/all_to_all | solution.py:60
  55.7 47.2 %reduce-scatter.3.cloned.1.call-start = ((), (), s32[]{:S(2)}) async-start(), calls=%async_computation.2 | async-start | bytes 393216 | tf_op jit(solution)/shard_map/reduce_scatter | solution.py:63
Sparse Core Ops, SparseCore 0:
  96.2 6.7 reduce-scatter.2
where the time goes:
time: 112 us; the launch traced here: 111 us
  blocking collectives  35 us (31%)
  waiting for transfers between devices  33 us (29%)
  matrix products  15.6 us (14%)
  between operations  14.2 us (13%)
  starting transfers between devices  5.5 us (5%)
  local copies, waits for them, and re-layouts  5.25 us (5%)
  other arithmetic  2.85 us (3%)
    all_gather x1, blocking collectives, per_device(): gathered = lax.all_gather(features, 'batch', axis=0, tiled=True)  32.5 us
    all_to_all x1, waiting for transfers between devices, per_device(): lax.all_to_all(adapter_update, 'batch', split_axis=1, concat_axis=0, tile...  26 us
    dot_general x1, matrix products, per_device(): jnp.dot(gathered, up_weight, preferred_element_type=jnp.float32)  13.5 us
    reduce_scatter x1, waiting for transfers between devices, per_device(): lax.psum_scatter(plain_output + adapter_output, 'tensor', scatter_dimensi...  6.91 us
    all_to_all x1, starting transfers between devices, per_device(): lax.all_to_all(adapter_update, 'batch', split_axis=1, concat_axis=0, tile...  5.46 us
    unnamed x1, blocking collectives  2.46 us
  transfers between devices with their start and end apart: 2, of which 2 were waited for; matrix products, arithmetic and copies ran while one was open for 0% of the time, Pallas kernels for 0%

commit v1 on v0

v1 whole, which is shorter than its diff:
```python
import functools

import jax
import jax.numpy as jnp
from jax import lax
from jax.experimental import pallas as pl
from jax.experimental.pallas import tpu as pltpu
from jax.sharding import PartitionSpec as P

OWN_MOST = 8
LANES = 128
MIB = 1 << 20
F32 = jnp.float32
BF16 = jnp.bfloat16
VMEM = pltpu.VMEM


def whole(n):
    return [pl.BlockSpec(memory_space=VMEM)] * n


def in_vmem(x):
    return pltpu.with_memory_space_constraint(x, VMEM)


def slots_of(ra, sr):
    requests, adapters = ra.shape[1], sr.shape[1]
    same = lax.broadcasted_iota(jnp.int32, (requests, requests), 0) == lax.broadcasted_iota(
        jnp.int32, (requests, requests), 1
    )
    ra = jnp.sum(jnp.where(same, ra, 0), axis=1, keepdims=True)
    hit = lax.broadcasted_iota(jnp.int32, (requests, adapters), 1) == ra
    return jnp.sum(jnp.where(hit, sr, 0), axis=1, keepdims=True)


def ranks_of(mine):
    requests = mine.shape[0]
    earlier = lax.broadcasted_iota(jnp.int32, (requests, requests), 1) < lax.broadcasted_iota(
        jnp.int32, (requests, requests), 0
    )
    marks = jnp.broadcast_to(mine.astype(F32), (requests, LANES)).astype(BF16)
    return jnp.dot(earlier.astype(F32).astype(BF16), marks, preferred_element_type=F32)[:, :OWN_MOST]


def place_of(slot, owner, adapters_here):
    mine = (slot >= owner * adapters_here) & (slot < (owner + 1) * adapters_here)
    place = lax.broadcasted_iota(jnp.int32, (slot.shape[0], OWN_MOST), 1).astype(F32)
    return jnp.where((ranks_of(mine) == place) & mine, 1.0, 0.0).astype(BF16)


def shrink_kernel(g_ref, down_ref, x_ref, f_ref, rows_ref):
    batches, each, _ = g_ref.shape
    for b in range(batches):
        rows_ref[b * each : (b + 1) * each] = g_ref[b].astype(F32)
    f_ref[...] = rows_ref[...].astype(BF16)
    x_ref[...] = lax.dot_general(
        f_ref[...], down_ref[...], (((1,), (1,)), ((), ())), preferred_element_type=F32
    )


def delta_kernel(adapters_here, ra_ref, sr_ref, x_ref, xo_ref, up_ref, upo_ref, d_ref):
    batches, _, cols = d_ref.shape
    me = lax.axis_index("batch")
    core = lax.axis_index("tensor")
    wide = x_ref.shape[1]
    rank = wide // adapters_here
    half = rank // 2
    slot = slots_of(ra_ref[...], sr_ref[...])
    column = lax.broadcasted_iota(jnp.int32, (slot.shape[0], wide), 1)
    low = (slot - me * adapters_here) * rank
    shrunk = (x_ref[...] + xo_ref[...]).astype(BF16)
    kept = jnp.where((column >= low) & (column < low + rank), shrunk.astype(F32), 0.0).astype(BF16)
    place = place_of(slot, me, adapters_here)
    rows = lax.dot_general(
        place, kept, (((0,), (0,)), ((), ())), preferred_element_type=F32
    ).astype(BF16)
    i = lax.broadcasted_iota(jnp.int32, (wide, wide // 2), 0)
    j = lax.broadcasted_iota(jnp.int32, (wide, wide // 2), 1)
    base = (j // half) * rank + j % half

    def part(c):
        pick = jnp.where(i == base + c * half, 1.0, 0.0).astype(BF16)
        return jnp.dot(rows, pick, preferred_element_type=F32).astype(BF16)

    own, other = part(core), part(1 - core)
    for d in range(batches):
        span = pl.ds(pl.multiple_of((2 * d + core) * cols, LANES), cols)
        total = jnp.dot(own, up_ref[:, span], preferred_element_type=F32)
        total += jnp.dot(other, upo_ref[:, span], preferred_element_type=F32)
        d_ref[d] = total.astype(BF16)


def base_kernel(step, f_ref, w_ref, keep_ref, send_ref):
    core = lax.axis_index("tensor")
    cols = keep_ref.shape[1]
    for k, ref in enumerate((send_ref, keep_ref)):
        first = (core + 1 - k) % 2 * cols
        for t in range(0, cols, step):
            span = pl.ds(pl.multiple_of(first + t, LANES), step)
            ref[:, t : t + step] = jnp.dot(f_ref[...], w_ref[:, span], preferred_element_type=F32)


def final_kernel(adapters_here, ra_ref, sr_ref, keep_ref, got_ref, d_ref, o_ref):
    slot = slots_of(ra_ref[...], sr_ref[...])
    total = keep_ref[...] + got_ref[...]
    for s in range(d_ref.shape[0]):
        total += jnp.dot(place_of(slot, s, adapters_here), d_ref[s], preferred_element_type=F32)
    o_ref[...] = jnp.square(jnp.maximum(total, 0.0)).astype(BF16)


def call(kernel, out, n_in, cost=None, limit=8, scratch=()):
    many = isinstance(out, (list, tuple))
    return pl.pallas_call(
        kernel,
        out_shape=out,
        in_specs=whole(n_in),
        out_specs=whole(len(out)) if many else whole(1)[0],
        compiler_params=pltpu.CompilerParams(vmem_limit_bytes=limit * MIB),
        cost_estimate=cost,
        scratch_shapes=scratch,
    )


def per_device(features, up_weight, down, up, request_adapter, storage_row):
    batches = lax.axis_size("batch")
    adapters_here, width, rank = down.shape
    hidden = up.shape[2]
    requests = request_adapter.shape[0]
    cols = up_weight.shape[1] // 2
    swap = functools.partial(lax.ppermute, axis_name="tensor", perm=[(0, 1), (1, 0)])
    ra = request_adapter.reshape(1, requests)
    sr = storage_row.reshape(1, -1)
    up = up.reshape(-1, hidden)
    up_other = swap(up)
    down = jnp.transpose(down, (0, 2, 1)).reshape(adapters_here * rank, width)
    sent = jnp.broadcast_to(features[None], (batches,) + features.shape)
    gathered = lax.all_to_all(sent, "batch", 0, 0, tiled=True)
    x, rows = call(
        shrink_kernel,
        [
            jax.ShapeDtypeStruct((requests, adapters_here * rank), F32),
            jax.ShapeDtypeStruct((requests, width), BF16),
        ],
        2,
        scratch=[VMEM((requests, width), F32)],
    )(gathered, down)
    x_other = swap(x)
    delta = call(
        functools.partial(delta_kernel, adapters_here),
        jax.ShapeDtypeStruct((batches, OWN_MOST, cols), BF16),
        6,
    )(ra, sr, x, x_other, up, up_other)
    received = lax.all_to_all(delta, "batch", 0, 0, tiled=True)
    half = jax.ShapeDtypeStruct((requests, cols), F32)
    keep, send = call(
        functools.partial(base_kernel, min(cols, 512)),
        [half, half],
        2,
        pl.CostEstimate(
            flops=2 * requests * up_weight.size, bytes_accessed=2 * up_weight.size, transcendentals=0
        ),
    )(rows, in_vmem(up_weight))
    got = swap(send)
    return call(
        functools.partial(final_kernel, adapters_here),
        jax.ShapeDtypeStruct((requests, cols), BF16),
        5,
    )(ra, sr, keep, got, received)


def solution(mesh):
    in_specs = (
        P(("group", "batch"), "tensor"),
        P("tensor", "batch"),
        P(("group", "batch"), "tensor", None),
        P(("group", "batch"), "tensor", None),
        P("group"),
        P("group"),
    )
    return jax.shard_map(
        per_device,
        mesh=mesh,
        in_specs=in_specs,
        out_specs=P("group", ("batch", "tensor")),
        check_vma=False,
    )
```

time: 112 us -> 44.9 us (0.40)
  waiting for transfers between devices: 33 us -> 2.38 us
  blocking collectives: 35 us -> 14.3 us
  matrix products: 15.6 us -> 0 us
  between operations: 14.2 us -> 0.04 us
  local copies, waits for them, and re-layouts: 5.25 us -> 15.3 us
  Pallas kernels: 0 us -> 8.45 us
  other arithmetic: 2.85 us -> 0 us
  starting transfers between devices: 5.5 us -> 4.05 us
    all_gather x1 -> x0, blocking collectives: 32.5 us -> none  [per_device(): gathered = lax.all_gather(features, 'batch', axis=0, tiled=True)]
    all_to_all x1, waiting for transfers between devices: 26 us -> 0.01 us  [per_device(): received = lax.all_to_all(delta, 'batch', 0, 0, tiled=True)]
    dot_general x3 -> x0, matrix products: 15.6 us -> none  [the longest x1 13.5 us: per_device(): jnp.dot(gathered, up_weight, preferred_element_type=jnp.float32)]
    all_to_all x0 -> x1, blocking collectives: none -> 14.3 us  [per_device(): gathered = lax.all_to_all(sent, 'batch', 0, 0, tiled=True)]
    unnamed x8 -> x14, local copies, waits for them, and re-layouts: 0.65 us -> 14.5 us
    pallas_call x0 -> x4, Pallas kernels: none -> 8.45 us  [the longest x1 4.43 us: per_device(): call(functools.partial(base_kernel, min(cols, 512)), [half, half], 2, pl....]
    reduce_scatter x1 -> x0, waiting for transfers between devices: 6.91 us -> none  [per_device(): lax.psum_scatter(plain_output + adapter_output, 'tensor', scatter_dimensi...]
    gather x4 -> x0, local copies, waits for them, and re-layouts: 3.19 us -> none  [the longest x1 1.31 us: per_device(): slot_of = adapter_storage_row[request_adapter]]
  transfers between devices with their start and end apart: 2 -> 4, of which waited for: 2 -> 2; matrix products, arithmetic and copies ran while one was open for 0% -> 2% of each run, Pallas kernels for 0% -> 11%
where the time goes in v1:
time: 44.9 us; the launch traced here: 44.4 us
  local copies, waits for them, and re-layouts  15.3 us (34%)
  blocking collectives  14.3 us (32%)
  Pallas kernels  8.45 us (19%)
  starting transfers between devices  4.05 us (9%)
  waiting for transfers between devices  2.38 us (5%)
    unnamed x14, local copies, waits for them, and re-layouts  14.5 us
    all_to_all x1, blocking collectives, per_device(): gathered = lax.all_to_all(sent, 'batch', 0, 0, tiled=True)  14.3 us
    pallas_call x1, Pallas kernels, per_device(): call(functools.partial(base_kernel, min(cols, 512)), [half, half], 2, pl....  4.43 us
    all_to_all x1, starting transfers between devices, per_device(): received = lax.all_to_all(delta, 'batch', 0, 0, tiled=True)  3.41 us
    pallas_call x1, Pallas kernels, per_device(): call(functools.partial(final_kernel, adapters_here), jax.ShapeDtypeStruct...  2.07 us
    pallas_call x1, Pallas kernels, per_device(): call(functools.partial(delta_kernel, adapters_here), jax.ShapeDtypeStruct...  1.68 us
    ppermute x1, waiting for transfers between devices, per_device(): x_other = swap(x)  1.2 us
    ppermute x1, waiting for transfers between devices, per_device(): got = swap(send)  1.18 us
  transfers between devices with their start and end apart: 4, of which 2 were waited for; matrix products, arithmetic and copies ran while one was open for 2% of the time, Pallas kernels for 11%

profile of v1, /device:TPU:0, one launch (start us, length us, event | category | flops | bytes accessed | tf_op | source)
XLA Modules:
  0.0 44.4 jit_solution(1062731504788010240)
XLA Ops:
  0.0 0.5 %collective-permute-start.2 = (bf16[32,32768]{1,0:T(8,128)(2,1)}, bf16[32,32768]{1,0:T(8,128)(2,1)S(1)}, u32[]{:S(2)}, u32[]{:S(2)}) collective-permute-start(bf16[32,32768]{1,0:T(8,128)(2,1)} %bitcast.6), channel_id=1, source_target_pairs={{0,1},{1,0},{2,3},{3,2},{4,5},{5,4},{6,7},{7,6},{8,9},{9,8},{10,11... | collective-permute-start | bytes 6291464 | tf_op jit(solution)/shard_map/ppermute | solution.py:134
  0.5 0.8 %broadcast_in_dim.2 = bf16[8,2,4096]{2,1,0:T(2,128)(2,1)S(1)} broadcast(bf16[2,4096]{1,0:T(2,128)(2,1)} %param.6), dimensions={1,2} | broadcast | bytes 147456 | tf_op jit(solution)/shard_map/broadcast_in_dim | solution.py:136
  1.2 14.3 %all_to_all.10.g_ref = bf16[8,2,4096]{2,1,0:T(2,128)(2,1)S(1)} all-to-all(bf16[8,2,4096]{2,1,0:T(2,128)(2,1)S(1)} %broadcast_in_dim.2), channel_id=1, replica_groups=mesh['group'=2,'batch'=8,'tensor'=2] {'batch'}, dimensions={0} | all-to-all | bytes 262144 | tf_op jit(solution)/shard_map/all_to_all | solution.py:137
  15.5 0.0 copy-start.2
  15.5 1.0 %copy-done.2 = bf16[4,4096,16]{1,2,0:T(8,128)(2,1)S(1)} copy-done((bf16[4,4096,16]{1,2,0:T(8,128)(2,1)S(1)}, bf16[4,4096,16]{1,2,0:T(8,128)(2,1)}, u32[]{:S(2)}) %copy-start.2) | copy-done | bytes 524312
  16.5 0.3 shard_map.64
  16.8 0.0 collective-permute-start.1
  16.8 1.2 %collective-permute-done.1.xo_ref = f32[16,64]{1,0:T(8,128)S(1)} collective-permute-done((f32[16,64]{1,0:T(8,128)S(1)}, f32[16,64]{1,0:T(8,128)S(1)}, u32[]{:S(2)}, u32[]{:S(2)}) %collective-permute-start.1) | collective-permute-done | bytes 4128 | tf_op jit(solution)/shard_map/ppermute | solution.py:147
  18.0 0.0 collective-permute-done.2.upo_ref
  18.0 0.0 copy-start.1
  18.0 1.6 %copy-done.1 = bf16[4,8,32768]{2,1,0:T(8,128)(2,1)S(1)} copy-done((bf16[4,8,32768]{2,1,0:T(8,128)(2,1)S(1)}, bf16[4,8,32768]{2,1,0:T(8,128)(2,1)}, u32[]{:S(2)}) %copy-start.1) | copy-done | bytes 2097176
  19.6 0.0 copy-start.3
  19.6 0.7 %copy-done.3 = s32[16]{0:T(128)S(1)} copy-done((s32[16]{0:T(128)S(1)}, s32[16]{0:T(128)}, u32[]{:S(2)}) %copy-start.3) | copy-done | bytes 88
  20.3 0.0 copy-start.5
  20.3 0.7 %copy-done.5 = s32[32]{0:T(128)S(1)} copy-done((s32[32]{0:T(128)S(1)}, s32[32]{0:T(128)}, u32[]{:S(2)}) %copy-start.5) | copy-done | bytes 152
  20.9 1.7 %shard_map.66 = bf16[8,8,2048]{2,1,0:T(8,128)(2,1)} custom-call(s32[1,16]{1,0:T(1,128)S(1)} %bitcast.9, s32[1,32]{1,0:T(1,128)S(1)} %bitcast.11, f32[16,64]{1,0:T(8,128)S(1)} %get-tuple-element.12.x_ref, f32[16,64]{1,0:T(8,128)S(1)} %collective-permute-done.1.xo_ref, bf16[32,32768]{1,0:T(8,128)(2,1)S(1)} %bitcast.7, ...), custom_call_target="tpu_custom_call" | custom-call | tf_op jit(solution)/shard_map/pallas_call | solution.py:148
  22.6 3.4 %all-to-all-start.1 = ((bf16[8,8,2048]{2,1,0:T(8,128)(2,1)}), bf16[8,8,2048]{2,1,0:T(8,128)(2,1)S(1)}, u32[]{:S(2)}, u32[]{:S(2)}) async-start(bf16[8,8,2048]{2,1,0:T(8,128)(2,1)} %shard_map.66), calls=%async_computation.1 | async-start | bytes 524288 | tf_op jit(solution)/shard_map/all_to_all | solution.py:153
  26.0 0.0 copy-start
  26.0 10.5 %copy-done = bf16[4096,4096]{1,0:T(8,128)(2,1)S(1)} copy-done((bf16[4096,4096]{1,0:T(8,128)(2,1)S(1)}, bf16[4096,4096]{1,0:T(8,128)(2,1)}, u32[]{:S(2)}) %copy-start) | copy-done | bytes 33554456
  36.6 0.0 copy-start.4
  36.6 0.0 copy-start.6
  36.6 4.4 %shard_map.65 = (f32[16,2048]{1,0:T(8,128)S(1)}, f32[16,2048]{1,0:T(8,128)S(1)}) custom-call(bf16[16,4096]{1,0:T(8,128)(2,1)S(1)} %get-tuple-element.9.f_ref, bf16[4096,4096]{1,0:T(8,128)(2,1)S(1)} %copy-done), custom_call_target="tpu_custom_call" | custom-call | flops 536870912 | bytes 33554432 | tf_op jit(solution)/shard_map/pallas_call | solution.py:155
  41.0 0.2 collective-permute-start
  41.2 1.2 %collective-permute-done.got_ref = f32[16,2048]{1,0:T(8,128)S(1)} collective-permute-done((f32[16,2048]{1,0:T(8,128)S(1)}, f32[16,2048]{1,0:T(8,128)S(1)}, u32[]{:S(2)}, u32[]{:S(2)}) %collective-permute-start) | collective-permute-done | bytes 131104 | tf_op jit(solution)/shard_map/ppermute | solution.py:163
  42.4 0.0 all-to-all-done.1.d_ref
  42.4 0.0 copy-done.4
  42.4 0.0 copy-done.6
  42.4 2.1 %shard_map.67 = bf16[16,2048]{1,0:T(8,128)(2,1)} custom-call(s32[1,16]{1,0:T(1,128)S(1)} %bitcast.10, s32[1,32]{1,0:T(1,128)S(1)} %bitcast.12, f32[16,2048]{1,0:T(8,128)S(1)} %get-tuple-element.10.keep_ref, f32[16,2048]{1,0:T(8,128)S(1)} %collective-permute-done.got_ref, bf16[8,8,2048]{2,1,0:T(8,128)(2,1)S(1)} %all-to-all-done.1.d_ref), custom_call_target="tpu_custom_call" | custom-call | tf_op jit(solution)/shard_map/pallas_call | solution.py:164
Async XLA Ops:
  0.0 18.0 %collective-permute-start.2 = (bf16[32,32768]{1,0:T(8,128)(2,1)}, bf16[32,32768]{1,0:T(8,128)(2,1)S(1)}, u32[]{:S(2)}, u32[]{:S(2)}) collective-permute-start(bf16[32,32768]{1,0:T(8,128)(2,1)} %bitcast.6), channel_id=1, source_target_pairs={{0,1},{1,0},{2,3},{3,2},{4,5},{5,4},{6,7},{7,6},{8,9},{9,8},{10,11... | collective-permute-start | bytes 6291464 | tf_op jit(solution)/shard_map/ppermute | solution.py:134
  15.5 1.0 %copy-start.2 = (bf16[4,4096,16]{1,2,0:T(8,128)(2,1)S(1)}, bf16[4,4096,16]{1,2,0:T(8,128)(2,1)}, u32[]{:S(2)}) copy-start(bf16[4,4096,16]{1,2,0:T(8,128)(2,1)} %param.8) | copy-start | bytes 1572868
  16.8 1.2 %collective-permute-start.1 = (f32[16,64]{1,0:T(8,128)S(1)}, f32[16,64]{1,0:T(8,128)S(1)}, u32[]{:S(2)}, u32[]{:S(2)}) collective-permute-start(f32[16,64]{1,0:T(8,128)S(1)} %get-tuple-element.12.x_ref), channel_id=1, source_target_pairs={{0,1},{1,0},{2,3},{3,2},{4,5},{5,4},{6,7},{7,6},{8,9},{9,8},{10,11... | collective-permute-start | bytes 12296 | tf_op jit(solution)/shard_map/ppermute | solution.py:147
  18.0 1.6 %copy-start.1 = (bf16[4,8,32768]{2,1,0:T(8,128)(2,1)S(1)}, bf16[4,8,32768]{2,1,0:T(8,128)(2,1)}, u32[]{:S(2)}) copy-start(bf16[4,8,32768]{2,1,0:T(8,128)(2,1)} %param.9) | copy-start | bytes 6291460
  19.6 0.7 %copy-start.3 = (s32[16]{0:T(128)S(1)}, s32[16]{0:T(128)}, u32[]{:S(2)}) copy-start(s32[16]{0:T(128)} %param.10) | copy-start | bytes 196
  20.3 0.7 %copy-start.5 = (s32[32]{0:T(128)S(1)}, s32[32]{0:T(128)}, u32[]{:S(2)}) copy-start(s32[32]{0:T(128)} %param.11) | copy-start | bytes 388
  22.6 19.8 %all-to-all-start.1 = ((bf16[8,8,2048]{2,1,0:T(8,128)(2,1)}), bf16[8,8,2048]{2,1,0:T(8,128)(2,1)S(1)}, u32[]{:S(2)}, u32[]{:S(2)}) async-start(bf16[8,8,2048]{2,1,0:T(8,128)(2,1)} %shard_map.66), calls=%async_computation.1 | async-start | bytes 524288 | tf_op jit(solution)/shard_map/all_to_all | solution.py:153
  26.0 10.5 %copy-start = (bf16[4096,4096]{1,0:T(8,128)(2,1)S(1)}, bf16[4096,4096]{1,0:T(8,128)(2,1)}, u32[]{:S(2)}) copy-start(bf16[4096,4096]{1,0:T(8,128)(2,1)} %w_ref.1) | copy-start | bytes 100663296
  36.6 5.8 %copy-start.4 = (s32[16]{0:T(128)S(1)}, s32[16]{0:T(128)}, u32[]{:S(2)}) copy-start(s32[16]{0:T(128)} %param.10) | copy-start | bytes 196
  36.6 5.8 %copy-start.6 = (s32[32]{0:T(128)S(1)}, s32[32]{0:T(128)}, u32[]{:S(2)}) copy-start(s32[32]{0:T(128)} %param.11) | copy-start | bytes 388
  41.0 1.4 %collective-permute-start = (f32[16,2048]{1,0:T(8,128)S(1)}, f32[16,2048]{1,0:T(8,128)S(1)}, u32[]{:S(2)}, u32[]{:S(2)}) collective-permute-start(f32[16,2048]{1,0:T(8,128)S(1)} %get-tuple-element.11), channel_id=1, source_target_pairs={{0,1},{1,0},{2,3},{3,2},{4,5},{5,4},{6,7},{7,6},{8,9},{9,8},{10,11... | collective-permute-start | bytes 393224 | tf_op jit(solution)/shard_map/ppermute | solution.py:163

commit v2 on v1

v2 whole, which is shorter than its diff:
```python
import functools

import jax
import jax.numpy as jnp
from jax import lax
from jax.experimental import pallas as pl
from jax.experimental.pallas import tpu as pltpu
from jax.sharding import PartitionSpec as P

OWN_MOST = 8
LANES = 128
MIB = 1 << 20
F32 = jnp.float32
BF16 = jnp.bfloat16
VMEM = pltpu.VMEM


def whole(n):
    return [pl.BlockSpec(memory_space=VMEM)] * n


def in_vmem(x):
    return pltpu.with_memory_space_constraint(x, VMEM)


def in_hbm(x):
    return pltpu.with_memory_space_constraint(x, pltpu.HBM)


def copies_kernel(v_ref, o_ref):
    o_ref[...] = jnp.broadcast_to(v_ref[...][None], o_ref.shape)


def ready_kernel(
    batches, ra_ref, sr_ref, down_ref, up_ref, upo_ref, keep_ref, place_ref, sel_ref, downv_ref, upv_ref, sems
):
    me = lax.axis_index("batch")
    core = lax.axis_index("tensor")
    rows, hidden = up_ref.shape
    cols = hidden // (2 * batches)
    copies = [pltpu.make_async_copy(down_ref, downv_ref, sems.at[0])]
    for d in range(batches):
        span = pl.ds(pl.multiple_of((2 * d + core) * cols, LANES), cols)
        for k, ref in enumerate((up_ref, upo_ref)):
            copies.append(
                pltpu.make_async_copy(
                    ref.at[:, span],
                    upv_ref.at[k * rows : (k + 1) * rows, d * cols : (d + 1) * cols],
                    sems.at[1 + 2 * d + k],
                )
            )
    for c in copies:
        c.start()
    requests, adapters = ra_ref.shape[1], sr_ref.shape[1]
    here = adapters // batches

    def iota(shape, dim):
        return lax.broadcasted_iota(jnp.int32, shape, dim)

    square = (requests, requests)
    ra = jnp.sum(jnp.where(iota(square, 0) == iota(square, 1), ra_ref[...], 0), axis=1, keepdims=True)
    slot = jnp.sum(
        jnp.where(iota((requests, adapters), 1) == ra, sr_ref[...], 0), axis=1, keepdims=True
    )
    first = iota((requests, batches), 1) * here
    hit = (slot >= first) & (slot < first + here)
    earlier = jnp.where(iota(square, 1) < iota(square, 0), 1.0, 0.0).astype(BF16)
    marks = jnp.where(hit, 1.0, 0.0)
    counts = jnp.dot(earlier, marks.astype(BF16), preferred_element_type=F32)
    rank = jnp.sum(counts * marks, axis=1, keepdims=True).astype(jnp.int32)
    owner = jnp.sum(jnp.where(hit, iota((requests, batches), 1), 0), axis=1, keepdims=True)
    wide = keep_ref.shape[1]
    width = wide // here
    low = (slot - me * here) * width
    column = iota((requests, wide), 1)
    keep_ref[...] = jnp.where((column >= low) & (column < low + width), 1.0, 0.0)
    mine = (owner == me) & (iota((requests, OWN_MOST), 1) == rank)
    place_ref[...] = jnp.where(mine, 1.0, 0.0).astype(BF16)
    sel_ref[...] = jnp.where(
        iota(sel_ref.shape, 1) == owner * OWN_MOST + rank, 1.0, 0.0
    ).astype(BF16)
    for c in copies:
        c.wait()


def shrink_kernel(g_ref, down_ref, x_ref, f_ref, rows_ref):
    batches, each, _ = g_ref.shape
    for b in range(batches):
        rows_ref[b * each : (b + 1) * each] = g_ref[b].astype(F32)
    f_ref[...] = rows_ref[...].astype(BF16)
    x_ref[...] = lax.dot_general(
        f_ref[...], down_ref[...], (((1,), (1,)), ((), ())), preferred_element_type=F32
    )


def delta_kernel(here, x_ref, xo_ref, keep_ref, place_ref, up_ref, acc_ref, d_ref):
    batches, _, cols = d_ref.shape
    core = lax.axis_index("tensor")
    wide = x_ref.shape[1]
    rank = wide // here
    half = rank // 2
    shrunk = (x_ref[...] + xo_ref[...]).astype(BF16)
    kept = (shrunk.astype(F32) * keep_ref[...]).astype(BF16)
    rows = lax.dot_general(
        place_ref[...], kept, (((0,), (0,)), ((), ())), preferred_element_type=F32
    ).astype(BF16)
    i = lax.broadcasted_iota(jnp.int32, (wide, wide), 0)
    j = lax.broadcasted_iota(jnp.int32, (wide, wide), 1)
    side = jnp.where(j < wide // 2, core, 1 - core)
    k = jnp.where(j < wide // 2, j, j - wide // 2)
    source = jnp.zeros_like(k)
    for h in range(here):
        within = (k >= h * half) & (k < (h + 1) * half)
        source = jnp.where(within, h * rank + k - h * half, source)
    pick = jnp.where(i == source + side * half, 1.0, 0.0).astype(BF16)
    rows = jnp.dot(rows, pick, preferred_element_type=F32).astype(BF16)
    for d in range(batches):
        d_ref[d] = jnp.dot(
            rows, up_ref[:, d * cols : (d + 1) * cols], preferred_element_type=F32
        ).astype(BF16)


def stream(step, first, count, f_ref, w_ref, buf, sems, add):
    depth = buf.shape[0]

    def copy(i):
        return pltpu.make_async_copy(
            w_ref.at[pl.ds((first + i) * step, step)], buf.at[i % depth], sems.at[i % depth]
        )

    for i in range(min(depth, count)):
        copy(i).start()
    for i in range(count):
        copy(i).wait()
        k = (first + i) * step
        add(i, jnp.dot(f_ref[:, k : k + step], buf[i % depth], preferred_element_type=F32))
        if i + depth < count:
            copy(i + depth).start()


def head_kernel(step, count, f_ref, w_ref, acc_ref, buf, sems):
    def add(i, part):
        acc_ref[...] = part if i == 0 else acc_ref[...] + part

    stream(step, 0, count, f_ref, w_ref, buf, sems, add)


def base_kernel(step, first, count, f_ref, head_ref, w_ref, keep_ref, send_ref, acc_ref, buf, sems):
    def add(i, part):
        acc_ref[...] = (head_ref if i == 0 else acc_ref)[...] + part

    stream(step, first, count, f_ref, w_ref, buf, sems, add)
    core = lax.axis_index("tensor")
    cols = keep_ref.shape[1]
    keep_ref[...] = acc_ref[:, pl.ds(pl.multiple_of(core * cols, LANES), cols)]
    send_ref[...] = acc_ref[:, pl.ds(pl.multiple_of((1 - core) * cols, LANES), cols)]


def final_kernel(sel_ref, keep_ref, got_ref, d_ref, o_ref):
    total = keep_ref[...] + got_ref[...]
    total += jnp.dot(sel_ref[...], d_ref[...], preferred_element_type=F32)
    o_ref[...] = jnp.square(jnp.maximum(total, 0.0)).astype(BF16)


def call(kernel, out, places, cost=None, limit=6, scratch=()):
    spec = {"v": pl.BlockSpec(memory_space=VMEM), "h": pl.BlockSpec(memory_space=pltpu.HBM),
            "a": pl.BlockSpec(memory_space=pl.ANY)}
    many = isinstance(out, (list, tuple))
    return pl.pallas_call(
        kernel,
        out_shape=out,
        in_specs=[spec[p] for p in places],
        out_specs=[spec["v"]] * len(out) if many else spec["v"],
        compiler_params=pltpu.CompilerParams(vmem_limit_bytes=limit * MIB),
        cost_estimate=cost,
        scratch_shapes=scratch,
    )


def moves(size, flops=0):
    return pl.CostEstimate(flops=flops, bytes_accessed=size, transcendentals=0)


def per_device(features, up_weight, down, up, request_adapter, storage_row):
    batches = lax.axis_size("batch")
    here, width, rank = down.shape
    hidden = up.shape[2]
    requests = request_adapter.shape[0]
    cols = up_weight.shape[1] // 2
    wide = here * rank
    shape = jax.ShapeDtypeStruct
    dma = pltpu.SemaphoreType.DMA
    swap = functools.partial(lax.ppermute, axis_name="tensor", perm=[(0, 1), (1, 0)])
    up = up.reshape(-1, hidden)
    up_other = swap(up)
    down = jnp.transpose(down, (0, 2, 1)).reshape(wide, width)
    sent = call(copies_kernel, shape((batches,) + features.shape, BF16), "v")(features)
    gathered = lax.all_to_all(sent, "batch", 0, 0, tiled=True)
    keep, place, sel, down, up = call(
        functools.partial(ready_kernel, batches),
        [
            shape((requests, wide), F32),
            shape((requests, OWN_MOST), BF16),
            shape((requests, batches * OWN_MOST), BF16),
            VMEM(down.shape, BF16),
            VMEM((wide, hidden // 2), BF16),
        ],
        "vvhha",
        moves(6 * up.size),
        scratch=[dma((1 + 2 * batches,))],
    )(request_adapter.reshape(1, -1), storage_row.reshape(1, -1), in_hbm(down), in_hbm(up), up_other)
    x, rows = call(
        shrink_kernel,
        [shape((requests, wide), F32), shape((requests, width), BF16)],
        "vv",
        scratch=[VMEM((requests, width), F32)],
    )(gathered, in_vmem(down))
    x_other = swap(x)
    step = 256
    head = 2
    blocks = width // step
    flops = 2 * requests * step * 2 * cols
    acc = call(
        functools.partial(head_kernel, step, head),
        shape((requests, 2 * cols), F32),
        "vh",
        moves(head * 4 * step * cols, head * flops),
        16,
        [VMEM((head, step, 2 * cols), BF16), dma((head,))],
    )(rows, in_hbm(up_weight))
    delta = call(
        functools.partial(delta_kernel, here), shape((batches, OWN_MOST, cols), BF16), "vvvvva"
    )(x, x_other, keep, place, in_vmem(up), acc)
    received = lax.all_to_all(delta, "batch", 0, 0, tiled=True)
    half = shape((requests, cols), F32)
    rest = blocks - head
    mine, send = call(
        functools.partial(base_kernel, step, head, rest),
        [half, half],
        "vvh",
        moves(rest * 4 * step * cols, rest * flops),
        40,
        [
            VMEM((requests, 2 * cols), F32),
            VMEM((12, step, 2 * cols), BF16),
            dma((12,)),
        ],
    )(rows, acc, in_hbm(up_weight))
    return call(final_kernel, shape((requests, cols), BF16), "vvvv")(
        sel, mine, swap(send), received.reshape(batches * OWN_MOST, cols)
    )


def solution(mesh):
    in_specs = (
        P(("group", "batch"), "tensor"),
        P("tensor", "batch"),
        P(("group", "batch"), "tensor", None),
        P(("group", "batch"), "tensor", None),
        P("group"),
        P("group"),
    )
    return jax.shard_map(
        per_device,
        mesh=mesh,
        in_specs=in_specs,
        out_specs=P("group", ("batch", "tensor")),
        check_vma=False,
    )
```

time: 44.9 us -> 37.2 us (0.83)
  blocking collectives: 14.3 us -> 0 us
  local copies, waits for them, and re-layouts: 15.3 us -> 3.43 us
  Pallas kernels: 8.45 us -> 17.6 us
  starting transfers between devices: 4.05 us -> 11.2 us
  waiting for transfers between devices: 2.38 us -> 4.42 us
    all_to_all x1 -> x0, blocking collectives: 14.3 us -> none  [per_device(): gathered = lax.all_to_all(sent, 'batch', 0, 0, tiled=True)]
    unnamed x14 -> x10, local copies, waits for them, and re-layouts: 14.5 us -> 3.43 us
    pallas_call x4 -> x7, Pallas kernels: 8.45 us -> 17.6 us  [the longest x1 10.2 us: per_device(): call(functools.partial(base_kernel, step, head, rest), [half, half], 'vvh...]
    all_to_all x0 -> x1, starting transfers between devices: none -> 6.8 us  [per_device(): gathered = lax.all_to_all(sent, 'batch', 0, 0, tiled=True)]
    all_to_all x0 -> x1, waiting for transfers between devices: none -> 3.43 us  [per_device(): gathered = lax.all_to_all(sent, 'batch', 0, 0, tiled=True)]
    ppermute x1, waiting for transfers between devices: 1.2 us -> 0.01 us  [per_device(): x_other = swap(x)]
    broadcast_in_dim x1 -> x0, local copies, waits for them, and re-layouts: 0.79 us -> none  [per_device(): sent = jnp.broadcast_to(features[None], (batches,) + features.shape)]
  transfers between devices with their start and end apart: 4 -> 5, of which waited for: 2 -> 2; matrix products, arithmetic and copies ran while one was open for 2% -> 0% of each run, Pallas kernels for 11% -> 41%
where the time goes in v2:
time: 37.2 us; the launch traced here: 36.8 us
  Pallas kernels  17.6 us (47%)
  starting transfers between devices  11.2 us (30%)
  waiting for transfers between devices  4.42 us (12%)
  local copies, waits for them, and re-layouts  3.43 us (9%)
    pallas_call x1, Pallas kernels, per_device(): call(functools.partial(base_kernel, step, head, rest), [half, half], 'vvh...  10.2 us
    all_to_all x1, starting transfers between devices, per_device(): gathered = lax.all_to_all(sent, 'batch', 0, 0, tiled=True)  6.8 us
    unnamed x10, local copies, waits for them, and re-layouts  3.43 us
    all_to_all x1, waiting for transfers between devices, per_device(): gathered = lax.all_to_all(sent, 'batch', 0, 0, tiled=True)  3.43 us
    all_to_all x1, starting transfers between devices, per_device(): received = lax.all_to_all(delta, 'batch', 0, 0, tiled=True)  3.41 us
    pallas_call x1, Pallas kernels, per_device(): call(functools.partial(head_kernel, step, head), shape((requests, 2 * col...  2.78 us
    pallas_call x1, Pallas kernels, per_device(): call(functools.partial(ready_kernel, batches), [shape((requests, wide), F...  1.56 us
    pallas_call x1, Pallas kernels, per_device(): call(functools.partial(delta_kernel, here), shape((batches, OWN_MOST, col...  1.37 us
  transfers between devices with their start and end apart: 5, of which 2 were waited for; matrix products, arithmetic and copies ran while one was open for 0% of the time, Pallas kernels for 41%

profile of v2, /device:TPU:0, one launch (start us, length us, event | category | flops | bytes accessed | tf_op | source)
XLA Modules:
  0.0 36.8 jit_solution(6529015288282802862)
XLA Ops:
  0.0 0.5 %collective-permute-start = (bf16[32,32768]{1,0:T(8,128)(2,1)}, bf16[32,32768]{1,0:T(8,128)(2,1)S(1)}, u32[]{:S(2)}, u32[]{:S(2)}) collective-permute-start(bf16[32,32768]{1,0:T(8,128)(2,1)} %bitcast.10), channel_id=1, source_target_pairs={{0,1},{1,0},{2,3},{3,2},{4,5},{5,4},{6,7},{7,6},{8,9},{9,8},{10,11... | collective-permute-start | bytes 6291464 | tf_op jit(solution)/shard_map/ppermute | solution.py:195
  0.5 0.0 copy-start.2
  0.5 0.7 %copy-done.2 = bf16[2,4096]{1,0:T(2,128)(2,1)S(1)} copy-done((bf16[2,4096]{1,0:T(2,128)(2,1)S(1)}, bf16[2,4096]{1,0:T(2,128)(2,1)}, u32[]{:S(2)}) %copy-start.2) | copy-done | bytes 16408
  1.2 0.7 %shard_map.65 = bf16[8,2,4096]{2,1,0:T(2,128)(2,1)} custom-call(bf16[2,4096]{1,0:T(2,128)(2,1)S(1)} %copy-done.2), custom_call_target="tpu_custom_call" | custom-call | tf_op jit(solution)/shard_map/pallas_call | solution.py:197
  1.8 6.8 %all-to-all-start = ((bf16[8,2,4096]{2,1,0:T(2,128)(2,1)}), bf16[8,2,4096]{2,1,0:T(2,128)(2,1)S(1)}, u32[]{:S(2)}, u32[]{:S(2)}) async-start(bf16[8,2,4096]{2,1,0:T(2,128)(2,1)} %shard_map.65), calls=%async_computation | async-start | bytes 262144 | tf_op jit(solution)/shard_map/all_to_all | solution.py:198
  8.6 0.0 collective-permute-done.upo_ref
  8.6 0.0 copy-start.3
  8.6 0.6 %copy-done.3 = s32[16]{0:T(128)S(1)} copy-done((s32[16]{0:T(128)S(1)}, s32[16]{0:T(128)}, u32[]{:S(2)}) %copy-start.3) | copy-done | bytes 88
  9.3 0.0 copy-start.4
  9.3 0.7 %copy-done.4 = s32[32]{0:T(128)S(1)} copy-done((s32[32]{0:T(128)S(1)}, s32[32]{0:T(128)}, u32[]{:S(2)}) %copy-start.4) | copy-done | bytes 152
  10.0 1.6 %shard_map.64 = (f32[16,64]{1,0:T(8,128)S(1)}, bf16[16,8]{1,0:T(8,128)(2,1)S(1)}, bf16[16,64]{1,0:T(8,128)(2,1)S(1)}, bf16[64,4096]{1,0:T(8,128)(2,1)S(1)}, bf16[64,16384]{1,0:T(8,128)(2,1)S(1)}) custom-call(s32[1,16]{1,0:T(1,128)S(1)} %bitcast.8, s32[1,32]{1,0:T(1,128)S(1)} %bitcast.9, bf16[64,4096]{1,0:T(8,128)(2,1)} %bitcast.12, ...), custom_call_target="tpu_custom_call" | custom-call | bytes 6291456 | tf_op jit(solution)/shard_map/pallas_call | solution.py:199
  11.5 0.0 copy-start
  11.5 1.3 %copy-done = bf16[64,16384]{1,0:T(8,128)(2,1)} copy-done((bf16[64,16384]{1,0:T(8,128)(2,1)}, bf16[64,16384]{1,0:T(8,128)(2,1)S(1)}, u32[]{:S(2)}) %copy-start) | copy-done | bytes 2097176
  12.9 3.4 %all-to-all-done.g_ref = bf16[8,2,4096]{2,1,0:T(2,128)(2,1)S(1)} async-done(((bf16[8,2,4096]{2,1,0:T(2,128)(2,1)}), bf16[8,2,4096]{2,1,0:T(2,128)(2,1)S(1)}, u32[]{:S(2)}, u32[]{:S(2)}) %all-to-all-start) | async-done | bytes 131104 | tf_op jit(solution)/shard_map/all_to_all | solution.py:198
  16.3 0.3 shard_map.66
  16.6 0.0 collective-permute-start.2
  16.6 0.0 copy-start.1
  16.6 2.8 %shard_map.67.head_ref.acc_ref = f32[16,4096]{1,0:T(8,128)S(1)} custom-call(bf16[16,4096]{1,0:T(8,128)(2,1)S(1)} %get-tuple-element.16.f_ref, bf16[4096,4096]{1,0:T(8,128)(2,1)} %w_ref.3), custom_call_target="tpu_custom_call" | custom-call | flops 67108864 | bytes 4194304 | tf_op jit(solution)/shard_map/pallas_call | solution.py:223
  19.4 0.0 collective-permute-done.2.xo_ref
  19.4 0.1 copy-done.1
  19.4 1.4 %shard_map.69 = bf16[8,8,2048]{2,1,0:T(8,128)(2,1)} custom-call(f32[16,64]{1,0:T(8,128)S(1)} %get-tuple-element.19.x_ref, f32[16,64]{1,0:T(8,128)S(1)} %collective-permute-done.2.xo_ref, f32[16,64]{1,0:T(8,128)S(1)} %get-tuple-element.20.keep_ref, bf16[16,8]{1,0:T(8,128)(2,1)S(1)} %get-tuple-element.21.place_ref, bf16[64,16384]{1,0:T(8,128)(2,1)S(1)} %copy-done.1, ...), custom_call_target="tpu_custom_call" | custom-call | tf_op jit(solution)/shard_map/pallas_call | solution.py:231
  20.8 3.4 %all-to-all-start.1 = ((bf16[8,8,2048]{2,1,0:T(8,128)(2,1)}), bf16[8,8,2048]{2,1,0:T(8,128)(2,1)S(1)}, u32[]{:S(2)}, u32[]{:S(2)}) async-start(bf16[8,8,2048]{2,1,0:T(8,128)(2,1)} %shard_map.69), calls=%async_computation.1 | async-start | bytes 524288 | tf_op jit(solution)/shard_map/all_to_all | solution.py:234
  24.2 10.2 %shard_map.68 = (f32[16,2048]{1,0:T(8,128)S(1)}, f32[16,2048]{1,0:T(8,128)S(1)}) custom-call(bf16[16,4096]{1,0:T(8,128)(2,1)S(1)} %get-tuple-element.16.f_ref, f32[16,4096]{1,0:T(8,128)S(1)} %shard_map.67.head_ref.acc_ref, bf16[4096,4096]{1,0:T(8,128)(2,1)} %w_ref.3), custom_call_target="tpu_custom_call" | custom-call | flops 469762048 | bytes 29360128 | tf_op jit(solution)/shard_map/pallas_call | solution.py:237
  34.4 0.6 %collective-permute-start.1 = (f32[16,2048]{1,0:T(8,128)S(1)}, f32[16,2048]{1,0:T(8,128)S(1)}, u32[]{:S(2)}, u32[]{:S(2)}) collective-permute-start(f32[16,2048]{1,0:T(8,128)S(1)} %get-tuple-element.18), channel_id=1, source_target_pairs={{0,1},{1,0},{2,3},{3,2},{4,5},{5,4},{6,7},{7,6},{8,9},{9,8},{10,11... | collective-permute-start | bytes 393224 | tf_op jit(solution)/shard_map/ppermute | solution.py:250
  35.0 1.0 %collective-permute-done.1.got_ref = f32[16,2048]{1,0:T(8,128)S(1)} collective-permute-done((f32[16,2048]{1,0:T(8,128)S(1)}, f32[16,2048]{1,0:T(8,128)S(1)}, u32[]{:S(2)}, u32[]{:S(2)}) %collective-permute-start.1) | collective-permute-done | bytes 131104 | tf_op jit(solution)/shard_map/ppermute | solution.py:250
  36.0 0.0 all-to-all-done.1
  36.0 0.8 %shard_map.70 = bf16[16,2048]{1,0:T(8,128)(2,1)} custom-call(bf16[16,64]{1,0:T(8,128)(2,1)S(1)} %get-tuple-element.14.sel_ref, f32[16,2048]{1,0:T(8,128)S(1)} %get-tuple-element.17.keep_ref, f32[16,2048]{1,0:T(8,128)S(1)} %collective-permute-done.1.got_ref, bf16[64,2048]{1,0:T(8,128)(2,1)S(1)} %bitcast.7), custom_call_target="tpu_custom_call" | custom-call | tf_op jit(solution)/shard_map/pallas_call | solution.py:249
Async XLA Ops:
  0.0 8.6 %collective-permute-start = (bf16[32,32768]{1,0:T(8,128)(2,1)}, bf16[32,32768]{1,0:T(8,128)(2,1)S(1)}, u32[]{:S(2)}, u32[]{:S(2)}) collective-permute-start(bf16[32,32768]{1,0:T(8,128)(2,1)} %bitcast.10), channel_id=1, source_target_pairs={{0,1},{1,0},{2,3},{3,2},{4,5},{5,4},{6,7},{7,6},{8,9},{9,8},{10,11... | collective-permute-start | bytes 6291464 | tf_op jit(solution)/shard_map/ppermute | solution.py:195
  0.5 0.7 %copy-start.2 = (bf16[2,4096]{1,0:T(2,128)(2,1)S(1)}, bf16[2,4096]{1,0:T(2,128)(2,1)}, u32[]{:S(2)}) copy-start(bf16[2,4096]{1,0:T(2,128)(2,1)} %v_ref.1) | copy-start | bytes 49156
  1.8 14.5 %all-to-all-start = ((bf16[8,2,4096]{2,1,0:T(2,128)(2,1)}), bf16[8,2,4096]{2,1,0:T(2,128)(2,1)S(1)}, u32[]{:S(2)}, u32[]{:S(2)}) async-start(bf16[8,2,4096]{2,1,0:T(2,128)(2,1)} %shard_map.65), calls=%async_computation | async-start | bytes 262144 | tf_op jit(solution)/shard_map/all_to_all | solution.py:198
  8.6 0.7 %copy-start.3 = (s32[16]{0:T(128)S(1)}, s32[16]{0:T(128)}, u32[]{:S(2)}) copy-start(s32[16]{0:T(128)} %param.10) | copy-start | bytes 196
  9.3 0.7 %copy-start.4 = (s32[32]{0:T(128)S(1)}, s32[32]{0:T(128)}, u32[]{:S(2)}) copy-start(s32[32]{0:T(128)} %param.11) | copy-start | bytes 388
  11.5 1.3 %copy-start = (bf16[64,16384]{1,0:T(8,128)(2,1)}, bf16[64,16384]{1,0:T(8,128)(2,1)S(1)}, u32[]{:S(2)}) copy-start(bf16[64,16384]{1,0:T(8,128)(2,1)S(1)} %get-tuple-element.22.up_ref) | copy-start | bytes 6291460
  16.6 2.8 %collective-permute-start.2 = (f32[16,64]{1,0:T(8,128)S(1)}, f32[16,64]{1,0:T(8,128)S(1)}, u32[]{:S(2)}, u32[]{:S(2)}) collective-permute-start(f32[16,64]{1,0:T(8,128)S(1)} %get-tuple-element.19.x_ref), channel_id=1, source_target_pairs={{0,1},{1,0},{2,3},{3,2},{4,5},{5,4},{6,7},{7,6},{8,9},{9,8},{10,11... | collective-permute-start | bytes 12296 | tf_op jit(solution)/shard_map/ppermute | solution.py:218
  16.6 2.9 %copy-start.1 = (bf16[64,16384]{1,0:T(8,128)(2,1)S(1)}, bf16[64,16384]{1,0:T(8,128)(2,1)}, u32[]{:S(2)}) copy-start(bf16[64,16384]{1,0:T(8,128)(2,1)} %copy-done) | copy-start | bytes 6291460
  20.8 15.2 %all-to-all-start.1 = ((bf16[8,8,2048]{2,1,0:T(8,128)(2,1)}), bf16[8,8,2048]{2,1,0:T(8,128)(2,1)S(1)}, u32[]{:S(2)}, u32[]{:S(2)}) async-start(bf16[8,8,2048]{2,1,0:T(8,128)(2,1)} %shard_map.69), calls=%async_computation.1 | async-start | bytes 524288 | tf_op jit(solution)/shard_map/all_to_all | solution.py:234
  34.4 1.6 %collective-permute-start.1 = (f32[16,2048]{1,0:T(8,128)S(1)}, f32[16,2048]{1,0:T(8,128)S(1)}, u32[]{:S(2)}, u32[]{:S(2)}) collective-permute-start(f32[16,2048]{1,0:T(8,128)S(1)} %get-tuple-element.18), channel_id=1, source_target_pairs={{0,1},{1,0},{2,3},{3,2},{4,5},{5,4},{6,7},{7,6},{8,9},{9,8},{10,11... | collective-permute-start | bytes 393224 | tf_op jit(solution)/shard_map/ppermute | solution.py:250

commit v3 on v2

--- a/solution.py
+++ b/solution.py
@@ -27,8 +27,29 @@
     return pltpu.with_memory_space_constraint(x, pltpu.HBM)
 
 
-def copies_kernel(v_ref, o_ref):
-    o_ref[...] = jnp.broadcast_to(v_ref[...][None], o_ref.shape)
+def order_of(batches):
+    return sorted(range(batches), key=lambda b: abs(2 * b - batches + 1))
+
+
+def place_in_order(b, batches):
+    return jnp.where(2 * b < batches, batches - 2 - 2 * b, 2 * b - batches + 1)
+
+
+def exchange(x):
+    batches = lax.axis_size("batch")
+    return lax.all_to_all(
+        x, "batch", 0, 0, tiled=True, axis_index_groups=[order_of(batches)]
+    )
+
+
+def copies_kernel(v_ref, o_ref, sems):
+    copies = [
+        pltpu.make_async_copy(v_ref, o_ref.at[b], sems.at[b]) for b in range(o_ref.shape[0])
+    ]
+    for c in copies:
+        c.start()
+    for c in copies:
+        c.wait()
 
 
 def ready_kernel(
@@ -39,8 +60,8 @@
     rows, hidden = up_ref.shape
     cols = hidden // (2 * batches)
     copies = [pltpu.make_async_copy(down_ref, downv_ref, sems.at[0])]
-    for d in range(batches):
-        span = pl.ds(pl.multiple_of((2 * d + core) * cols, LANES), cols)
+    for d, b in enumerate(order_of(batches)):
+        span = pl.ds(pl.multiple_of((2 * b + core) * cols, LANES), cols)
         for k, ref in enumerate((up_ref, upo_ref)):
             copies.append(
                 pltpu.make_async_copy(
@@ -77,7 +98,7 @@
     mine = (owner == me) & (iota((requests, OWN_MOST), 1) == rank)
     place_ref[...] = jnp.where(mine, 1.0, 0.0).astype(BF16)
     sel_ref[...] = jnp.where(
-        iota(sel_ref.shape, 1) == owner * OWN_MOST + rank, 1.0, 0.0
+        iota(sel_ref.shape, 1) == place_in_order(owner, batches) * OWN_MOST + rank, 1.0, 0.0
     ).astype(BF16)
     for c in copies:
         c.wait()
@@ -85,8 +106,8 @@
 
 def shrink_kernel(g_ref, down_ref, x_ref, f_ref, rows_ref):
     batches, each, _ = g_ref.shape
-    for b in range(batches):
-        rows_ref[b * each : (b + 1) * each] = g_ref[b].astype(F32)
+    for k, b in enumerate(order_of(batches)):
+        rows_ref[b * each : (b + 1) * each] = g_ref[k].astype(F32)
     f_ref[...] = rows_ref[...].astype(BF16)
     x_ref[...] = lax.dot_general(
         f_ref[...], down_ref[...], (((1,), (1,)), ((), ())), preferred_element_type=F32
@@ -145,15 +166,16 @@
     stream(step, 0, count, f_ref, w_ref, buf, sems, add)
 
 
-def base_kernel(step, first, count, f_ref, head_ref, w_ref, keep_ref, send_ref, acc_ref, buf, sems):
+def base_kernel(own, step, first, count, f_ref, head_ref, w_ref, acc_ref, buf, sems):
+    core = lax.axis_index("tensor")
+    cols = acc_ref.shape[1]
+    side = core if own else 1 - core
+    span = pl.ds(pl.multiple_of(side * cols, LANES), cols)
+
     def add(i, part):
-        acc_ref[...] = (head_ref if i == 0 else acc_ref)[...] + part
-
-    stream(step, first, count, f_ref, w_ref, buf, sems, add)
-    core = lax.axis_index("tensor")
-    cols = keep_ref.shape[1]
-    keep_ref[...] = acc_ref[:, pl.ds(pl.multiple_of(core * cols, LANES), cols)]
-    send_ref[...] = acc_ref[:, pl.ds(pl.multiple_of((1 - core) * cols, LANES), cols)]
+        acc_ref[...] = part + (head_ref[:, span] if i == 0 else acc_ref[...])
+
+    stream(step, first, count, f_ref, w_ref.at[:, span], buf, sems, add)
 
 
 def final_kernel(sel_ref, keep_ref, got_ref, d_ref, o_ref):
@@ -194,8 +216,8 @@
     up = up.reshape(-1, hidden)
     up_other = swap(up)
     down = jnp.transpose(down, (0, 2, 1)).reshape(wide, width)
-    sent = call(copies_kernel, shape((batches,) + features.shape, BF16), "v")(features)
-    gathered = lax.all_to_all(sent, "batch", 0, 0, tiled=True)
+    sent = call(copies_kernel, shape((batches,) + features.shape, BF16), "h", scratch=[dma((batches,))])(in_hbm(features))
+    gathered = exchange(sent)
     keep, place, sel, down, up = call(
         functools.partial(ready_kernel, batches),
         [
@@ -217,7 +239,7 @@
     )(gathered, in_vmem(down))
     x_other = swap(x)
     step = 256
-    head = 2
+    head = 1
     blocks = width // step
     flops = 2 * requests * step * 2 * cols
     acc = call(
@@ -231,23 +253,23 @@
     delta = call(
         functools.partial(delta_kernel, here), shape((batches, OWN_MOST, cols), BF16), "vvvvva"
     )(x, x_other, keep, place, in_vmem(up), acc)
-    received = lax.all_to_all(delta, "batch", 0, 0, tiled=True)
-    half = shape((requests, cols), F32)
+    received = exchange(delta)
     rest = blocks - head
-    mine, send = call(
-        functools.partial(base_kernel, step, head, rest),
-        [half, half],
-        "vvh",
-        moves(rest * 4 * step * cols, rest * flops),
-        40,
-        [
-            VMEM((requests, 2 * cols), F32),
-            VMEM((12, step, 2 * cols), BF16),
-            dma((12,)),
-        ],
-    )(rows, acc, in_hbm(up_weight))
+
+    def base(own):
+        return call(
+            functools.partial(base_kernel, own, step, head, rest),
+            shape((requests, cols), F32),
+            "vvh",
+            moves(rest * 2 * step * cols, rest * flops // 2),
+            40,
+            [VMEM((min(15, rest), step, cols), BF16), dma((min(15, rest),))],
+        )(rows, acc, in_hbm(up_weight))
+
+    other = swap(base(False))
+    mine = base(True)
     return call(final_kernel, shape((requests, cols), BF16), "vvvv")(
-        sel, mine, swap(send), received.reshape(batches * OWN_MOST, cols)
+        sel, mine, other, received.reshape(batches * OWN_MOST, cols)
     )
 
 

time: 37.2 us -> 36.4 us (0.978)
  waiting for transfers between devices: 4.42 us -> 1.11 us
  Pallas kernels: 17.6 us -> 19.6 us
  starting transfers between devices: 11.2 us -> 12.4 us
  local copies, waits for them, and re-layouts: 3.43 us -> 2.72 us
    pallas_call x2 -> x3, Pallas kernels: 10.8 us -> 13.5 us  [the longest x2 11.7 us: base(): call(functools.partial(base_kernel, own, step, head, rest), shape((reques...]
    all_to_all x2, waiting for transfers between devices: 3.43 us -> 1.1 us  [exchange(): lax.all_to_all(x, 'batch', 0, 0, tiled=True, axis_index_groups=[order_of(...]
    all_to_all x2, starting transfers between devices: 10.2 us -> 11.6 us  [exchange(): lax.all_to_all(x, 'batch', 0, 0, tiled=True, axis_index_groups=[order_of(...]
    ppermute x1, waiting for transfers between devices: 0.99 us -> 0.01 us  [per_device(): other = swap(base(False))]
    unnamed x10 -> x8, local copies, waits for them, and re-layouts: 3.43 us -> 2.72 us
    pallas_call x1, Pallas kernels: 2.78 us -> 2.14 us  [per_device(): call(functools.partial(head_kernel, step, head), shape((requests, 2 * col...]
  transfers between devices with their start and end apart: 5 -> 5, of which waited for: 2 -> 1; matrix products, arithmetic and copies ran while one was open for 0% -> 0% of each run, Pallas kernels for 41% -> 48%
where the time goes in v3:
time: 36.4 us; the launch traced here: 35.9 us
  Pallas kernels  19.6 us (54%)
  starting transfers between devices  12.4 us (34%)
  local copies, waits for them, and re-layouts  2.72 us (7%)
  waiting for transfers between devices  1.11 us (3%)
    pallas_call x2, Pallas kernels, base(): call(functools.partial(base_kernel, own, step, head, rest), shape((reques...  11.7 us
    all_to_all x2, starting transfers between devices, exchange(): lax.all_to_all(x, 'batch', 0, 0, tiled=True, axis_index_groups=[order_of(...  11.6 us
    unnamed x8, local copies, waits for them, and re-layouts  2.72 us
    pallas_call x1, Pallas kernels, per_device(): call(functools.partial(head_kernel, step, head), shape((requests, 2 * col...  2.14 us
    pallas_call x1, Pallas kernels, per_device(): call(copies_kernel, shape((batches,) + features.shape, BF16), 'h', scratc...  1.72 us
    pallas_call x1, Pallas kernels, per_device(): call(functools.partial(ready_kernel, batches), [shape((requests, wide), F...  1.56 us
    pallas_call x1, Pallas kernels, per_device(): call(functools.partial(delta_kernel, here), shape((batches, OWN_MOST, col...  1.37 us
    all_to_all x2, waiting for transfers between devices, exchange(): lax.all_to_all(x, 'batch', 0, 0, tiled=True, axis_index_groups=[order_of(...  1.1 us
  transfers between devices with their start and end apart: 5, of which 1 were waited for; matrix products, arithmetic and copies ran while one was open for 0% of the time, Pallas kernels for 48%

profile of v3, /device:TPU:0, one launch (start us, length us, event | category | flops | bytes accessed | tf_op | source)
XLA Modules:
  0.0 35.9 jit_solution(6004956654680547992)
XLA Ops:
  0.0 0.5 %collective-permute-start = (bf16[32,32768]{1,0:T(8,128)(2,1)}, bf16[32,32768]{1,0:T(8,128)(2,1)S(1)}, u32[]{:S(2)}, u32[]{:S(2)}) collective-permute-start(bf16[32,32768]{1,0:T(8,128)(2,1)} %bitcast.10), channel_id=1, source_target_pairs={{0,1},{1,0},{2,3},{3,2},{4,5},{5,4},{6,7},{7,6},{8,9},{9,8},{10,11... | collective-permute-start | bytes 6291464 | tf_op jit(solution)/shard_map/ppermute | solution.py:217
  0.5 1.7 %shard_map.65 = bf16[8,2,4096]{2,1,0:T(2,128)(2,1)} custom-call(bf16[2,4096]{1,0:T(2,128)(2,1)} %v_ref.1), custom_call_target="tpu_custom_call" | custom-call | tf_op jit(solution)/shard_map/pallas_call | solution.py:219
  2.2 7.4 %all-to-all-start = ((bf16[8,2,4096]{2,1,0:T(2,128)(2,1)}), bf16[8,2,4096]{2,1,0:T(2,128)(2,1)S(1)}, u32[]{:S(2)}, u32[]{:S(2)}) async-start(bf16[8,2,4096]{2,1,0:T(2,128)(2,1)} %shard_map.65), calls=%async_computation | async-start | bytes 262144 | tf_op jit(solution)/shard_map/all_to_all | solution.py:40
  9.6 0.0 collective-permute-done.upo_ref
  9.6 0.0 copy-start.2
  9.6 0.7 %copy-done.2 = s32[16]{0:T(128)S(1)} copy-done((s32[16]{0:T(128)S(1)}, s32[16]{0:T(128)}, u32[]{:S(2)}) %copy-start.2) | copy-done | bytes 88
  10.2 0.0 copy-start.3
  10.2 0.7 %copy-done.3 = s32[32]{0:T(128)S(1)} copy-done((s32[32]{0:T(128)S(1)}, s32[32]{0:T(128)}, u32[]{:S(2)}) %copy-start.3) | copy-done | bytes 152
  10.9 1.6 %shard_map.64 = (f32[16,64]{1,0:T(8,128)S(1)}, bf16[16,8]{1,0:T(8,128)(2,1)S(1)}, bf16[16,64]{1,0:T(8,128)(2,1)S(1)}, bf16[64,4096]{1,0:T(8,128)(2,1)S(1)}, bf16[64,16384]{1,0:T(8,128)(2,1)S(1)}) custom-call(s32[1,16]{1,0:T(1,128)S(1)} %bitcast.8, s32[1,32]{1,0:T(1,128)S(1)} %bitcast.9, bf16[64,4096]{1,0:T(8,128)(2,1)} %bitcast.12, ...), custom_call_target="tpu_custom_call" | custom-call | bytes 6291456 | tf_op jit(solution)/shard_map/pallas_call | solution.py:221
  12.4 0.0 copy-start
  12.4 1.3 %copy-done = bf16[64,16384]{1,0:T(8,128)(2,1)} copy-done((bf16[64,16384]{1,0:T(8,128)(2,1)}, bf16[64,16384]{1,0:T(8,128)(2,1)S(1)}, u32[]{:S(2)}) %copy-start) | copy-done | bytes 2097176
  13.8 1.1 %all-to-all-done.g_ref = bf16[8,2,4096]{2,1,0:T(2,128)(2,1)S(1)} async-done(((bf16[8,2,4096]{2,1,0:T(2,128)(2,1)}), bf16[8,2,4096]{2,1,0:T(2,128)(2,1)S(1)}, u32[]{:S(2)}, u32[]{:S(2)}) %all-to-all-start) | async-done | bytes 131104 | tf_op jit(solution)/shard_map/all_to_all | solution.py:40
  14.9 0.3 shard_map.66
  15.1 0.0 collective-permute-start.2
  15.1 0.0 copy-start.1
  15.2 2.1 %shard_map.67.head_ref.acc_ref = f32[16,4096]{1,0:T(8,128)S(1)} custom-call(bf16[16,4096]{1,0:T(8,128)(2,1)S(1)} %get-tuple-element.14.f_ref, bf16[4096,4096]{1,0:T(8,128)(2,1)} %w_ref.5), custom_call_target="tpu_custom_call" | custom-call | flops 33554432 | bytes 2097152 | tf_op jit(solution)/shard_map/pallas_call | solution.py:245
  17.3 0.0 collective-permute-done.2.xo_ref
  17.3 0.1 copy-done.1
  17.4 1.4 %shard_map.70 = bf16[8,8,2048]{2,1,0:T(8,128)(2,1)} custom-call(f32[16,64]{1,0:T(8,128)S(1)} %get-tuple-element.15.x_ref, f32[16,64]{1,0:T(8,128)S(1)} %collective-permute-done.2.xo_ref, f32[16,64]{1,0:T(8,128)S(1)} %get-tuple-element.16.keep_ref, bf16[16,8]{1,0:T(8,128)(2,1)S(1)} %get-tuple-element.17.place_ref, bf16[64,16384]{1,0:T(8,128)(2,1)S(1)} %copy-done.1, ...), custom_call_target="tpu_custom_call" | custom-call | tf_op jit(solution)/shard_map/pallas_call | solution.py:253
  18.8 4.3 %all-to-all-start.1 = ((bf16[8,8,2048]{2,1,0:T(8,128)(2,1)}), bf16[8,8,2048]{2,1,0:T(8,128)(2,1)S(1)}, u32[]{:S(2)}, u32[]{:S(2)}) async-start(bf16[8,8,2048]{2,1,0:T(8,128)(2,1)} %shard_map.70), calls=%async_computation.1 | async-start | bytes 524288 | tf_op jit(solution)/shard_map/all_to_all | solution.py:40
  23.0 5.9 %shard_map.69 = f32[16,2048]{1,0:T(8,128)S(1)} custom-call(bf16[16,4096]{1,0:T(8,128)(2,1)S(1)} %get-tuple-element.14.f_ref, f32[16,4096]{1,0:T(8,128)S(1)} %shard_map.67.head_ref.acc_ref, bf16[4096,4096]{1,0:T(8,128)(2,1)} %w_ref.5), custom_call_target="tpu_custom_call" | custom-call | flops 251658240 | bytes 15728640 | tf_op jit(solution)/shard_map/pallas_call | solution.py:260
  28.9 0.3 collective-permute-start.1
  29.2 5.9 %shard_map.68.keep_ref = f32[16,2048]{1,0:T(8,128)S(1)} custom-call(bf16[16,4096]{1,0:T(8,128)(2,1)S(1)} %get-tuple-element.14.f_ref, f32[16,4096]{1,0:T(8,128)S(1)} %shard_map.67.head_ref.acc_ref, bf16[4096,4096]{1,0:T(8,128)(2,1)} %w_ref.5), custom_call_target="tpu_custom_call" | custom-call | flops 251658240 | bytes 15728640 | tf_op jit(solution)/shard_map/pallas_call | solution.py:260
  35.1 0.0 collective-permute-done.1.got_ref
  35.1 0.0 all-to-all-done.1
  35.1 0.8 %shard_map.71 = bf16[16,2048]{1,0:T(8,128)(2,1)} custom-call(bf16[16,64]{1,0:T(8,128)(2,1)S(1)} %get-tuple-element.12.sel_ref, f32[16,2048]{1,0:T(8,128)S(1)} %shard_map.68.keep_ref, f32[16,2048]{1,0:T(8,128)S(1)} %collective-permute-done.1.got_ref, bf16[64,2048]{1,0:T(8,128)(2,1)S(1)} %bitcast.7), custom_call_target="tpu_custom_call" | custom-call | tf_op jit(solution)/shard_map/pallas_call | solution.py:271
Async XLA Ops:
  0.0 9.6 %collective-permute-start = (bf16[32,32768]{1,0:T(8,128)(2,1)}, bf16[32,32768]{1,0:T(8,128)(2,1)S(1)}, u32[]{:S(2)}, u32[]{:S(2)}) collective-permute-start(bf16[32,32768]{1,0:T(8,128)(2,1)} %bitcast.10), channel_id=1, source_target_pairs={{0,1},{1,0},{2,3},{3,2},{4,5},{5,4},{6,7},{7,6},{8,9},{9,8},{10,11... | collective-permute-start | bytes 6291464 | tf_op jit(solution)/shard_map/ppermute | solution.py:217
  2.2 12.7 %all-to-all-start = ((bf16[8,2,4096]{2,1,0:T(2,128)(2,1)}), bf16[8,2,4096]{2,1,0:T(2,128)(2,1)S(1)}, u32[]{:S(2)}, u32[]{:S(2)}) async-start(bf16[8,2,4096]{2,1,0:T(2,128)(2,1)} %shard_map.65), calls=%async_computation | async-start | bytes 262144 | tf_op jit(solution)/shard_map/all_to_all | solution.py:40
  9.6 0.7 %copy-start.2 = (s32[16]{0:T(128)S(1)}, s32[16]{0:T(128)}, u32[]{:S(2)}) copy-start(s32[16]{0:T(128)} %param.10) | copy-start | bytes 196
  10.2 0.7 %copy-start.3 = (s32[32]{0:T(128)S(1)}, s32[32]{0:T(128)}, u32[]{:S(2)}) copy-start(s32[32]{0:T(128)} %param.11) | copy-start | bytes 388
  12.4 1.3 %copy-start = (bf16[64,16384]{1,0:T(8,128)(2,1)}, bf16[64,16384]{1,0:T(8,128)(2,1)S(1)}, u32[]{:S(2)}) copy-start(bf16[64,16384]{1,0:T(8,128)(2,1)S(1)} %get-tuple-element.18.up_ref) | copy-start | bytes 6291460
  15.1 2.2 %collective-permute-start.2 = (f32[16,64]{1,0:T(8,128)S(1)}, f32[16,64]{1,0:T(8,128)S(1)}, u32[]{:S(2)}, u32[]{:S(2)}) collective-permute-start(f32[16,64]{1,0:T(8,128)S(1)} %get-tuple-element.15.x_ref), channel_id=1, source_target_pairs={{0,1},{1,0},{2,3},{3,2},{4,5},{5,4},{6,7},{7,6},{8,9},{9,8},{10,11... | collective-permute-start | bytes 12296 | tf_op jit(solution)/shard_map/ppermute | solution.py:240
  15.1 2.3 %copy-start.1 = (bf16[64,16384]{1,0:T(8,128)(2,1)S(1)}, bf16[64,16384]{1,0:T(8,128)(2,1)}, u32[]{:S(2)}) copy-start(bf16[64,16384]{1,0:T(8,128)(2,1)} %copy-done) | copy-start | bytes 6291460
  18.8 16.3 %all-to-all-start.1 = ((bf16[8,8,2048]{2,1,0:T(8,128)(2,1)}), bf16[8,8,2048]{2,1,0:T(8,128)(2,1)S(1)}, u32[]{:S(2)}, u32[]{:S(2)}) async-start(bf16[8,8,2048]{2,1,0:T(8,128)(2,1)} %shard_map.70), calls=%async_computation.1 | async-start | bytes 524288 | tf_op jit(solution)/shard_map/all_to_all | solution.py:40
  28.9 6.2 %collective-permute-start.1 = (f32[16,2048]{1,0:T(8,128)S(1)}, f32[16,2048]{1,0:T(8,128)S(1)}, u32[]{:S(2)}, u32[]{:S(2)}) collective-permute-start(f32[16,2048]{1,0:T(8,128)S(1)} %shard_map.69), channel_id=1, source_target_pairs={{0,1},{1,0},{2,3},{3,2},{4,5},{5,4},{6,7},{7,6},{8,9},{9,8},{10,11... | collective-permute-start | bytes 393224 | tf_op jit(solution)/shard_map/ppermute | solution.py:269

commit v4 on v3

--- a/solution.py
+++ b/solution.py
@@ -42,34 +42,25 @@
     )
 
 
-def copies_kernel(v_ref, o_ref, sems):
-    copies = [
-        pltpu.make_async_copy(v_ref, o_ref.at[b], sems.at[b]) for b in range(o_ref.shape[0])
+def columns(batches, ref, out, sems):
+    core = lax.axis_index("tensor")
+    cols = out.shape[1] // batches
+    return [
+        pltpu.make_async_copy(
+            ref.at[:, pl.ds(pl.multiple_of((2 * b + core) * cols, LANES), cols)],
+            out.at[:, d * cols : (d + 1) * cols],
+            sems.at[d],
+        )
+        for d, b in enumerate(order_of(batches))
     ]
-    for c in copies:
-        c.start()
-    for c in copies:
-        c.wait()
 
 
 def ready_kernel(
-    batches, ra_ref, sr_ref, down_ref, up_ref, upo_ref, keep_ref, place_ref, sel_ref, downv_ref, upv_ref, sems
+    batches, ra_ref, sr_ref, down_ref, up_ref, keep_ref, place_ref, sel_ref, downv_ref, upv_ref, sems
 ):
     me = lax.axis_index("batch")
-    core = lax.axis_index("tensor")
-    rows, hidden = up_ref.shape
-    cols = hidden // (2 * batches)
-    copies = [pltpu.make_async_copy(down_ref, downv_ref, sems.at[0])]
-    for d, b in enumerate(order_of(batches)):
-        span = pl.ds(pl.multiple_of((2 * b + core) * cols, LANES), cols)
-        for k, ref in enumerate((up_ref, upo_ref)):
-            copies.append(
-                pltpu.make_async_copy(
-                    ref.at[:, span],
-                    upv_ref.at[k * rows : (k + 1) * rows, d * cols : (d + 1) * cols],
-                    sems.at[1 + 2 * d + k],
-                )
-            )
+    copies = [pltpu.make_async_copy(down_ref, downv_ref, sems.at[batches])]
+    copies += columns(batches, up_ref, upv_ref, sems)
     for c in copies:
         c.start()
     requests, adapters = ra_ref.shape[1], sr_ref.shape[1]
@@ -114,7 +105,14 @@
     )
 
 
-def delta_kernel(here, x_ref, xo_ref, keep_ref, place_ref, up_ref, acc_ref, d_ref):
+def delta_kernel(
+    here, step, first, x_ref, xo_ref, keep_ref, place_ref, upa_ref, upb_ref, f_ref, head_ref, w_ref,
+    out_ref, acc_ref, next_ref, d_ref, buf, sems, out_sems
+):
+    taken = pltpu.make_async_copy(w_ref.at[pl.ds(first * step, step)], buf, sems.at[0])
+    coming = pltpu.make_async_copy(w_ref.at[pl.ds((first + 1) * step, step)], next_ref, sems.at[1])
+    taken.start()
+    coming.start()
     batches, _, cols = d_ref.shape
     core = lax.axis_index("tensor")
     wide = x_ref.shape[1]
@@ -125,20 +123,35 @@
     rows = lax.dot_general(
         place_ref[...], kept, (((0,), (0,)), ((), ())), preferred_element_type=F32
     ).astype(BF16)
-    i = lax.broadcasted_iota(jnp.int32, (wide, wide), 0)
-    j = lax.broadcasted_iota(jnp.int32, (wide, wide), 1)
-    side = jnp.where(j < wide // 2, core, 1 - core)
-    k = jnp.where(j < wide // 2, j, j - wide // 2)
+    i = lax.broadcasted_iota(jnp.int32, (wide, wide // 2), 0)
+    k = lax.broadcasted_iota(jnp.int32, (wide, wide // 2), 1)
     source = jnp.zeros_like(k)
     for h in range(here):
         within = (k >= h * half) & (k < (h + 1) * half)
         source = jnp.where(within, h * rank + k - h * half, source)
-    pick = jnp.where(i == source + side * half, 1.0, 0.0).astype(BF16)
-    rows = jnp.dot(rows, pick, preferred_element_type=F32).astype(BF16)
+
+    def part(side):
+        pick = jnp.where(i == source + side * half, 1.0, 0.0).astype(BF16)
+        return jnp.dot(rows, pick, preferred_element_type=F32).astype(BF16)
+
+    def out(d):
+        return pltpu.make_async_copy(d_ref.at[d], out_ref.at[d], out_sems.at[d])
+
+    own, other = part(core), part(1 - core)
     for d in range(batches):
-        d_ref[d] = jnp.dot(
-            rows, up_ref[:, d * cols : (d + 1) * cols], preferred_element_type=F32
-        ).astype(BF16)
+        span = slice(d * cols, (d + 1) * cols)
+        total = jnp.dot(own, upa_ref[:, span], preferred_element_type=F32)
+        total += jnp.dot(other, upb_ref[:, span], preferred_element_type=F32)
+        d_ref[d] = total.astype(BF16)
+        out(d).start()
+    taken.wait()
+    k = first * step
+    acc_ref[...] = head_ref[...] + jnp.dot(
+        f_ref[:, k : k + step], buf[...], preferred_element_type=F32
+    )
+    coming.wait()
+    for d in range(batches):
+        out(d).wait()
 
 
 def stream(step, first, count, f_ref, w_ref, buf, sems, add):
@@ -159,23 +172,39 @@
             copy(i + depth).start()
 
 
-def head_kernel(step, count, f_ref, w_ref, acc_ref, buf, sems):
+def head_kernel(batches, step, count, f_ref, w_ref, up_ref, acc_ref, upv_ref, buf, sems, upsems):
+    copies = columns(batches, up_ref, upv_ref, upsems)
+    for c in copies:
+        c.start()
+
     def add(i, part):
         acc_ref[...] = part if i == 0 else acc_ref[...] + part
 
     stream(step, 0, count, f_ref, w_ref, buf, sems, add)
-
-
-def base_kernel(own, step, first, count, f_ref, head_ref, w_ref, acc_ref, buf, sems):
+    for c in copies:
+        c.wait()
+
+
+def base_kernel(own, step, first, count, f_ref, head_ref, here_ref, w_ref, acc_ref, buf, sems):
     core = lax.axis_index("tensor")
     cols = acc_ref.shape[1]
     side = core if own else 1 - core
     span = pl.ds(pl.multiple_of(side * cols, LANES), cols)
 
-    def add(i, part):
-        acc_ref[...] = part + (head_ref[:, span] if i == 0 else acc_ref[...])
-
-    stream(step, first, count, f_ref, w_ref.at[:, span], buf, sems, add)
+    def copy(i):
+        k = (first + 1 + i) * step
+        return pltpu.make_async_copy(w_ref.at[k : k + step, span], buf.at[i], sems.at[i])
+
+    for i in range(count):
+        copy(i).start()
+    k = first * step
+    acc_ref[...] = head_ref[:, span] + jnp.dot(
+        f_ref[:, k : k + step], here_ref[:, span], preferred_element_type=F32
+    )
+    for i in range(count):
+        copy(i).wait()
+        k = (first + 1 + i) * step
+        acc_ref[...] += jnp.dot(f_ref[:, k : k + step], buf[i], preferred_element_type=F32)
 
 
 def final_kernel(sel_ref, keep_ref, got_ref, d_ref, o_ref):
@@ -184,7 +213,7 @@
     o_ref[...] = jnp.square(jnp.maximum(total, 0.0)).astype(BF16)
 
 
-def call(kernel, out, places, cost=None, limit=6, scratch=()):
+def call(kernel, out, places, cost=None, limit=6, scratch=(), outs=None):
     spec = {"v": pl.BlockSpec(memory_space=VMEM), "h": pl.BlockSpec(memory_space=pltpu.HBM),
             "a": pl.BlockSpec(memory_space=pl.ANY)}
     many = isinstance(out, (list, tuple))
@@ -192,7 +221,7 @@
         kernel,
         out_shape=out,
         in_specs=[spec[p] for p in places],
-        out_specs=[spec["v"]] * len(out) if many else spec["v"],
+        out_specs=[spec[p] for p in outs or "v" * len(out)] if many else spec["v"],
         compiler_params=pltpu.CompilerParams(vmem_limit_bytes=limit * MIB),
         cost_estimate=cost,
         scratch_shapes=scratch,
@@ -213,24 +242,24 @@
     shape = jax.ShapeDtypeStruct
     dma = pltpu.SemaphoreType.DMA
     swap = functools.partial(lax.ppermute, axis_name="tensor", perm=[(0, 1), (1, 0)])
-    up = up.reshape(-1, hidden)
+    down = jnp.transpose(down, (0, 2, 1)).reshape(wide, width)
+    sent = jnp.broadcast_to(features[None], (batches,) + features.shape)
+    sent, up = lax.optimization_barrier((sent, up.reshape(-1, hidden)))
     up_other = swap(up)
-    down = jnp.transpose(down, (0, 2, 1)).reshape(wide, width)
-    sent = call(copies_kernel, shape((batches,) + features.shape, BF16), "h", scratch=[dma((batches,))])(in_hbm(features))
     gathered = exchange(sent)
-    keep, place, sel, down, up = call(
+    keep, place, sel, down, up_b = call(
         functools.partial(ready_kernel, batches),
         [
             shape((requests, wide), F32),
             shape((requests, OWN_MOST), BF16),
             shape((requests, batches * OWN_MOST), BF16),
             VMEM(down.shape, BF16),
-            VMEM((wide, hidden // 2), BF16),
+            VMEM((wide // 2, hidden // 2), BF16),
         ],
-        "vvhha",
+        "vvhh",
         moves(6 * up.size),
-        scratch=[dma((1 + 2 * batches,))],
-    )(request_adapter.reshape(1, -1), storage_row.reshape(1, -1), in_hbm(down), in_hbm(up), up_other)
+        scratch=[dma((1 + batches,))],
+    )(request_adapter.reshape(1, -1), storage_row.reshape(1, -1), in_hbm(down), in_hbm(up_other))
     x, rows = call(
         shrink_kernel,
         [shape((requests, wide), F32), shape((requests, width), BF16)],
@@ -242,29 +271,39 @@
     head = 1
     blocks = width // step
     flops = 2 * requests * step * 2 * cols
-    acc = call(
-        functools.partial(head_kernel, step, head),
-        shape((requests, 2 * cols), F32),
-        "vh",
+    total = shape((requests, 2 * cols), F32)
+    acc, up_a = call(
+        functools.partial(head_kernel, batches, step, head),
+        [total, VMEM((wide // 2, hidden // 2), BF16)],
+        "vhh",
         moves(head * 4 * step * cols, head * flops),
         16,
-        [VMEM((head, step, 2 * cols), BF16), dma((head,))],
-    )(rows, in_hbm(up_weight))
-    delta = call(
-        functools.partial(delta_kernel, here), shape((batches, OWN_MOST, cols), BF16), "vvvvva"
-    )(x, x_other, keep, place, in_vmem(up), acc)
+        [VMEM((head, step, 2 * cols), BF16), dma((head,)), dma((batches,))],
+    )(rows, in_hbm(up_weight), in_hbm(up))
+    delta, acc, ahead = call(
+        functools.partial(delta_kernel, here, step, head),
+        [pltpu.HBM((batches, OWN_MOST, cols), BF16), total, VMEM((step, 2 * cols), BF16)],
+        "vvvvvvvvh",
+        scratch=[
+            VMEM((batches, OWN_MOST, cols), BF16),
+            VMEM((step, 2 * cols), BF16),
+            dma((2,)),
+            dma((batches,)),
+        ],
+        outs="hvv",
+    )(x, x_other, keep, place, in_vmem(up_a), in_vmem(up_b), rows, acc, in_hbm(up_weight))
     received = exchange(delta)
-    rest = blocks - head
+    rest = blocks - head - 2
 
     def base(own):
         return call(
-            functools.partial(base_kernel, own, step, head, rest),
+            functools.partial(base_kernel, own, step, head + 1, rest),
             shape((requests, cols), F32),
-            "vvh",
+            "vvvh",
             moves(rest * 2 * step * cols, rest * flops // 2),
-            40,
-            [VMEM((min(15, rest), step, cols), BF16), dma((min(15, rest),))],
-        )(rows, acc, in_hbm(up_weight))
+            24,
+            [VMEM((rest, step, cols), BF16), dma((rest,))],
+        )(rows, acc, in_vmem(ahead), in_hbm(up_weight))
 
     other = swap(base(False))
     mine = base(True)

time: 36.4 us -> 36.8 us (1.011)
  local copies, waits for them, and re-layouts: 2.72 us -> 4.06 us
  Pallas kernels: 19.6 us -> 18.6 us
    broadcast_in_dim x0 -> x1, local copies, waits for them, and re-layouts: none -> 1.43 us  [per_device(): sent = jnp.broadcast_to(features[None], (batches,) + features.shape)]
    pallas_call x5 -> x4, Pallas kernels: 17 us -> 16.1 us  [the longest x2 10.6 us: base(): call(functools.partial(base_kernel, own, step, head + 1, rest), shape((re...]
    unnamed x8 -> x6, local copies, waits for them, and re-layouts: 2.72 us -> 2.63 us
  transfers between devices with their start and end apart: 5 -> 5, of which waited for: 1 -> 1; matrix products, arithmetic and copies ran while one was open for 0% -> 0% of each run, Pallas kernels for 48% -> 40%
where the time goes in v4:
time: 36.8 us; the launch traced here: 36.3 us
  Pallas kernels  18.6 us (51%)
  starting transfers between devices  12.4 us (34%)
  local copies, waits for them, and re-layouts  4.06 us (11%)
  waiting for transfers between devices  1.2 us (3%)
    all_to_all x2, starting transfers between devices, exchange(): lax.all_to_all(x, 'batch', 0, 0, tiled=True, axis_index_groups=[order_of(...  11.6 us
    pallas_call x2, Pallas kernels, base(): call(functools.partial(base_kernel, own, step, head + 1, rest), shape((re...  10.6 us
    pallas_call x1, Pallas kernels, per_device(): call(functools.partial(delta_kernel, here, step, head), [pltpu.HBM((batch...  2.94 us
    unnamed x6, local copies, waits for them, and re-layouts  2.63 us
    pallas_call x1, Pallas kernels, per_device(): call(functools.partial(head_kernel, batches, step, head), [total, VMEM((w...  2.54 us
    pallas_call x1, Pallas kernels, per_device(): call(functools.partial(ready_kernel, batches), [shape((requests, wide), F...  1.47 us
    broadcast_in_dim x1, local copies, waits for them, and re-layouts, per_device(): sent = jnp.broadcast_to(features[None], (batches,) + features.shape)  1.43 us
    all_to_all x2, waiting for transfers between devices, exchange(): lax.all_to_all(x, 'batch', 0, 0, tiled=True, axis_index_groups=[order_of(...  1.19 us
  transfers between devices with their start and end apart: 5, of which 1 were waited for; matrix products, arithmetic and copies ran while one was open for 0% of the time, Pallas kernels for 40%

profile of v4, /device:TPU:0, one launch (start us, length us, event | category | flops | bytes accessed | tf_op | source)
XLA Modules:
  0.0 36.3 jit_solution(7186013968040465646)
XLA Ops:
  0.0 1.4 %broadcast_in_dim.2 = bf16[8,2,4096]{2,1,0:T(2,128)(2,1)} broadcast(bf16[2,4096]{1,0:T(2,128)(2,1)} %param.6), dimensions={1,2} | broadcast | bytes 147456 | tf_op jit(solution)/shard_map/broadcast_in_dim | solution.py:246
  1.4 0.5 %collective-permute-start = (bf16[32,32768]{1,0:T(8,128)(2,1)}, bf16[32,32768]{1,0:T(8,128)(2,1)S(1)}, u32[]{:S(2)}, u32[]{:S(2)}) collective-permute-start(bf16[32,32768]{1,0:T(8,128)(2,1)} %bitcast.10), channel_id=1, source_target_pairs={{0,1},{1,0},{2,3},{3,2},{4,5},{5,4},{6,7},{7,6},{8,9},{9,8},{10,11... | collective-permute-start | bytes 6291464 | tf_op jit(solution)/shard_map/ppermute | solution.py:248
  1.9 7.4 %all-to-all-start = ((bf16[8,2,4096]{2,1,0:T(2,128)(2,1)}), bf16[8,2,4096]{2,1,0:T(2,128)(2,1)S(1)}, u32[]{:S(2)}, u32[]{:S(2)}) async-start(bf16[8,2,4096]{2,1,0:T(2,128)(2,1)} %broadcast_in_dim.2), calls=%async_computation | async-start | bytes 262144 | tf_op jit(solution)/shard_map/all_to_all | solution.py:40
  9.3 0.0 collective-permute-done.up_ref
  9.3 0.0 copy-start.2
  9.3 1.3 %copy-done.2 = bf16[32,32768]{1,0:T(8,128)(2,1)} copy-done((bf16[32,32768]{1,0:T(8,128)(2,1)}, bf16[32,32768]{1,0:T(8,128)(2,1)S(1)}, u32[]{:S(2)}) %copy-start.2) | copy-done | bytes 2097176
  10.6 0.0 copy-start
  10.6 0.7 %copy-done = s32[16]{0:T(128)S(1)} copy-done((s32[16]{0:T(128)S(1)}, s32[16]{0:T(128)}, u32[]{:S(2)}) %copy-start) | copy-done | bytes 88
  11.2 0.0 copy-start.1
  11.2 0.7 %copy-done.1 = s32[32]{0:T(128)S(1)} copy-done((s32[32]{0:T(128)S(1)}, s32[32]{0:T(128)}, u32[]{:S(2)}) %copy-start.1) | copy-done | bytes 152
  11.9 1.5 %shard_map.64 = (f32[16,64]{1,0:T(8,128)S(1)}, bf16[16,8]{1,0:T(8,128)(2,1)S(1)}, bf16[16,64]{1,0:T(8,128)(2,1)S(1)}, bf16[64,4096]{1,0:T(8,128)(2,1)S(1)}, bf16[32,16384]{1,0:T(8,128)(2,1)S(1)}) custom-call(s32[1,16]{1,0:T(1,128)S(1)} %bitcast.8, s32[1,32]{1,0:T(1,128)S(1)} %bitcast.9, bf16[64,4096]{1,0:T(8,128)(2,1)} %bitcast.12, bf16[32,32768]{1,0:T(8,128)(2,1)} %copy-done.2), custom_call_target="tpu_custom_call" | custom-call | bytes 6291456 | tf_op jit(solution)/shard_map/pallas_call | solution.py:250
  13.4 1.2 %all-to-all-done.g_ref = bf16[8,2,4096]{2,1,0:T(2,128)(2,1)S(1)} async-done(((bf16[8,2,4096]{2,1,0:T(2,128)(2,1)}), bf16[8,2,4096]{2,1,0:T(2,128)(2,1)S(1)}, u32[]{:S(2)}, u32[]{:S(2)}) %all-to-all-start) | async-done | bytes 131104 | tf_op jit(solution)/shard_map/all_to_all | solution.py:40
  14.6 0.3 shard_map.65
  14.8 0.0 collective-permute-start.1
  14.8 2.5 %shard_map.66 = (f32[16,4096]{1,0:T(8,128)S(1)}, bf16[32,16384]{1,0:T(8,128)(2,1)S(1)}) custom-call(bf16[16,4096]{1,0:T(8,128)(2,1)S(1)} %get-tuple-element.23.f_ref, bf16[4096,4096]{1,0:T(8,128)(2,1)} %w_ref.7, bf16[32,32768]{1,0:T(8,128)(2,1)} %bitcast.11), custom_call_target="tpu_custom_call" | custom-call | flops 33554432 | bytes 2097152 | tf_op jit(solution)/shard_map/pallas_call | solution.py:275
  17.4 0.0 collective-permute-done.1.xo_ref
  17.4 2.9 %shard_map.67 = (bf16[8,8,2048]{2,1,0:T(8,128)(2,1)}, f32[16,4096]{1,0:T(8,128)S(1)}, bf16[256,4096]{1,0:T(8,128)(2,1)S(1)}) custom-call(f32[16,64]{1,0:T(8,128)S(1)} %get-tuple-element.24.x_ref, f32[16,64]{1,0:T(8,128)S(1)} %collective-permute-done.1.xo_ref, f32[16,64]{1,0:T(8,128)S(1)} %get-tuple-element.25.keep_ref, ...), custom_call_target="tpu_custom_call" | custom-call | tf_op jit(solution)/shard_map/pallas_call | solution.py:283
  20.3 4.3 %all-to-all-start.1 = ((bf16[8,8,2048]{2,1,0:T(8,128)(2,1)}), bf16[8,8,2048]{2,1,0:T(8,128)(2,1)S(1)}, u32[]{:S(2)}, u32[]{:S(2)}) async-start(bf16[8,8,2048]{2,1,0:T(8,128)(2,1)} %get-tuple-element.32), calls=%async_computation.1 | async-start | bytes 524288 | tf_op jit(solution)/shard_map/all_to_all | solution.py:40
  24.6 5.3 %shard_map.69 = f32[16,2048]{1,0:T(8,128)S(1)} custom-call(bf16[16,4096]{1,0:T(8,128)(2,1)S(1)} %get-tuple-element.23.f_ref, f32[16,4096]{1,0:T(8,128)S(1)} %get-tuple-element.30.head_ref, bf16[256,4096]{1,0:T(8,128)(2,1)S(1)} %get-tuple-element.31.here_ref, bf16[4096,4096]{1,0:T(8,128)(2,1)} %w_ref.7), custom_call_target="tpu_custom_call" | custom-call | flops 218103808 | bytes 13631488 | tf_op jit(solution)/shard_map/pallas_call | solution.py:299
  29.9 0.3 collective-permute-start.2
  30.2 5.3 %shard_map.68.keep_ref = f32[16,2048]{1,0:T(8,128)S(1)} custom-call(bf16[16,4096]{1,0:T(8,128)(2,1)S(1)} %get-tuple-element.23.f_ref, f32[16,4096]{1,0:T(8,128)S(1)} %get-tuple-element.30.head_ref, bf16[256,4096]{1,0:T(8,128)(2,1)S(1)} %get-tuple-element.31.here_ref, bf16[4096,4096]{1,0:T(8,128)(2,1)} %w_ref.7), custom_call_target="tpu_custom_call" | custom-call | flops 218103808 | bytes 13631488 | tf_op jit(solution)/shard_map/pallas_call | solution.py:299
  35.5 0.0 collective-permute-done.2.got_ref
  35.5 0.0 all-to-all-done.1
  35.5 0.8 %shard_map.70 = bf16[16,2048]{1,0:T(8,128)(2,1)} custom-call(bf16[16,64]{1,0:T(8,128)(2,1)S(1)} %get-tuple-element.20.sel_ref, f32[16,2048]{1,0:T(8,128)S(1)} %shard_map.68.keep_ref, f32[16,2048]{1,0:T(8,128)S(1)} %collective-permute-done.2.got_ref, bf16[64,2048]{1,0:T(8,128)(2,1)S(1)} %bitcast.7), custom_call_target="tpu_custom_call" | custom-call | tf_op jit(solution)/shard_map/pallas_call | solution.py:310
Async XLA Ops:
  1.4 7.8 %collective-permute-start = (bf16[32,32768]{1,0:T(8,128)(2,1)}, bf16[32,32768]{1,0:T(8,128)(2,1)S(1)}, u32[]{:S(2)}, u32[]{:S(2)}) collective-permute-start(bf16[32,32768]{1,0:T(8,128)(2,1)} %bitcast.10), channel_id=1, source_target_pairs={{0,1},{1,0},{2,3},{3,2},{4,5},{5,4},{6,7},{7,6},{8,9},{9,8},{10,11... | collective-permute-start | bytes 6291464 | tf_op jit(solution)/shard_map/ppermute | solution.py:248
  1.9 12.7 %all-to-all-start = ((bf16[8,2,4096]{2,1,0:T(2,128)(2,1)}), bf16[8,2,4096]{2,1,0:T(2,128)(2,1)S(1)}, u32[]{:S(2)}, u32[]{:S(2)}) async-start(bf16[8,2,4096]{2,1,0:T(2,128)(2,1)} %broadcast_in_dim.2), calls=%async_computation | async-start | bytes 262144 | tf_op jit(solution)/shard_map/all_to_all | solution.py:40
  9.3 1.3 %copy-start.2 = (bf16[32,32768]{1,0:T(8,128)(2,1)}, bf16[32,32768]{1,0:T(8,128)(2,1)S(1)}, u32[]{:S(2)}) copy-start(bf16[32,32768]{1,0:T(8,128)(2,1)S(1)} %collective-permute-done.up_ref) | copy-start | bytes 6291460
  10.6 0.7 %copy-start = (s32[16]{0:T(128)S(1)}, s32[16]{0:T(128)}, u32[]{:S(2)}) copy-start(s32[16]{0:T(128)} %param.10) | copy-start | bytes 196
  11.2 0.7 %copy-start.1 = (s32[32]{0:T(128)S(1)}, s32[32]{0:T(128)}, u32[]{:S(2)}) copy-start(s32[32]{0:T(128)} %param.11) | copy-start | bytes 388
  14.8 2.6 %collective-permute-start.1 = (f32[16,64]{1,0:T(8,128)S(1)}, f32[16,64]{1,0:T(8,128)S(1)}, u32[]{:S(2)}, u32[]{:S(2)}) collective-permute-start(f32[16,64]{1,0:T(8,128)S(1)} %get-tuple-element.24.x_ref), channel_id=1, source_target_pairs={{0,1},{1,0},{2,3},{3,2},{4,5},{5,4},{6,7},{7,6},{8,9},{9,8},{10,11... | collective-permute-start | bytes 12296 | tf_op jit(solution)/shard_map/ppermute | solution.py:269
  20.3 15.2 %all-to-all-start.1 = ((bf16[8,8,2048]{2,1,0:T(8,128)(2,1)}), bf16[8,8,2048]{2,1,0:T(8,128)(2,1)S(1)}, u32[]{:S(2)}, u32[]{:S(2)}) async-start(bf16[8,8,2048]{2,1,0:T(8,128)(2,1)} %get-tuple-element.32), calls=%async_computation.1 | async-start | bytes 524288 | tf_op jit(solution)/shard_map/all_to_all | solution.py:40
  29.9 5.6 %collective-permute-start.2 = (f32[16,2048]{1,0:T(8,128)S(1)}, f32[16,2048]{1,0:T(8,128)S(1)}, u32[]{:S(2)}, u32[]{:S(2)}) collective-permute-start(f32[16,2048]{1,0:T(8,128)S(1)} %shard_map.69), channel_id=1, source_target_pairs={{0,1},{1,0},{2,3},{3,2},{4,5},{5,4},{6,7},{7,6},{8,9},{9,8},{10,11... | collective-permute-start | bytes 393224 | tf_op jit(solution)/shard_map/ppermute | solution.py:308

commit v5 on v3

--- a/solution.py
+++ b/solution.py
@@ -42,24 +42,18 @@
     )
 
 
-def copies_kernel(v_ref, o_ref, sems):
-    copies = [
-        pltpu.make_async_copy(v_ref, o_ref.at[b], sems.at[b]) for b in range(o_ref.shape[0])
-    ]
-    for c in copies:
-        c.start()
-    for c in copies:
-        c.wait()
-
-
 def ready_kernel(
-    batches, ra_ref, sr_ref, down_ref, up_ref, upo_ref, keep_ref, place_ref, sel_ref, downv_ref, upv_ref, sems
+    batches, ra_in, sr_in, down_ref, up_ref, upo_ref, w_ref,
+    keep_ref, place_ref, sel_ref, downv_ref, upv_ref, wv_ref, ra_ref, sr_ref, sems, index_sems
 ):
     me = lax.axis_index("batch")
     core = lax.axis_index("tensor")
     rows, hidden = up_ref.shape
     cols = hidden // (2 * batches)
-    copies = [pltpu.make_async_copy(down_ref, downv_ref, sems.at[0])]
+    copies = [
+        pltpu.make_async_copy(down_ref, downv_ref, sems.at[0]),
+        pltpu.make_async_copy(w_ref.at[: wv_ref.shape[0]], wv_ref, sems.at[2 * batches + 1]),
+    ]
     for d, b in enumerate(order_of(batches)):
         span = pl.ds(pl.multiple_of((2 * b + core) * cols, LANES), cols)
         for k, ref in enumerate((up_ref, upo_ref)):
@@ -70,8 +64,14 @@
                     sems.at[1 + 2 * d + k],
                 )
             )
-    for c in copies:
+    indices = [
+        pltpu.make_async_copy(ra_in, ra_ref, index_sems.at[0]),
+        pltpu.make_async_copy(sr_in, sr_ref, index_sems.at[1]),
+    ]
+    for c in indices + copies:
         c.start()
+    for c in indices:
+        c.wait()
     requests, adapters = ra_ref.shape[1], sr_ref.shape[1]
     here = adapters // batches
 
@@ -114,7 +114,7 @@
     )
 
 
-def delta_kernel(here, x_ref, xo_ref, keep_ref, place_ref, up_ref, acc_ref, d_ref):
+def delta_kernel(here, x_ref, xo_ref, keep_ref, place_ref, up_ref, acc_ref, out_ref, d_ref, sems):
     batches, _, cols = d_ref.shape
     core = lax.axis_index("tensor")
     wide = x_ref.shape[1]
@@ -135,10 +135,15 @@
         source = jnp.where(within, h * rank + k - h * half, source)
     pick = jnp.where(i == source + side * half, 1.0, 0.0).astype(BF16)
     rows = jnp.dot(rows, pick, preferred_element_type=F32).astype(BF16)
+    copies = []
     for d in range(batches):
         d_ref[d] = jnp.dot(
             rows, up_ref[:, d * cols : (d + 1) * cols], preferred_element_type=F32
         ).astype(BF16)
+        copies.append(pltpu.make_async_copy(d_ref.at[d], out_ref.at[d], sems.at[d]))
+        copies[d].start()
+    for c in copies:
+        c.wait()
 
 
 def stream(step, first, count, f_ref, w_ref, buf, sems, add):
@@ -159,11 +164,10 @@
             copy(i + depth).start()
 
 
-def head_kernel(step, count, f_ref, w_ref, acc_ref, buf, sems):
-    def add(i, part):
-        acc_ref[...] = part if i == 0 else acc_ref[...] + part
-
-    stream(step, 0, count, f_ref, w_ref, buf, sems, add)
+def head_kernel(f_ref, w_ref, acc_ref):
+    acc_ref[...] = jnp.dot(
+        f_ref[:, : w_ref.shape[0]], w_ref[...], preferred_element_type=F32
+    )
 
 
 def base_kernel(own, step, first, count, f_ref, head_ref, w_ref, acc_ref, buf, sems):
@@ -184,7 +188,7 @@
     o_ref[...] = jnp.square(jnp.maximum(total, 0.0)).astype(BF16)
 
 
-def call(kernel, out, places, cost=None, limit=6, scratch=()):
+def call(kernel, out, places, cost=None, limit=6, scratch=(), outs=None):
     spec = {"v": pl.BlockSpec(memory_space=VMEM), "h": pl.BlockSpec(memory_space=pltpu.HBM),
             "a": pl.BlockSpec(memory_space=pl.ANY)}
     many = isinstance(out, (list, tuple))
@@ -192,7 +196,7 @@
         kernel,
         out_shape=out,
         in_specs=[spec[p] for p in places],
-        out_specs=[spec["v"]] * len(out) if many else spec["v"],
+        out_specs=[spec[p] for p in outs or "v" * len(out)] if many else spec["v"],
         compiler_params=pltpu.CompilerParams(vmem_limit_bytes=limit * MIB),
         cost_estimate=cost,
         scratch_shapes=scratch,
@@ -216,9 +220,11 @@
     up = up.reshape(-1, hidden)
     up_other = swap(up)
     down = jnp.transpose(down, (0, 2, 1)).reshape(wide, width)
-    sent = call(copies_kernel, shape((batches,) + features.shape, BF16), "h", scratch=[dma((batches,))])(in_hbm(features))
+    sent = jnp.broadcast_to(features[None], (batches,) + features.shape)
     gathered = exchange(sent)
-    keep, place, sel, down, up = call(
+    step = 256
+    head = 1
+    keep, place, sel, down, up, first = call(
         functools.partial(ready_kernel, batches),
         [
             shape((requests, wide), F32),
@@ -226,11 +232,24 @@
             shape((requests, batches * OWN_MOST), BF16),
             VMEM(down.shape, BF16),
             VMEM((wide, hidden // 2), BF16),
+            VMEM((head * step, 2 * cols), BF16),
         ],
-        "vvhha",
+        "hhhhhh",
         moves(6 * up.size),
-        scratch=[dma((1 + 2 * batches,))],
-    )(request_adapter.reshape(1, -1), storage_row.reshape(1, -1), in_hbm(down), in_hbm(up), up_other)
+        scratch=[
+            VMEM((1, requests), jnp.int32),
+            VMEM((1, storage_row.shape[0]), jnp.int32),
+            dma((2 + 2 * batches,)),
+            dma((2,)),
+        ],
+    )(
+        in_hbm(request_adapter.reshape(1, -1)),
+        in_hbm(storage_row.reshape(1, -1)),
+        in_hbm(down),
+        in_hbm(up),
+        in_hbm(up_other),
+        in_hbm(up_weight),
+    )
     x, rows = call(
         shrink_kernel,
         [shape((requests, wide), F32), shape((requests, width), BF16)],
@@ -238,20 +257,20 @@
         scratch=[VMEM((requests, width), F32)],
     )(gathered, in_vmem(down))
     x_other = swap(x)
-    step = 256
-    head = 1
     blocks = width // step
     flops = 2 * requests * step * 2 * cols
     acc = call(
-        functools.partial(head_kernel, step, head),
+        head_kernel,
         shape((requests, 2 * cols), F32),
-        "vh",
+        "vv",
         moves(head * 4 * step * cols, head * flops),
-        16,
-        [VMEM((head, step, 2 * cols), BF16), dma((head,))],
-    )(rows, in_hbm(up_weight))
-    delta = call(
-        functools.partial(delta_kernel, here), shape((batches, OWN_MOST, cols), BF16), "vvvvva"
+    )(rows, in_vmem(first))
+    (delta,) = call(
+        functools.partial(delta_kernel, here),
+        [pltpu.HBM((batches, OWN_MOST, cols), BF16)],
+        "vvvvva",
+        scratch=[VMEM((batches, OWN_MOST, cols), BF16), dma((batches,))],
+        outs="h",
     )(x, x_other, keep, place, in_vmem(up), acc)
     received = exchange(delta)
     rest = blocks - head

time: 36.4 us -> 35.7 us (0.981)
  Pallas kernels: 19.6 us -> 17.2 us
  local copies, waits for them, and re-layouts: 2.72 us -> 4.21 us
  starting transfers between devices: 12.4 us -> 13 us
    pallas_call x3 -> x2, Pallas kernels: 5.23 us -> 1.75 us  [the longest x1 1.34 us: per_device(): call(functools.partial(delta_kernel, here), [pltpu.HBM((batches, OWN_MOST...]
    broadcast_in_dim x0 -> x1, local copies, waits for them, and re-layouts: none -> 1.44 us  [per_device(): sent = jnp.broadcast_to(features[None], (batches,) + features.shape)]
    all_to_all x2, waiting for transfers between devices: 1.1 us -> 0.03 us  [exchange(): lax.all_to_all(x, 'batch', 0, 0, tiled=True, axis_index_groups=[order_of(...]
    pallas_call x1, Pallas kernels: 1.56 us -> 2.61 us  [per_device(): call(functools.partial(ready_kernel, batches), [shape((requests, wide), F...]
    all_to_all x2, starting transfers between devices: 11.6 us -> 12.5 us  [exchange(): lax.all_to_all(x, 'batch', 0, 0, tiled=True, axis_index_groups=[order_of(...]
    ppermute x1, waiting for transfers between devices: 0.01 us -> 0.79 us  [per_device(): x_other = swap(x)]
    unnamed x8 -> x6, local copies, waits for them, and re-layouts: 2.72 us -> 2.77 us
  transfers between devices with their start and end apart: 5 -> 5, of which waited for: 1 -> 1; matrix products, arithmetic and copies ran while one was open for 0% -> 4% of each run, Pallas kernels for 48% -> 42%
where the time goes in v5:
time: 35.7 us; the launch traced here: 35.3 us
  Pallas kernels  17.2 us (48%)
  starting transfers between devices  13 us (36%)
  local copies, waits for them, and re-layouts  4.21 us (12%)
  waiting for transfers between devices  0.83 us (2%)
    all_to_all x2, starting transfers between devices, exchange(): lax.all_to_all(x, 'batch', 0, 0, tiled=True, axis_index_groups=[order_of(...  12.5 us
    pallas_call x2, Pallas kernels, base(): call(functools.partial(base_kernel, own, step, head, rest), shape((reques...  11.8 us
    unnamed x6, local copies, waits for them, and re-layouts  2.77 us
    pallas_call x1, Pallas kernels, per_device(): call(functools.partial(ready_kernel, batches), [shape((requests, wide), F...  2.61 us
    broadcast_in_dim x1, local copies, waits for them, and re-layouts, per_device(): sent = jnp.broadcast_to(features[None], (batches,) + features.shape)  1.44 us
    pallas_call x1, Pallas kernels, per_device(): call(functools.partial(delta_kernel, here), [pltpu.HBM((batches, OWN_MOST...  1.34 us
    pallas_call x1, Pallas kernels, per_device(): call(final_kernel, shape((requests, cols), BF16), 'vvvv')  0.79 us
    ppermute x1, waiting for transfers between devices, per_device(): x_other = swap(x)  0.79 us
  transfers between devices with their start and end apart: 5, of which 1 were waited for; matrix products, arithmetic and copies ran while one was open for 4% of the time, Pallas kernels for 42%

profile of v5, /device:TPU:0, one launch (start us, length us, event | category | flops | bytes accessed | tf_op | source)
XLA Modules:
  0.0 35.3 jit_solution(8662284530982404961)
XLA Ops:
  0.0 0.5 %collective-permute-start = (bf16[32,32768]{1,0:T(8,128)(2,1)}, bf16[32,32768]{1,0:T(8,128)(2,1)S(1)}, u32[]{:S(2)}, u32[]{:S(2)}) collective-permute-start(bf16[32,32768]{1,0:T(8,128)(2,1)} %bitcast.8), channel_id=1, source_target_pairs={{0,1},{1,0},{2,3},{3,2},{4,5},{5,4},{6,7},{7,6},{8,9},{9,8},{10,11... | collective-permute-start | bytes 6291464 | tf_op jit(solution)/shard_map/ppermute | solution.py:221
  0.5 1.4 %broadcast_in_dim.2 = bf16[8,2,4096]{2,1,0:T(2,128)(2,1)} broadcast(bf16[2,4096]{1,0:T(2,128)(2,1)} %param.6), dimensions={1,2} | broadcast | bytes 147456 | tf_op jit(solution)/shard_map/broadcast_in_dim | solution.py:223
  1.9 7.4 %all-to-all-start = ((bf16[8,2,4096]{2,1,0:T(2,128)(2,1)}), bf16[8,2,4096]{2,1,0:T(2,128)(2,1)S(1)}, u32[]{:S(2)}, u32[]{:S(2)}) async-start(bf16[8,2,4096]{2,1,0:T(2,128)(2,1)} %broadcast_in_dim.2), calls=%async_computation | async-start | bytes 262144 | tf_op jit(solution)/shard_map/all_to_all | solution.py:40
  9.3 0.0 collective-permute-done.upo_ref
  9.3 0.0 copy-start.2
  9.3 1.3 %copy-done.2 = bf16[32,32768]{1,0:T(8,128)(2,1)} copy-done((bf16[32,32768]{1,0:T(8,128)(2,1)}, bf16[32,32768]{1,0:T(8,128)(2,1)S(1)}, u32[]{:S(2)}) %copy-start.2) | copy-done | bytes 2097176
  10.6 2.6 %shard_map.64 = (f32[16,64]{1,0:T(8,128)S(1)}, bf16[16,8]{1,0:T(8,128)(2,1)S(1)}, bf16[16,64]{1,0:T(8,128)(2,1)S(1)}, bf16[64,4096]{1,0:T(8,128)(2,1)S(1)}, bf16...) custom-call(s32[1,16]{1,0:T(1,128)} %bitcast.11, s32[1,32]{1,0:T(1,128)} %bitcast.12, bf16[64,4096]{1,0:T(8,128)(2,1)} %bitcast.10, ...), custom_call_target="tpu_custom_call" | custom-call | bytes 6291456 | tf_op jit(solution)/shard_map/pallas_call | solution.py:227
  13.2 0.0 copy-start
  13.2 1.3 %copy-done = bf16[64,16384]{1,0:T(8,128)(2,1)} copy-done((bf16[64,16384]{1,0:T(8,128)(2,1)}, bf16[64,16384]{1,0:T(8,128)(2,1)S(1)}, u32[]{:S(2)}) %copy-start) | copy-done | bytes 2097176
  14.5 0.0 all-to-all-done.g_ref
  14.6 0.0 copy-start.1
  14.6 0.3 shard_map.65
  14.8 0.0 collective-permute-start.2
  14.8 0.4 %shard_map.66.head_ref.acc_ref = f32[16,4096]{1,0:T(8,128)S(1)} custom-call(bf16[16,4096]{1,0:T(8,128)(2,1)S(1)} %get-tuple-element.15.f_ref, bf16[256,4096]{1,0:T(8,128)(2,1)S(1)} %get-tuple-element.16.w_ref), custom_call_target="tpu_custom_call" | custom-call | flops 33554432 | bytes 2097152 | tf_op jit(solution)/shard_map/pallas_call | solution.py:262
  15.2 0.8 %collective-permute-done.2.xo_ref = f32[16,64]{1,0:T(8,128)S(1)} collective-permute-done((f32[16,64]{1,0:T(8,128)S(1)}, f32[16,64]{1,0:T(8,128)S(1)}, u32[]{:S(2)}, u32[]{:S(2)}) %collective-permute-start.2) | collective-permute-done | bytes 4128 | tf_op jit(solution)/shard_map/ppermute | solution.py:259
  16.0 0.1 copy-done.1
  16.2 1.3 %shard_map.69 = bf16[8,8,2048]{2,1,0:T(8,128)(2,1)} custom-call(f32[16,64]{1,0:T(8,128)S(1)} %get-tuple-element.17.x_ref, f32[16,64]{1,0:T(8,128)S(1)} %collective-permute-done.2.xo_ref, f32[16,64]{1,0:T(8,128)S(1)} %get-tuple-element.18.keep_ref, bf16[16,8]{1,0:T(8,128)(2,1)S(1)} %get-tuple-element.19.place_ref, bf16[64,16384]{1,0:T(8,128)(2,1)S(1)} %copy-done.1, ...), custom_call_target="tpu_custom_call" | custom-call | tf_op jit(solution)/shard_map/pallas_call | solution.py:268
  17.5 5.1 %all-to-all-start.1 = ((bf16[8,8,2048]{2,1,0:T(8,128)(2,1)}), bf16[8,8,2048]{2,1,0:T(8,128)(2,1)S(1)}, u32[]{:S(2)}, u32[]{:S(2)}) async-start(bf16[8,8,2048]{2,1,0:T(8,128)(2,1)} %shard_map.69), calls=%async_computation.1 | async-start | bytes 524288 | tf_op jit(solution)/shard_map/all_to_all | solution.py:40
  22.6 5.9 %shard_map.68 = f32[16,2048]{1,0:T(8,128)S(1)} custom-call(bf16[16,4096]{1,0:T(8,128)(2,1)S(1)} %get-tuple-element.15.f_ref, f32[16,4096]{1,0:T(8,128)S(1)} %shard_map.66.head_ref.acc_ref, bf16[4096,4096]{1,0:T(8,128)(2,1)} %w_ref.5), custom_call_target="tpu_custom_call" | custom-call | flops 251658240 | bytes 15728640 | tf_op jit(solution)/shard_map/pallas_call | solution.py:279
  28.5 0.1 collective-permute-start.1
  28.6 5.9 %shard_map.67.keep_ref = f32[16,2048]{1,0:T(8,128)S(1)} custom-call(bf16[16,4096]{1,0:T(8,128)(2,1)S(1)} %get-tuple-element.15.f_ref, f32[16,4096]{1,0:T(8,128)S(1)} %shard_map.66.head_ref.acc_ref, bf16[4096,4096]{1,0:T(8,128)(2,1)} %w_ref.5), custom_call_target="tpu_custom_call" | custom-call | flops 251658240 | bytes 15728640 | tf_op jit(solution)/shard_map/pallas_call | solution.py:279
  34.5 0.0 collective-permute-done.1.got_ref
  34.5 0.0 all-to-all-done.1
  34.5 0.8 %shard_map.70 = bf16[16,2048]{1,0:T(8,128)(2,1)} custom-call(bf16[16,64]{1,0:T(8,128)(2,1)S(1)} %get-tuple-element.13.sel_ref, f32[16,2048]{1,0:T(8,128)S(1)} %shard_map.67.keep_ref, f32[16,2048]{1,0:T(8,128)S(1)} %collective-permute-done.1.got_ref, bf16[64,2048]{1,0:T(8,128)(2,1)S(1)} %bitcast.7), custom_call_target="tpu_custom_call" | custom-call | tf_op jit(solution)/shard_map/pallas_call | solution.py:290
Async XLA Ops:
  0.0 9.3 %collective-permute-start = (bf16[32,32768]{1,0:T(8,128)(2,1)}, bf16[32,32768]{1,0:T(8,128)(2,1)S(1)}, u32[]{:S(2)}, u32[]{:S(2)}) collective-permute-start(bf16[32,32768]{1,0:T(8,128)(2,1)} %bitcast.8), channel_id=1, source_target_pairs={{0,1},{1,0},{2,3},{3,2},{4,5},{5,4},{6,7},{7,6},{8,9},{9,8},{10,11... | collective-permute-start | bytes 6291464 | tf_op jit(solution)/shard_map/ppermute | solution.py:221
  1.9 12.7 %all-to-all-start = ((bf16[8,2,4096]{2,1,0:T(2,128)(2,1)}), bf16[8,2,4096]{2,1,0:T(2,128)(2,1)S(1)}, u32[]{:S(2)}, u32[]{:S(2)}) async-start(bf16[8,2,4096]{2,1,0:T(2,128)(2,1)} %broadcast_in_dim.2), calls=%async_computation | async-start | bytes 262144 | tf_op jit(solution)/shard_map/all_to_all | solution.py:40
  9.3 1.3 %copy-start.2 = (bf16[32,32768]{1,0:T(8,128)(2,1)}, bf16[32,32768]{1,0:T(8,128)(2,1)S(1)}, u32[]{:S(2)}) copy-start(bf16[32,32768]{1,0:T(8,128)(2,1)S(1)} %collective-permute-done.upo_ref) | copy-start | bytes 6291460
  13.2 1.3 %copy-start = (bf16[64,16384]{1,0:T(8,128)(2,1)}, bf16[64,16384]{1,0:T(8,128)(2,1)S(1)}, u32[]{:S(2)}) copy-start(bf16[64,16384]{1,0:T(8,128)(2,1)S(1)} %get-tuple-element.20.up_ref) | copy-start | bytes 6291460
  14.6 1.6 %copy-start.1 = (bf16[64,16384]{1,0:T(8,128)(2,1)S(1)}, bf16[64,16384]{1,0:T(8,128)(2,1)}, u32[]{:S(2)}) copy-start(bf16[64,16384]{1,0:T(8,128)(2,1)} %copy-done) | copy-start | bytes 6291460
  14.8 1.2 %collective-permute-start.2 = (f32[16,64]{1,0:T(8,128)S(1)}, f32[16,64]{1,0:T(8,128)S(1)}, u32[]{:S(2)}, u32[]{:S(2)}) collective-permute-start(f32[16,64]{1,0:T(8,128)S(1)} %get-tuple-element.17.x_ref), channel_id=1, source_target_pairs={{0,1},{1,0},{2,3},{3,2},{4,5},{5,4},{6,7},{7,6},{8,9},{9,8},{10,11... | collective-permute-start | bytes 12296 | tf_op jit(solution)/shard_map/ppermute | solution.py:259
  17.5 17.0 %all-to-all-start.1 = ((bf16[8,8,2048]{2,1,0:T(8,128)(2,1)}), bf16[8,8,2048]{2,1,0:T(8,128)(2,1)S(1)}, u32[]{:S(2)}, u32[]{:S(2)}) async-start(bf16[8,8,2048]{2,1,0:T(8,128)(2,1)} %shard_map.69), calls=%async_computation.1 | async-start | bytes 524288 | tf_op jit(solution)/shard_map/all_to_all | solution.py:40
  28.5 6.0 %collective-permute-start.1 = (f32[16,2048]{1,0:T(8,128)S(1)}, f32[16,2048]{1,0:T(8,128)S(1)}, u32[]{:S(2)}, u32[]{:S(2)}) collective-permute-start(f32[16,2048]{1,0:T(8,128)S(1)} %shard_map.68), channel_id=1, source_target_pairs={{0,1},{1,0},{2,3},{3,2},{4,5},{5,4},{6,7},{7,6},{8,9},{9,8},{10,11... | collective-permute-start | bytes 393224 | tf_op jit(solution)/shard_map/ppermute | solution.py:288

commit v6 on v5

--- a/solution.py
+++ b/solution.py
@@ -44,23 +44,24 @@
 
 def ready_kernel(
     batches, ra_in, sr_in, down_ref, up_ref, upo_ref, w_ref,
-    keep_ref, place_ref, sel_ref, downv_ref, upv_ref, wv_ref, ra_ref, sr_ref, sems, index_sems
+    keep_ref, place_ref, sel_ref, downv_ref, upv_ref, wv_ref, ra_ref, sr_ref, stage, sems, index_sems
 ):
     me = lax.axis_index("batch")
     core = lax.axis_index("tensor")
     rows, hidden = up_ref.shape
     cols = hidden // (2 * batches)
-    copies = [
+    last = [
         pltpu.make_async_copy(down_ref, downv_ref, sems.at[0]),
         pltpu.make_async_copy(w_ref.at[: wv_ref.shape[0]], wv_ref, sems.at[2 * batches + 1]),
     ]
+    copies = []
     for d, b in enumerate(order_of(batches)):
         span = pl.ds(pl.multiple_of((2 * b + core) * cols, LANES), cols)
         for k, ref in enumerate((up_ref, upo_ref)):
             copies.append(
                 pltpu.make_async_copy(
                     ref.at[:, span],
-                    upv_ref.at[k * rows : (k + 1) * rows, d * cols : (d + 1) * cols],
+                    stage.at[k * rows : (k + 1) * rows, d * cols : (d + 1) * cols],
                     sems.at[1 + 2 * d + k],
                 )
             )
@@ -68,7 +69,7 @@
         pltpu.make_async_copy(ra_in, ra_ref, index_sems.at[0]),
         pltpu.make_async_copy(sr_in, sr_ref, index_sems.at[1]),
     ]
-    for c in indices + copies:
+    for c in indices + copies + last:
         c.start()
     for c in indices:
         c.wait()
@@ -101,6 +102,10 @@
         iota(sel_ref.shape, 1) == place_in_order(owner, batches) * OWN_MOST + rank, 1.0, 0.0
     ).astype(BF16)
     for c in copies:
+        c.wait()
+    back = pltpu.make_async_copy(stage, upv_ref, sems.at[2 * batches + 2])
+    back.start()
+    for c in last + [back]:
         c.wait()
 
 
@@ -231,7 +236,7 @@
             shape((requests, OWN_MOST), BF16),
             shape((requests, batches * OWN_MOST), BF16),
             VMEM(down.shape, BF16),
-            VMEM((wide, hidden // 2), BF16),
+            pltpu.HBM((wide, hidden // 2), BF16),
             VMEM((head * step, 2 * cols), BF16),
         ],
         "hhhhhh",
@@ -239,9 +244,11 @@
         scratch=[
             VMEM((1, requests), jnp.int32),
             VMEM((1, storage_row.shape[0]), jnp.int32),
-            dma((2 + 2 * batches,)),
+            VMEM((wide, hidden // 2), BF16),
+            dma((3 + 2 * batches,)),
             dma((2,)),
         ],
+        outs="vvvvhv",
     )(
         in_hbm(request_adapter.reshape(1, -1)),
         in_hbm(storage_row.reshape(1, -1)),
@@ -271,7 +278,7 @@
         "vvvvva",
         scratch=[VMEM((batches, OWN_MOST, cols), BF16), dma((batches,))],
         outs="h",
-    )(x, x_other, keep, place, in_vmem(up), acc)
+    )(x, x_other, keep, place, up, acc)
     received = exchange(delta)
     rest = blocks - head
 

time: 35.7 us -> 35.2 us (0.986)
  local copies, waits for them, and re-layouts: 4.21 us -> 2.87 us
  Pallas kernels: 17.2 us -> 18 us
  starting transfers between devices: 13 us -> 12.5 us
  waiting for transfers between devices: 0.83 us -> 1.32 us
    unnamed x6 -> x4, local copies, waits for them, and re-layouts: 2.77 us -> 1.44 us
    pallas_call x1, Pallas kernels: 2.61 us -> 3.45 us  [per_device(): call(functools.partial(ready_kernel, batches), [shape((requests, wide), F...]
    all_to_all x2, waiting for transfers between devices: 0.03 us -> 0.52 us  [exchange(): lax.all_to_all(x, 'batch', 0, 0, tiled=True, axis_index_groups=[order_of(...]
    all_to_all x2, starting transfers between devices: 12.5 us -> 12 us  [exchange(): lax.all_to_all(x, 'batch', 0, 0, tiled=True, axis_index_groups=[order_of(...]
  transfers between devices with their start and end apart: 5 -> 5, of which waited for: 1 -> 2; matrix products, arithmetic and copies ran while one was open for 4% -> 4% of each run, Pallas kernels for 42% -> 45%
where the time goes in v6:
time: 35.2 us; the launch traced here: 34.8 us
  Pallas kernels  18 us (51%)
  starting transfers between devices  12.5 us (36%)
  local copies, waits for them, and re-layouts  2.87 us (8%)
  waiting for transfers between devices  1.32 us (4%)
    all_to_all x2, starting transfers between devices, exchange(): lax.all_to_all(x, 'batch', 0, 0, tiled=True, axis_index_groups=[order_of(...  12 us
    pallas_call x2, Pallas kernels, base(): call(functools.partial(base_kernel, own, step, head, rest), shape((reques...  11.8 us
    pallas_call x1, Pallas kernels, per_device(): call(functools.partial(ready_kernel, batches), [shape((requests, wide), F...  3.45 us
    unnamed x4, local copies, waits for them, and re-layouts  1.44 us
    broadcast_in_dim x1, local copies, waits for them, and re-layouts, per_device(): sent = jnp.broadcast_to(features[None], (batches,) + features.shape)  1.43 us
    pallas_call x1, Pallas kernels, per_device(): call(functools.partial(delta_kernel, here), [pltpu.HBM((batches, OWN_MOST...  1.36 us
    pallas_call x1, Pallas kernels, per_device(): call(final_kernel, shape((requests, cols), BF16), 'vvvv')  0.79 us
    ppermute x1, waiting for transfers between devices, per_device(): x_other = swap(x)  0.79 us
  transfers between devices with their start and end apart: 5, of which 2 were waited for; matrix products, arithmetic and copies ran while one was open for 4% of the time, Pallas kernels for 45%

profile of v6, /device:TPU:0, one launch (start us, length us, event | category | flops | bytes accessed | tf_op | source)
XLA Modules:
  0.0 34.8 jit_solution(7670149318488331719)
XLA Ops:
  0.0 0.5 %collective-permute-start = (bf16[32,32768]{1,0:T(8,128)(2,1)}, bf16[32,32768]{1,0:T(8,128)(2,1)S(1)}, u32[]{:S(2)}, u32[]{:S(2)}) collective-permute-start(bf16[32,32768]{1,0:T(8,128)(2,1)} %bitcast.8), channel_id=1, source_target_pairs={{0,1},{1,0},{2,3},{3,2},{4,5},{5,4},{6,7},{7,6},{8,9},{9,8},{10,11... | collective-permute-start | bytes 6291464 | tf_op jit(solution)/shard_map/ppermute | solution.py:226
  0.5 1.4 %broadcast_in_dim.2 = bf16[8,2,4096]{2,1,0:T(2,128)(2,1)} broadcast(bf16[2,4096]{1,0:T(2,128)(2,1)} %param.6), dimensions={1,2} | broadcast | bytes 147456 | tf_op jit(solution)/shard_map/broadcast_in_dim | solution.py:228
  1.9 7.4 %all-to-all-start = ((bf16[8,2,4096]{2,1,0:T(2,128)(2,1)}), bf16[8,2,4096]{2,1,0:T(2,128)(2,1)S(1)}, u32[]{:S(2)}, u32[]{:S(2)}) async-start(bf16[8,2,4096]{2,1,0:T(2,128)(2,1)} %broadcast_in_dim.2), calls=%async_computation | async-start | bytes 262144 | tf_op jit(solution)/shard_map/all_to_all | solution.py:40
  9.2 0.0 collective-permute-done.upo_ref
  9.2 0.0 copy-start.1
  9.3 1.3 %copy-done.1 = bf16[32,32768]{1,0:T(8,128)(2,1)} copy-done((bf16[32,32768]{1,0:T(8,128)(2,1)}, bf16[32,32768]{1,0:T(8,128)(2,1)S(1)}, u32[]{:S(2)}) %copy-start.1) | copy-done | bytes 2097176
  10.6 3.5 %shard_map.64 = (f32[16,64]{1,0:T(8,128)S(1)}, bf16[16,8]{1,0:T(8,128)(2,1)S(1)}, bf16[16,64]{1,0:T(8,128)(2,1)S(1)}, bf16[64,4096]{1,0:T(8,128)(2,1)S(1)}, bf16...) custom-call(s32[1,16]{1,0:T(1,128)} %bitcast.11, s32[1,32]{1,0:T(1,128)} %bitcast.12, bf16[64,4096]{1,0:T(8,128)(2,1)} %bitcast.10, ...), custom_call_target="tpu_custom_call" | custom-call | bytes 6291456 | tf_op jit(solution)/shard_map/pallas_call | solution.py:232
  14.0 0.5 %all-to-all-done.g_ref = bf16[8,2,4096]{2,1,0:T(2,128)(2,1)S(1)} async-done(((bf16[8,2,4096]{2,1,0:T(2,128)(2,1)}), bf16[8,2,4096]{2,1,0:T(2,128)(2,1)S(1)}, u32[]{:S(2)}, u32[]{:S(2)}) %all-to-all-start) | async-done | bytes 131104 | tf_op jit(solution)/shard_map/all_to_all | solution.py:40
  14.6 0.0 copy-start
  14.6 0.3 shard_map.65
  14.8 0.0 collective-permute-start.2
  14.8 0.4 %shard_map.66.head_ref.acc_ref = f32[16,4096]{1,0:T(8,128)S(1)} custom-call(bf16[16,4096]{1,0:T(8,128)(2,1)S(1)} %get-tuple-element.15.f_ref, bf16[256,4096]{1,0:T(8,128)(2,1)S(1)} %get-tuple-element.16.w_ref), custom_call_target="tpu_custom_call" | custom-call | flops 33554432 | bytes 2097152 | tf_op jit(solution)/shard_map/pallas_call | solution.py:269
  15.2 0.8 %collective-permute-done.2.xo_ref = f32[16,64]{1,0:T(8,128)S(1)} collective-permute-done((f32[16,64]{1,0:T(8,128)S(1)}, f32[16,64]{1,0:T(8,128)S(1)}, u32[]{:S(2)}, u32[]{:S(2)}) %collective-permute-start.2) | collective-permute-done | bytes 4128 | tf_op jit(solution)/shard_map/ppermute | solution.py:266
  16.0 0.1 copy-done
  16.1 1.4 %shard_map.69 = bf16[8,8,2048]{2,1,0:T(8,128)(2,1)} custom-call(f32[16,64]{1,0:T(8,128)S(1)} %get-tuple-element.17.x_ref, f32[16,64]{1,0:T(8,128)S(1)} %collective-permute-done.2.xo_ref, f32[16,64]{1,0:T(8,128)S(1)} %get-tuple-element.18.keep_ref, bf16[16,8]{1,0:T(8,128)(2,1)S(1)} %get-tuple-element.19.place_ref, bf16[64,16384]{1,0:T(8,128)(2,1)S(1)} %copy-done, ...), custom_call_target="tpu_custom_call" | custom-call | tf_op jit(solution)/shard_map/pallas_call | solution.py:275
  17.5 4.6 %all-to-all-start.1 = ((bf16[8,8,2048]{2,1,0:T(8,128)(2,1)}), bf16[8,8,2048]{2,1,0:T(8,128)(2,1)S(1)}, u32[]{:S(2)}, u32[]{:S(2)}) async-start(bf16[8,8,2048]{2,1,0:T(8,128)(2,1)} %shard_map.69), calls=%async_computation.1 | async-start | bytes 524288 | tf_op jit(solution)/shard_map/all_to_all | solution.py:40
  22.1 5.9 %shard_map.68 = f32[16,2048]{1,0:T(8,128)S(1)} custom-call(bf16[16,4096]{1,0:T(8,128)(2,1)S(1)} %get-tuple-element.15.f_ref, f32[16,4096]{1,0:T(8,128)S(1)} %shard_map.66.head_ref.acc_ref, bf16[4096,4096]{1,0:T(8,128)(2,1)} %w_ref.5), custom_call_target="tpu_custom_call" | custom-call | flops 251658240 | bytes 15728640 | tf_op jit(solution)/shard_map/pallas_call | solution.py:286
  28.0 0.1 collective-permute-start.1
  28.1 5.9 %shard_map.67.keep_ref = f32[16,2048]{1,0:T(8,128)S(1)} custom-call(bf16[16,4096]{1,0:T(8,128)(2,1)S(1)} %get-tuple-element.15.f_ref, f32[16,4096]{1,0:T(8,128)S(1)} %shard_map.66.head_ref.acc_ref, bf16[4096,4096]{1,0:T(8,128)(2,1)} %w_ref.5), custom_call_target="tpu_custom_call" | custom-call | flops 251658240 | bytes 15728640 | tf_op jit(solution)/shard_map/pallas_call | solution.py:286
  34.0 0.0 collective-permute-done.1.got_ref
  34.0 0.0 all-to-all-done.1
  34.0 0.8 %shard_map.70 = bf16[16,2048]{1,0:T(8,128)(2,1)} custom-call(bf16[16,64]{1,0:T(8,128)(2,1)S(1)} %get-tuple-element.13.sel_ref, f32[16,2048]{1,0:T(8,128)S(1)} %shard_map.67.keep_ref, f32[16,2048]{1,0:T(8,128)S(1)} %collective-permute-done.1.got_ref, bf16[64,2048]{1,0:T(8,128)(2,1)S(1)} %bitcast.7), custom_call_target="tpu_custom_call" | custom-call | tf_op jit(solution)/shard_map/pallas_call | solution.py:297
Async XLA Ops:
  0.0 9.2 %collective-permute-start = (bf16[32,32768]{1,0:T(8,128)(2,1)}, bf16[32,32768]{1,0:T(8,128)(2,1)S(1)}, u32[]{:S(2)}, u32[]{:S(2)}) collective-permute-start(bf16[32,32768]{1,0:T(8,128)(2,1)} %bitcast.8), channel_id=1, source_target_pairs={{0,1},{1,0},{2,3},{3,2},{4,5},{5,4},{6,7},{7,6},{8,9},{9,8},{10,11... | collective-permute-start | bytes 6291464 | tf_op jit(solution)/shard_map/ppermute | solution.py:226
  1.9 12.7 %all-to-all-start = ((bf16[8,2,4096]{2,1,0:T(2,128)(2,1)}), bf16[8,2,4096]{2,1,0:T(2,128)(2,1)S(1)}, u32[]{:S(2)}, u32[]{:S(2)}) async-start(bf16[8,2,4096]{2,1,0:T(2,128)(2,1)} %broadcast_in_dim.2), calls=%async_computation | async-start | bytes 262144 | tf_op jit(solution)/shard_map/all_to_all | solution.py:40
  9.2 1.3 %copy-start.1 = (bf16[32,32768]{1,0:T(8,128)(2,1)}, bf16[32,32768]{1,0:T(8,128)(2,1)S(1)}, u32[]{:S(2)}) copy-start(bf16[32,32768]{1,0:T(8,128)(2,1)S(1)} %collective-permute-done.upo_ref) | copy-start | bytes 6291460
  14.6 1.6 %copy-start = (bf16[64,16384]{1,0:T(8,128)(2,1)S(1)}, bf16[64,16384]{1,0:T(8,128)(2,1)}, u32[]{:S(2)}) copy-start(bf16[64,16384]{1,0:T(8,128)(2,1)} %get-tuple-element.20.up_ref) | copy-start | bytes 6291460
  14.8 1.2 %collective-permute-start.2 = (f32[16,64]{1,0:T(8,128)S(1)}, f32[16,64]{1,0:T(8,128)S(1)}, u32[]{:S(2)}, u32[]{:S(2)}) collective-permute-start(f32[16,64]{1,0:T(8,128)S(1)} %get-tuple-element.17.x_ref), channel_id=1, source_target_pairs={{0,1},{1,0},{2,3},{3,2},{4,5},{5,4},{6,7},{7,6},{8,9},{9,8},{10,11... | collective-permute-start | bytes 12296 | tf_op jit(solution)/shard_map/ppermute | solution.py:266
  17.5 16.5 %all-to-all-start.1 = ((bf16[8,8,2048]{2,1,0:T(8,128)(2,1)}), bf16[8,8,2048]{2,1,0:T(8,128)(2,1)S(1)}, u32[]{:S(2)}, u32[]{:S(2)}) async-start(bf16[8,8,2048]{2,1,0:T(8,128)(2,1)} %shard_map.69), calls=%async_computation.1 | async-start | bytes 524288 | tf_op jit(solution)/shard_map/all_to_all | solution.py:40
  28.0 6.0 %collective-permute-start.1 = (f32[16,2048]{1,0:T(8,128)S(1)}, f32[16,2048]{1,0:T(8,128)S(1)}, u32[]{:S(2)}, u32[]{:S(2)}) collective-permute-start(f32[16,2048]{1,0:T(8,128)S(1)} %shard_map.68), channel_id=1, source_target_pairs={{0,1},{1,0},{2,3},{3,2},{4,5},{5,4},{6,7},{7,6},{8,9},{9,8},{10,11... | collective-permute-start | bytes 393224 | tf_op jit(solution)/shard_map/ppermute | solution.py:295

commit v7 on v6

--- a/solution.py
+++ b/solution.py
@@ -151,40 +151,51 @@
         c.wait()
 
 
-def stream(step, first, count, f_ref, w_ref, buf, sems, add):
-    depth = buf.shape[0]
-
-    def copy(i):
-        return pltpu.make_async_copy(
-            w_ref.at[pl.ds((first + i) * step, step)], buf.at[i % depth], sems.at[i % depth]
-        )
-
-    for i in range(min(depth, count)):
-        copy(i).start()
-    for i in range(count):
-        copy(i).wait()
-        k = (first + i) * step
-        add(i, jnp.dot(f_ref[:, k : k + step], buf[i % depth], preferred_element_type=F32))
-        if i + depth < count:
-            copy(i + depth).start()
-
-
 def head_kernel(f_ref, w_ref, acc_ref):
     acc_ref[...] = jnp.dot(
         f_ref[:, : w_ref.shape[0]], w_ref[...], preferred_element_type=F32
     )
 
 
-def base_kernel(own, step, first, count, f_ref, head_ref, w_ref, acc_ref, buf, sems):
+def base_kernel(
+    step, first, count, f_ref, head_ref, w_ref, send_ref, mine_ref, rest_ref, send_buf, mine_buf, sems
+):
     core = lax.axis_index("tensor")
-    cols = acc_ref.shape[1]
-    side = core if own else 1 - core
-    span = pl.ds(pl.multiple_of(side * cols, LANES), cols)
-
-    def add(i, part):
-        acc_ref[...] = part + (head_ref[:, span] if i == 0 else acc_ref[...])
-
-    stream(step, first, count, f_ref, w_ref.at[:, span], buf, sems, add)
+    cols = send_ref.shape[1]
+    other = pl.ds(pl.multiple_of((1 - core) * cols, LANES), cols)
+    own = pl.ds(pl.multiple_of(core * cols, LANES), cols)
+    done = mine_buf.shape[0]
+    copies = []
+    for i in range(count):
+        rows = slice((first + i) * step, (first + i + 1) * step)
+        target = mine_buf.at[i] if i < done else rest_ref.at[i - done]
+        copies.append(
+            (
+                pltpu.make_async_copy(w_ref.at[rows, other], send_buf.at[i], sems.at[i, 0]),
+                pltpu.make_async_copy(w_ref.at[rows, own], target, sems.at[i, 1]),
+            )
+        )
+    for pair in copies:
+        for c in pair:
+            c.start()
+    for i, (to_send, to_keep) in enumerate(copies):
+        f = f_ref[:, (first + i) * step : (first + i + 1) * step]
+        to_send.wait()
+        part = jnp.dot(f, send_buf[i], preferred_element_type=F32)
+        send_ref[...] = part + (send_ref[...] if i else head_ref[:, other])
+        to_keep.wait()
+        if i < done:
+            part = jnp.dot(f, mine_buf[i], preferred_element_type=F32)
+            mine_ref[...] = part + (mine_ref[...] if i else head_ref[:, own])
+
+
+def rest_kernel(first, f_ref, mine_ref, w_ref, o_ref):
+    count, step, _ = w_ref.shape
+    total = mine_ref[...]
+    for i in range(count):
+        k = (first + i) * step
+        total += jnp.dot(f_ref[:, k : k + step], w_ref[i], preferred_element_type=F32)
+    o_ref[...] = total
 
 
 def final_kernel(sel_ref, keep_ref, got_ref, d_ref, o_ref):
@@ -280,20 +291,28 @@
         outs="h",
     )(x, x_other, keep, place, up, acc)
     received = exchange(delta)
-    rest = blocks - head
-
-    def base(own):
-        return call(
-            functools.partial(base_kernel, own, step, head, rest),
-            shape((requests, cols), F32),
-            "vvh",
-            moves(rest * 2 * step * cols, rest * flops // 2),
-            40,
-            [VMEM((min(15, rest), step, cols), BF16), dma((min(15, rest),))],
-        )(rows, acc, in_hbm(up_weight))
-
-    other = swap(base(False))
-    mine = base(True)
+    count = blocks - head
+    later = count // 2 + 1
+    half = shape((requests, cols), F32)
+    send, mine, rest = call(
+        functools.partial(base_kernel, step, head, count),
+        [half, half, VMEM((later, step, cols), BF16)],
+        "vvh",
+        moves(count * 4 * step * cols, count * flops),
+        32,
+        [
+            VMEM((count, step, cols), BF16),
+            VMEM((count - later, step, cols), BF16),
+            dma((count, 2)),
+        ],
+    )(rows, acc, in_hbm(up_weight))
+    other = swap(send)
+    mine = call(
+        functools.partial(rest_kernel, blocks - later),
+        half,
+        "vvv",
+        moves(later * 4 * step * cols, later * flops),
+    )(rows, mine, in_vmem(rest))
     return call(final_kernel, shape((requests, cols), BF16), "vvvv")(
         sel, mine, other, received.reshape(batches * OWN_MOST, cols)
     )

time: 35.2 us -> 34.9 us (level)
  transfers between devices with their start and end apart: 5 -> 5, of which waited for: 2 -> 3; matrix products, arithmetic and copies ran while one was open for 4% -> 4% of each run, Pallas kernels for 45% -> 44%
where the time goes in v7:
time: 34.9 us; the launch traced here: 34.5 us
  Pallas kernels  17.7 us (51%)
  starting transfers between devices  12.5 us (36%)
  local copies, waits for them, and re-layouts  2.87 us (8%)
  waiting for transfers between devices  1.48 us (4%)
    all_to_all x2, starting transfers between devices, exchange(): lax.all_to_all(x, 'batch', 0, 0, tiled=True, axis_index_groups=[order_of(...  12 us
    pallas_call x1, Pallas kernels, per_device(): call(functools.partial(base_kernel, step, head, count), [half, half, VMEM...  10.2 us
    pallas_call x1, Pallas kernels, per_device(): call(functools.partial(ready_kernel, batches), [shape((requests, wide), F...  3.45 us
    broadcast_in_dim x1, local copies, waits for them, and re-layouts, per_device(): sent = jnp.broadcast_to(features[None], (batches,) + features.shape)  1.44 us
    unnamed x4, local copies, waits for them, and re-layouts  1.43 us
    pallas_call x1, Pallas kernels, per_device(): call(functools.partial(delta_kernel, here), [pltpu.HBM((batches, OWN_MOST...  1.34 us
    pallas_call x1, Pallas kernels, per_device(): call(functools.partial(rest_kernel, blocks - later), half, 'vvv', moves(l...  1.19 us
    pallas_call x1, Pallas kernels, per_device(): call(final_kernel, shape((requests, cols), BF16), 'vvvv')  0.79 us
  transfers between devices with their start and end apart: 5, of which 3 were waited for; matrix products, arithmetic and copies ran while one was open for 4% of the time, Pallas kernels for 44%

profile of v7, /device:TPU:0, one launch (start us, length us, event | category | flops | bytes accessed | tf_op | source)
XLA Modules:
  0.0 34.5 jit_solution(3970248885544329079)
XLA Ops:
  0.0 0.5 %collective-permute-start = (bf16[32,32768]{1,0:T(8,128)(2,1)}, bf16[32,32768]{1,0:T(8,128)(2,1)S(1)}, u32[]{:S(2)}, u32[]{:S(2)}) collective-permute-start(bf16[32,32768]{1,0:T(8,128)(2,1)} %bitcast.8), channel_id=1, source_target_pairs={{0,1},{1,0},{2,3},{3,2},{4,5},{5,4},{6,7},{7,6},{8,9},{9,8},{10,11... | collective-permute-start | bytes 6291464 | tf_op jit(solution)/shard_map/ppermute | solution.py:237
  0.5 1.4 %broadcast_in_dim.2 = bf16[8,2,4096]{2,1,0:T(2,128)(2,1)} broadcast(bf16[2,4096]{1,0:T(2,128)(2,1)} %param.6), dimensions={1,2} | broadcast | bytes 147456 | tf_op jit(solution)/shard_map/broadcast_in_dim | solution.py:239
  1.9 7.4 %all-to-all-start = ((bf16[8,2,4096]{2,1,0:T(2,128)(2,1)}), bf16[8,2,4096]{2,1,0:T(2,128)(2,1)S(1)}, u32[]{:S(2)}, u32[]{:S(2)}) async-start(bf16[8,2,4096]{2,1,0:T(2,128)(2,1)} %broadcast_in_dim.2), calls=%async_computation | async-start | bytes 262144 | tf_op jit(solution)/shard_map/all_to_all | solution.py:40
  9.3 0.0 collective-permute-done.upo_ref
  9.3 0.0 copy-start.1
  9.3 1.3 %copy-done.1 = bf16[32,32768]{1,0:T(8,128)(2,1)} copy-done((bf16[32,32768]{1,0:T(8,128)(2,1)}, bf16[32,32768]{1,0:T(8,128)(2,1)S(1)}, u32[]{:S(2)}) %copy-start.1) | copy-done | bytes 2097176
  10.6 3.4 %shard_map.64 = (f32[16,64]{1,0:T(8,128)S(1)}, bf16[16,8]{1,0:T(8,128)(2,1)S(1)}, bf16[16,64]{1,0:T(8,128)(2,1)S(1)}, bf16[64,4096]{1,0:T(8,128)(2,1)S(1)}, bf16...) custom-call(s32[1,16]{1,0:T(1,128)} %bitcast.11, s32[1,32]{1,0:T(1,128)} %bitcast.12, bf16[64,4096]{1,0:T(8,128)(2,1)} %bitcast.10, ...), custom_call_target="tpu_custom_call" | custom-call | bytes 6291456 | tf_op jit(solution)/shard_map/pallas_call | solution.py:243
  14.0 0.5 %all-to-all-done.g_ref = bf16[8,2,4096]{2,1,0:T(2,128)(2,1)S(1)} async-done(((bf16[8,2,4096]{2,1,0:T(2,128)(2,1)}), bf16[8,2,4096]{2,1,0:T(2,128)(2,1)S(1)}, u32[]{:S(2)}, u32[]{:S(2)}) %all-to-all-start) | async-done | bytes 131104 | tf_op jit(solution)/shard_map/all_to_all | solution.py:40
  14.6 0.0 copy-start
  14.6 0.3 shard_map.65
  14.8 0.0 collective-permute-start.2
  14.9 0.4 %shard_map.66.head_ref.acc_ref = f32[16,4096]{1,0:T(8,128)S(1)} custom-call(bf16[16,4096]{1,0:T(8,128)(2,1)S(1)} %get-tuple-element.18.f_ref, bf16[256,4096]{1,0:T(8,128)(2,1)S(1)} %get-tuple-element.19.w_ref), custom_call_target="tpu_custom_call" | custom-call | flops 33554432 | bytes 2097152 | tf_op jit(solution)/shard_map/pallas_call | solution.py:280
  15.3 0.8 %collective-permute-done.2.xo_ref = f32[16,64]{1,0:T(8,128)S(1)} collective-permute-done((f32[16,64]{1,0:T(8,128)S(1)}, f32[16,64]{1,0:T(8,128)S(1)}, u32[]{:S(2)}, u32[]{:S(2)}) %collective-permute-start.2) | collective-permute-done | bytes 4128 | tf_op jit(solution)/shard_map/ppermute | solution.py:277
  16.0 0.1 copy-done
  16.2 1.3 %shard_map.69 = bf16[8,8,2048]{2,1,0:T(8,128)(2,1)} custom-call(f32[16,64]{1,0:T(8,128)S(1)} %get-tuple-element.23.x_ref, f32[16,64]{1,0:T(8,128)S(1)} %collective-permute-done.2.xo_ref, f32[16,64]{1,0:T(8,128)S(1)} %get-tuple-element.24.keep_ref, bf16[16,8]{1,0:T(8,128)(2,1)S(1)} %get-tuple-element.25.place_ref, bf16[64,16384]{1,0:T(8,128)(2,1)S(1)} %copy-done, ...), custom_call_target="tpu_custom_call" | custom-call | tf_op jit(solution)/shard_map/pallas_call | solution.py:286
  17.5 4.6 %all-to-all-start.1 = ((bf16[8,8,2048]{2,1,0:T(8,128)(2,1)}), bf16[8,8,2048]{2,1,0:T(8,128)(2,1)S(1)}, u32[]{:S(2)}, u32[]{:S(2)}) async-start(bf16[8,8,2048]{2,1,0:T(8,128)(2,1)} %shard_map.69), calls=%async_computation.1 | async-start | bytes 524288 | tf_op jit(solution)/shard_map/all_to_all | solution.py:40
  22.1 10.2 %shard_map.67 = (f32[16,2048]{1,0:T(8,128)S(1)}, f32[16,2048]{1,0:T(8,128)S(1)}, bf16[8,256,2048]{2,1,0:T(8,128)(2,1)S(1)}) custom-call(bf16[16,4096]{1,0:T(8,128)(2,1)S(1)} %get-tuple-element.18.f_ref, f32[16,4096]{1,0:T(8,128)S(1)} %shard_map.66.head_ref.acc_ref, bf16[4096,4096]{1,0:T(8,128)(2,1)} %w_ref.3), custom_call_target="tpu_custom_call" | custom-call | flops 503316480 | bytes 31457280 | tf_op jit(solution)/shard_map/pallas_call | solution.py:297
  32.3 0.1 collective-permute-start.1
  32.4 1.2 %shard_map.68.keep_ref = f32[16,2048]{1,0:T(8,128)S(1)} custom-call(bf16[16,4096]{1,0:T(8,128)(2,1)S(1)} %get-tuple-element.18.f_ref, f32[16,2048]{1,0:T(8,128)S(1)} %get-tuple-element.20.mine_ref, bf16[8,256,2048]{2,1,0:T(8,128)(2,1)S(1)} %get-tuple-element.21.w_ref), custom_call_target="tpu_custom_call" | custom-call | flops 268435456 | bytes 16777216 | tf_op jit(solution)/shard_map/pallas_call | solution.py:310
  33.6 0.1 collective-permute-done.1.got_ref
  33.7 0.0 all-to-all-done.1
  33.8 0.8 %shard_map.70 = bf16[16,2048]{1,0:T(8,128)(2,1)} custom-call(bf16[16,64]{1,0:T(8,128)(2,1)S(1)} %get-tuple-element.16.sel_ref, f32[16,2048]{1,0:T(8,128)S(1)} %shard_map.68.keep_ref, f32[16,2048]{1,0:T(8,128)S(1)} %collective-permute-done.1.got_ref, bf16[64,2048]{1,0:T(8,128)(2,1)S(1)} %bitcast.7), custom_call_target="tpu_custom_call" | custom-call | tf_op jit(solution)/shard_map/pallas_call | solution.py:316
Async XLA Ops:
  0.0 9.3 %collective-permute-start = (bf16[32,32768]{1,0:T(8,128)(2,1)}, bf16[32,32768]{1,0:T(8,128)(2,1)S(1)}, u32[]{:S(2)}, u32[]{:S(2)}) collective-permute-start(bf16[32,32768]{1,0:T(8,128)(2,1)} %bitcast.8), channel_id=1, source_target_pairs={{0,1},{1,0},{2,3},{3,2},{4,5},{5,4},{6,7},{7,6},{8,9},{9,8},{10,11... | collective-permute-start | bytes 6291464 | tf_op jit(solution)/shard_map/ppermute | solution.py:237
  1.9 12.7 %all-to-all-start = ((bf16[8,2,4096]{2,1,0:T(2,128)(2,1)}), bf16[8,2,4096]{2,1,0:T(2,128)(2,1)S(1)}, u32[]{:S(2)}, u32[]{:S(2)}) async-start(bf16[8,2,4096]{2,1,0:T(2,128)(2,1)} %broadcast_in_dim.2), calls=%async_computation | async-start | bytes 262144 | tf_op jit(solution)/shard_map/all_to_all | solution.py:40
  9.3 1.3 %copy-start.1 = (bf16[32,32768]{1,0:T(8,128)(2,1)}, bf16[32,32768]{1,0:T(8,128)(2,1)S(1)}, u32[]{:S(2)}) copy-start(bf16[32,32768]{1,0:T(8,128)(2,1)S(1)} %collective-permute-done.upo_ref) | copy-start | bytes 6291460
  14.6 1.6 %copy-start = (bf16[64,16384]{1,0:T(8,128)(2,1)S(1)}, bf16[64,16384]{1,0:T(8,128)(2,1)}, u32[]{:S(2)}) copy-start(bf16[64,16384]{1,0:T(8,128)(2,1)} %get-tuple-element.26.up_ref) | copy-start | bytes 6291460
  14.8 1.2 %collective-permute-start.2 = (f32[16,64]{1,0:T(8,128)S(1)}, f32[16,64]{1,0:T(8,128)S(1)}, u32[]{:S(2)}, u32[]{:S(2)}) collective-permute-start(f32[16,64]{1,0:T(8,128)S(1)} %get-tuple-element.23.x_ref), channel_id=1, source_target_pairs={{0,1},{1,0},{2,3},{3,2},{4,5},{5,4},{6,7},{7,6},{8,9},{9,8},{10,11... | collective-permute-start | bytes 12296 | tf_op jit(solution)/shard_map/ppermute | solution.py:277
  17.5 16.2 %all-to-all-start.1 = ((bf16[8,8,2048]{2,1,0:T(8,128)(2,1)}), bf16[8,8,2048]{2,1,0:T(8,128)(2,1)S(1)}, u32[]{:S(2)}, u32[]{:S(2)}) async-start(bf16[8,8,2048]{2,1,0:T(8,128)(2,1)} %shard_map.69), calls=%async_computation.1 | async-start | bytes 524288 | tf_op jit(solution)/shard_map/all_to_all | solution.py:40
  32.3 1.4 %collective-permute-start.1 = (f32[16,2048]{1,0:T(8,128)S(1)}, f32[16,2048]{1,0:T(8,128)S(1)}, u32[]{:S(2)}, u32[]{:S(2)}) collective-permute-start(f32[16,2048]{1,0:T(8,128)S(1)} %get-tuple-element.22), channel_id=1, source_target_pairs={{0,1},{1,0},{2,3},{3,2},{4,5},{5,4},{6,7},{7,6},{8,9},{9,8},{10,11... | collective-permute-start | bytes 393224 | tf_op jit(solution)/shard_map/ppermute | solution.py:309

commit v8 on v7

--- a/solution.py
+++ b/solution.py
@@ -28,11 +28,16 @@
 
 
 def order_of(batches):
-    return sorted(range(batches), key=lambda b: abs(2 * b - batches + 1))
+    quarter = batches // 4
+    middle = range(quarter, batches - quarter)
+    return [*reversed(middle), *reversed(range(batches - quarter, batches)), *range(quarter)]
 
 
 def place_in_order(b, batches):
-    return jnp.where(2 * b < batches, batches - 2 - 2 * b, 2 * b - batches + 1)
+    quarter = batches // 4
+    upper = batches - quarter
+    ends = jnp.where(b < quarter, upper + b, 2 * upper - 1 - b)
+    return jnp.where((b >= quarter) & (b < upper), upper - 1 - b, ends)
 
 
 def exchange(x):

time: 34.9 us -> 35.8 us (1.026)
  starting transfers between devices: 12.5 us -> 14.1 us
  waiting for transfers between devices: 1.48 us -> 0.73 us
    all_to_all x2, starting transfers between devices: 12 us -> 13.3 us  [exchange(): lax.all_to_all(x, 'batch', 0, 0, tiled=True, axis_index_groups=[order_of(...]
    all_to_all x2, waiting for transfers between devices: 0.53 us -> 0.01 us  [exchange(): lax.all_to_all(x, 'batch', 0, 0, tiled=True, axis_index_groups=[order_of(...]
  transfers between devices with their start and end apart: 5 -> 5, of which waited for: 3 -> 2; matrix products, arithmetic and copies ran while one was open for 4% -> 4% of each run, Pallas kernels for 44% -> 43%
where the time goes in v8:
time: 35.8 us; the launch traced here: 35.4 us
  Pallas kernels  17.7 us (49%)
  starting transfers between devices  14.1 us (39%)
  local copies, waits for them, and re-layouts  2.86 us (8%)
  waiting for transfers between devices  0.73 us (2%)
    all_to_all x2, starting transfers between devices, exchange(): lax.all_to_all(x, 'batch', 0, 0, tiled=True, axis_index_groups=[order_of(...  13.3 us
    pallas_call x1, Pallas kernels, per_device(): call(functools.partial(base_kernel, step, head, count), [half, half, VMEM...  10.2 us
    pallas_call x1, Pallas kernels, per_device(): call(functools.partial(ready_kernel, batches), [shape((requests, wide), F...  3.45 us
    broadcast_in_dim x1, local copies, waits for them, and re-layouts, per_device(): sent = jnp.broadcast_to(features[None], (batches,) + features.shape)  1.44 us
    unnamed x4, local copies, waits for them, and re-layouts  1.42 us
    pallas_call x1, Pallas kernels, per_device(): call(functools.partial(delta_kernel, here), [pltpu.HBM((batches, OWN_MOST...  1.34 us
    pallas_call x1, Pallas kernels, per_device(): call(functools.partial(rest_kernel, blocks - later), half, 'vvv', moves(l...  1.19 us
    pallas_call x1, Pallas kernels, per_device(): call(final_kernel, shape((requests, cols), BF16), 'vvvv')  0.79 us
  transfers between devices with their start and end apart: 5, of which 2 were waited for; matrix products, arithmetic and copies ran while one was open for 4% of the time, Pallas kernels for 43%

profile of v8, /device:TPU:0, one launch (start us, length us, event | category | flops | bytes accessed | tf_op | source)
XLA Modules:
  0.0 35.4 jit_solution(10031431489909207386)
XLA Ops:
  0.0 0.5 %collective-permute-start = (bf16[32,32768]{1,0:T(8,128)(2,1)}, bf16[32,32768]{1,0:T(8,128)(2,1)S(1)}, u32[]{:S(2)}, u32[]{:S(2)}) collective-permute-start(bf16[32,32768]{1,0:T(8,128)(2,1)} %bitcast.8), channel_id=1, source_target_pairs={{0,1},{1,0},{2,3},{3,2},{4,5},{5,4},{6,7},{7,6},{8,9},{9,8},{10,11... | collective-permute-start | bytes 6291464 | tf_op jit(solution)/shard_map/ppermute | solution.py:242
  0.5 1.4 %broadcast_in_dim.2 = bf16[8,2,4096]{2,1,0:T(2,128)(2,1)} broadcast(bf16[2,4096]{1,0:T(2,128)(2,1)} %param.6), dimensions={1,2} | broadcast | bytes 147456 | tf_op jit(solution)/shard_map/broadcast_in_dim | solution.py:244
  1.9 7.8 %all-to-all-start = ((bf16[8,2,4096]{2,1,0:T(2,128)(2,1)}), bf16[8,2,4096]{2,1,0:T(2,128)(2,1)S(1)}, u32[]{:S(2)}, u32[]{:S(2)}) async-start(bf16[8,2,4096]{2,1,0:T(2,128)(2,1)} %broadcast_in_dim.2), calls=%async_computation | async-start | bytes 262144 | tf_op jit(solution)/shard_map/all_to_all | solution.py:45
  9.7 0.0 collective-permute-done.upo_ref
  9.7 0.0 copy-start.1
  9.7 1.3 %copy-done.1 = bf16[32,32768]{1,0:T(8,128)(2,1)} copy-done((bf16[32,32768]{1,0:T(8,128)(2,1)}, bf16[32,32768]{1,0:T(8,128)(2,1)S(1)}, u32[]{:S(2)}) %copy-start.1) | copy-done | bytes 2097176
  11.0 3.4 %shard_map.64 = (f32[16,64]{1,0:T(8,128)S(1)}, bf16[16,8]{1,0:T(8,128)(2,1)S(1)}, bf16[16,64]{1,0:T(8,128)(2,1)S(1)}, bf16[64,4096]{1,0:T(8,128)(2,1)S(1)}, bf16...) custom-call(s32[1,16]{1,0:T(1,128)} %bitcast.11, s32[1,32]{1,0:T(1,128)} %bitcast.12, bf16[64,4096]{1,0:T(8,128)(2,1)} %bitcast.10, ...), custom_call_target="tpu_custom_call" | custom-call | bytes 6291456 | tf_op jit(solution)/shard_map/pallas_call | solution.py:248
  14.5 0.0 all-to-all-done.g_ref
  14.5 0.0 copy-start
  14.5 0.3 shard_map.65
  14.8 0.3 collective-permute-start.2
  15.0 0.4 %shard_map.66.head_ref.acc_ref = f32[16,4096]{1,0:T(8,128)S(1)} custom-call(bf16[16,4096]{1,0:T(8,128)(2,1)S(1)} %get-tuple-element.18.f_ref, bf16[256,4096]{1,0:T(8,128)(2,1)S(1)} %get-tuple-element.19.w_ref), custom_call_target="tpu_custom_call" | custom-call | flops 33554432 | bytes 2097152 | tf_op jit(solution)/shard_map/pallas_call | solution.py:285
  15.4 0.6 %collective-permute-done.2.xo_ref = f32[16,64]{1,0:T(8,128)S(1)} collective-permute-done((f32[16,64]{1,0:T(8,128)S(1)}, f32[16,64]{1,0:T(8,128)S(1)}, u32[]{:S(2)}, u32[]{:S(2)}) %collective-permute-start.2) | collective-permute-done | bytes 4128 | tf_op jit(solution)/shard_map/ppermute | solution.py:282
  16.0 0.1 copy-done
  16.1 1.3 %shard_map.69 = bf16[8,8,2048]{2,1,0:T(8,128)(2,1)} custom-call(f32[16,64]{1,0:T(8,128)S(1)} %get-tuple-element.23.x_ref, f32[16,64]{1,0:T(8,128)S(1)} %collective-permute-done.2.xo_ref, f32[16,64]{1,0:T(8,128)S(1)} %get-tuple-element.24.keep_ref, bf16[16,8]{1,0:T(8,128)(2,1)S(1)} %get-tuple-element.25.place_ref, bf16[64,16384]{1,0:T(8,128)(2,1)S(1)} %copy-done, ...), custom_call_target="tpu_custom_call" | custom-call | tf_op jit(solution)/shard_map/pallas_call | solution.py:291
  17.4 5.5 %all-to-all-start.1 = ((bf16[8,8,2048]{2,1,0:T(8,128)(2,1)}), bf16[8,8,2048]{2,1,0:T(8,128)(2,1)S(1)}, u32[]{:S(2)}, u32[]{:S(2)}) async-start(bf16[8,8,2048]{2,1,0:T(8,128)(2,1)} %shard_map.69), calls=%async_computation.1 | async-start | bytes 524288 | tf_op jit(solution)/shard_map/all_to_all | solution.py:45
  22.9 10.2 %shard_map.67 = (f32[16,2048]{1,0:T(8,128)S(1)}, f32[16,2048]{1,0:T(8,128)S(1)}, bf16[8,256,2048]{2,1,0:T(8,128)(2,1)S(1)}) custom-call(bf16[16,4096]{1,0:T(8,128)(2,1)S(1)} %get-tuple-element.18.f_ref, f32[16,4096]{1,0:T(8,128)S(1)} %shard_map.66.head_ref.acc_ref, bf16[4096,4096]{1,0:T(8,128)(2,1)} %w_ref.3), custom_call_target="tpu_custom_call" | custom-call | flops 503316480 | bytes 31457280 | tf_op jit(solution)/shard_map/pallas_call | solution.py:302
  33.2 0.1 collective-permute-start.1
  33.2 1.2 %shard_map.68.keep_ref = f32[16,2048]{1,0:T(8,128)S(1)} custom-call(bf16[16,4096]{1,0:T(8,128)(2,1)S(1)} %get-tuple-element.18.f_ref, f32[16,2048]{1,0:T(8,128)S(1)} %get-tuple-element.20.mine_ref, bf16[8,256,2048]{2,1,0:T(8,128)(2,1)S(1)} %get-tuple-element.21.w_ref), custom_call_target="tpu_custom_call" | custom-call | flops 268435456 | bytes 16777216 | tf_op jit(solution)/shard_map/pallas_call | solution.py:315
  34.4 0.1 collective-permute-done.1.got_ref
  34.6 0.0 all-to-all-done.1
  34.6 0.8 %shard_map.70 = bf16[16,2048]{1,0:T(8,128)(2,1)} custom-call(bf16[16,64]{1,0:T(8,128)(2,1)S(1)} %get-tuple-element.16.sel_ref, f32[16,2048]{1,0:T(8,128)S(1)} %shard_map.68.keep_ref, f32[16,2048]{1,0:T(8,128)S(1)} %collective-permute-done.1.got_ref, bf16[64,2048]{1,0:T(8,128)(2,1)S(1)} %bitcast.7), custom_call_target="tpu_custom_call" | custom-call | tf_op jit(solution)/shard_map/pallas_call | solution.py:321
Async XLA Ops:
  0.0 9.7 %collective-permute-start = (bf16[32,32768]{1,0:T(8,128)(2,1)}, bf16[32,32768]{1,0:T(8,128)(2,1)S(1)}, u32[]{:S(2)}, u32[]{:S(2)}) collective-permute-start(bf16[32,32768]{1,0:T(8,128)(2,1)} %bitcast.8), channel_id=1, source_target_pairs={{0,1},{1,0},{2,3},{3,2},{4,5},{5,4},{6,7},{7,6},{8,9},{9,8},{10,11... | collective-permute-start | bytes 6291464 | tf_op jit(solution)/shard_map/ppermute | solution.py:242
  1.9 12.6 %all-to-all-start = ((bf16[8,2,4096]{2,1,0:T(2,128)(2,1)}), bf16[8,2,4096]{2,1,0:T(2,128)(2,1)S(1)}, u32[]{:S(2)}, u32[]{:S(2)}) async-start(bf16[8,2,4096]{2,1,0:T(2,128)(2,1)} %broadcast_in_dim.2), calls=%async_computation | async-start | bytes 262144 | tf_op jit(solution)/shard_map/all_to_all | solution.py:45
  9.7 1.3 %copy-start.1 = (bf16[32,32768]{1,0:T(8,128)(2,1)}, bf16[32,32768]{1,0:T(8,128)(2,1)S(1)}, u32[]{:S(2)}) copy-start(bf16[32,32768]{1,0:T(8,128)(2,1)S(1)} %collective-permute-done.upo_ref) | copy-start | bytes 6291460
  14.5 1.6 %copy-start = (bf16[64,16384]{1,0:T(8,128)(2,1)S(1)}, bf16[64,16384]{1,0:T(8,128)(2,1)}, u32[]{:S(2)}) copy-start(bf16[64,16384]{1,0:T(8,128)(2,1)} %get-tuple-element.26.up_ref) | copy-start | bytes 6291460
  14.8 1.2 %collective-permute-start.2 = (f32[16,64]{1,0:T(8,128)S(1)}, f32[16,64]{1,0:T(8,128)S(1)}, u32[]{:S(2)}, u32[]{:S(2)}) collective-permute-start(f32[16,64]{1,0:T(8,128)S(1)} %get-tuple-element.23.x_ref), channel_id=1, source_target_pairs={{0,1},{1,0},{2,3},{3,2},{4,5},{5,4},{6,7},{7,6},{8,9},{9,8},{10,11... | collective-permute-start | bytes 12296 | tf_op jit(solution)/shard_map/ppermute | solution.py:282
  17.4 17.1 %all-to-all-start.1 = ((bf16[8,8,2048]{2,1,0:T(8,128)(2,1)}), bf16[8,8,2048]{2,1,0:T(8,128)(2,1)S(1)}, u32[]{:S(2)}, u32[]{:S(2)}) async-start(bf16[8,8,2048]{2,1,0:T(8,128)(2,1)} %shard_map.69), calls=%async_computation.1 | async-start | bytes 524288 | tf_op jit(solution)/shard_map/all_to_all | solution.py:45
  33.2 1.4 %collective-permute-start.1 = (f32[16,2048]{1,0:T(8,128)S(1)}, f32[16,2048]{1,0:T(8,128)S(1)}, u32[]{:S(2)}, u32[]{:S(2)}) collective-permute-start(f32[16,2048]{1,0:T(8,128)S(1)} %get-tuple-element.22), channel_id=1, source_target_pairs={{0,1},{1,0},{2,3},{3,2},{4,5},{5,4},{6,7},{7,6},{8,9},{9,8},{10,11... | collective-permute-start | bytes 393224 | tf_op jit(solution)/shard_map/ppermute | solution.py:314

commit v9 on v7

--- a/solution.py
+++ b/solution.py
@@ -28,18 +28,9 @@
 
 
 def order_of(batches):
-    return sorted(range(batches), key=lambda b: abs(2 * b - batches + 1))
-
-
-def place_in_order(b, batches):
-    return jnp.where(2 * b < batches, batches - 2 - 2 * b, 2 * b - batches + 1)
-
-
-def exchange(x):
-    batches = lax.axis_size("batch")
-    return lax.all_to_all(
-        x, "batch", 0, 0, tiled=True, axis_index_groups=[order_of(batches)]
-    )
+    first, quarter = batches // 2 - 1, batches // 4
+    middle = [b for b in range(quarter, batches - quarter) if b != first]
+    return [first, *reversed(middle), *reversed(range(batches - quarter, batches)), *range(quarter)]
 
 
 def ready_kernel(
@@ -55,8 +46,8 @@
         pltpu.make_async_copy(w_ref.at[: wv_ref.shape[0]], wv_ref, sems.at[2 * batches + 1]),
     ]
     copies = []
-    for d, b in enumerate(order_of(batches)):
-        span = pl.ds(pl.multiple_of((2 * b + core) * cols, LANES), cols)
+    for d in range(batches):
+        span = pl.ds(pl.multiple_of((2 * d + core) * cols, LANES), cols)
         for k, ref in enumerate((up_ref, upo_ref)):
             copies.append(
                 pltpu.make_async_copy(
@@ -99,7 +90,7 @@
     mine = (owner == me) & (iota((requests, OWN_MOST), 1) == rank)
     place_ref[...] = jnp.where(mine, 1.0, 0.0).astype(BF16)
     sel_ref[...] = jnp.where(
-        iota(sel_ref.shape, 1) == place_in_order(owner, batches) * OWN_MOST + rank, 1.0, 0.0
+        iota(sel_ref.shape, 1) == owner * OWN_MOST + rank, 1.0, 0.0
     ).astype(BF16)
     for c in copies:
         c.wait()
@@ -237,7 +228,9 @@
     up_other = swap(up)
     down = jnp.transpose(down, (0, 2, 1)).reshape(wide, width)
     sent = jnp.broadcast_to(features[None], (batches,) + features.shape)
-    gathered = exchange(sent)
+    gathered = lax.all_to_all(
+        sent, "batch", 0, 0, tiled=True, axis_index_groups=[order_of(batches)]
+    )
     step = 256
     head = 1
     keep, place, sel, down, up, first = call(
@@ -290,7 +283,7 @@
         scratch=[VMEM((batches, OWN_MOST, cols), BF16), dma((batches,))],
         outs="h",
     )(x, x_other, keep, place, up, acc)
-    received = exchange(delta)
+    received = lax.all_to_all(delta, "batch", 0, 0, tiled=True)
     count = blocks - head
     later = count // 2 + 1
     half = shape((requests, cols), F32)

time: 34.9 us -> 33.8 us (0.968)
  starting transfers between devices: 12.5 us -> 11.4 us
    all_to_all x2, starting transfers between devices: 12 us -> 10.8 us  [the longest x1 7.36 us: per_device(): lax.all_to_all(sent, 'batch', 0, 0, tiled=True, axis_index_groups=[order_...]
  transfers between devices with their start and end apart: 5 -> 5, of which waited for: 3 -> 3; matrix products, arithmetic and copies ran while one was open for 4% -> 4% of each run, Pallas kernels for 44% -> 46%
where the time goes in v9:
time: 33.8 us; the launch traced here: 33.4 us
  Pallas kernels  17.7 us (52%)
  starting transfers between devices  11.4 us (34%)
  local copies, waits for them, and re-layouts  2.86 us (8%)
  waiting for transfers between devices  1.48 us (4%)
    pallas_call x1, Pallas kernels, per_device(): call(functools.partial(base_kernel, step, head, count), [half, half, VMEM...  10.2 us
    all_to_all x1, starting transfers between devices, per_device(): lax.all_to_all(sent, 'batch', 0, 0, tiled=True, axis_index_groups=[order_...  7.36 us
    all_to_all x1, starting transfers between devices, per_device(): received = lax.all_to_all(delta, 'batch', 0, 0, tiled=True)  3.47 us
    pallas_call x1, Pallas kernels, per_device(): call(functools.partial(ready_kernel, batches), [shape((requests, wide), F...  3.45 us
    broadcast_in_dim x1, local copies, waits for them, and re-layouts, per_device(): sent = jnp.broadcast_to(features[None], (batches,) + features.shape)  1.44 us
    unnamed x4, local copies, waits for them, and re-layouts  1.43 us
    pallas_call x1, Pallas kernels, per_device(): call(functools.partial(delta_kernel, here), [pltpu.HBM((batches, OWN_MOST...  1.34 us
    pallas_call x1, Pallas kernels, per_device(): call(functools.partial(rest_kernel, blocks - later), half, 'vvv', moves(l...  1.18 us
  transfers between devices with their start and end apart: 5, of which 3 were waited for; matrix products, arithmetic and copies ran while one was open for 4% of the time, Pallas kernels for 46%

profile of v9, /device:TPU:0, one launch (start us, length us, event | category | flops | bytes accessed | tf_op | source)
XLA Modules:
  0.0 33.4 jit_solution(14914978581065806934)
XLA Ops:
  0.0 0.5 %collective-permute-start = (bf16[32,32768]{1,0:T(8,128)(2,1)}, bf16[32,32768]{1,0:T(8,128)(2,1)S(1)}, u32[]{:S(2)}, u32[]{:S(2)}) collective-permute-start(bf16[32,32768]{1,0:T(8,128)(2,1)} %bitcast.8), channel_id=1, source_target_pairs={{0,1},{1,0},{2,3},{3,2},{4,5},{5,4},{6,7},{7,6},{8,9},{9,8},{10,11... | collective-permute-start | bytes 6291464 | tf_op jit(solution)/shard_map/ppermute | solution.py:228
  0.5 1.4 %broadcast_in_dim.2 = bf16[8,2,4096]{2,1,0:T(2,128)(2,1)} broadcast(bf16[2,4096]{1,0:T(2,128)(2,1)} %param.6), dimensions={1,2} | broadcast | bytes 147456 | tf_op jit(solution)/shard_map/broadcast_in_dim | solution.py:230
  1.9 7.4 %all-to-all-start = ((bf16[8,2,4096]{2,1,0:T(2,128)(2,1)}), bf16[8,2,4096]{2,1,0:T(2,128)(2,1)S(1)}, u32[]{:S(2)}, u32[]{:S(2)}) async-start(bf16[8,2,4096]{2,1,0:T(2,128)(2,1)} %broadcast_in_dim.2), calls=%async_computation | async-start | bytes 262144 | tf_op jit(solution)/shard_map/all_to_all | solution.py:231
  9.3 0.0 collective-permute-done.upo_ref
  9.3 0.0 copy-start.1
  9.3 1.3 %copy-done.1 = bf16[32,32768]{1,0:T(8,128)(2,1)} copy-done((bf16[32,32768]{1,0:T(8,128)(2,1)}, bf16[32,32768]{1,0:T(8,128)(2,1)S(1)}, u32[]{:S(2)}) %copy-start.1) | copy-done | bytes 2097176
  10.6 3.4 %shard_map.64 = (f32[16,64]{1,0:T(8,128)S(1)}, bf16[16,8]{1,0:T(8,128)(2,1)S(1)}, bf16[16,64]{1,0:T(8,128)(2,1)S(1)}, bf16[64,4096]{1,0:T(8,128)(2,1)S(1)}, bf16...) custom-call(s32[1,16]{1,0:T(1,128)} %bitcast.11, s32[1,32]{1,0:T(1,128)} %bitcast.12, bf16[64,4096]{1,0:T(8,128)(2,1)} %bitcast.10, ...), custom_call_target="tpu_custom_call" | custom-call | bytes 6291456 | tf_op jit(solution)/shard_map/pallas_call | solution.py:236
  14.0 0.5 %all-to-all-done.g_ref = bf16[8,2,4096]{2,1,0:T(2,128)(2,1)S(1)} async-done(((bf16[8,2,4096]{2,1,0:T(2,128)(2,1)}), bf16[8,2,4096]{2,1,0:T(2,128)(2,1)S(1)}, u32[]{:S(2)}, u32[]{:S(2)}) %all-to-all-start) | async-done | bytes 131104 | tf_op jit(solution)/shard_map/all_to_all | solution.py:231
  14.6 0.0 copy-start
  14.6 0.3 shard_map.65
  14.9 0.0 collective-permute-start.2
  14.9 0.4 %shard_map.66.head_ref.acc_ref = f32[16,4096]{1,0:T(8,128)S(1)} custom-call(bf16[16,4096]{1,0:T(8,128)(2,1)S(1)} %get-tuple-element.18.f_ref, bf16[256,4096]{1,0:T(8,128)(2,1)S(1)} %get-tuple-element.19.w_ref), custom_call_target="tpu_custom_call" | custom-call | flops 33554432 | bytes 2097152 | tf_op jit(solution)/shard_map/pallas_call | solution.py:273
  15.3 0.8 %collective-permute-done.2.xo_ref = f32[16,64]{1,0:T(8,128)S(1)} collective-permute-done((f32[16,64]{1,0:T(8,128)S(1)}, f32[16,64]{1,0:T(8,128)S(1)}, u32[]{:S(2)}, u32[]{:S(2)}) %collective-permute-start.2) | collective-permute-done | bytes 4128 | tf_op jit(solution)/shard_map/ppermute | solution.py:270
  16.1 0.1 copy-done
  16.2 1.3 %shard_map.69 = bf16[8,8,2048]{2,1,0:T(8,128)(2,1)} custom-call(f32[16,64]{1,0:T(8,128)S(1)} %get-tuple-element.23.x_ref, f32[16,64]{1,0:T(8,128)S(1)} %collective-permute-done.2.xo_ref, f32[16,64]{1,0:T(8,128)S(1)} %get-tuple-element.24.keep_ref, bf16[16,8]{1,0:T(8,128)(2,1)S(1)} %get-tuple-element.25.place_ref, bf16[64,16384]{1,0:T(8,128)(2,1)S(1)} %copy-done, ...), custom_call_target="tpu_custom_call" | custom-call | tf_op jit(solution)/shard_map/pallas_call | solution.py:279
  17.5 3.5 %all-to-all-start.1 = ((bf16[8,8,2048]{2,1,0:T(8,128)(2,1)}), bf16[8,8,2048]{2,1,0:T(8,128)(2,1)S(1)}, u32[]{:S(2)}, u32[]{:S(2)}) async-start(bf16[8,8,2048]{2,1,0:T(8,128)(2,1)} %shard_map.69), calls=%async_computation.1 | async-start | bytes 524288 | tf_op jit(solution)/shard_map/all_to_all | solution.py:286
  21.0 10.2 %shard_map.67 = (f32[16,2048]{1,0:T(8,128)S(1)}, f32[16,2048]{1,0:T(8,128)S(1)}, bf16[8,256,2048]{2,1,0:T(8,128)(2,1)S(1)}) custom-call(bf16[16,4096]{1,0:T(8,128)(2,1)S(1)} %get-tuple-element.18.f_ref, f32[16,4096]{1,0:T(8,128)S(1)} %shard_map.66.head_ref.acc_ref, bf16[4096,4096]{1,0:T(8,128)(2,1)} %w_ref.3), custom_call_target="tpu_custom_call" | custom-call | flops 503316480 | bytes 31457280 | tf_op jit(solution)/shard_map/pallas_call | solution.py:290
  31.2 0.1 collective-permute-start.1
  31.3 1.2 %shard_map.68.keep_ref = f32[16,2048]{1,0:T(8,128)S(1)} custom-call(bf16[16,4096]{1,0:T(8,128)(2,1)S(1)} %get-tuple-element.18.f_ref, f32[16,2048]{1,0:T(8,128)S(1)} %get-tuple-element.20.mine_ref, bf16[8,256,2048]{2,1,0:T(8,128)(2,1)S(1)} %get-tuple-element.21.w_ref), custom_call_target="tpu_custom_call" | custom-call | flops 268435456 | bytes 16777216 | tf_op jit(solution)/shard_map/pallas_call | solution.py:303
  32.5 0.1 collective-permute-done.1.got_ref
  32.6 0.0 all-to-all-done.1
  32.6 0.8 %shard_map.70 = bf16[16,2048]{1,0:T(8,128)(2,1)} custom-call(bf16[16,64]{1,0:T(8,128)(2,1)S(1)} %get-tuple-element.16.sel_ref, f32[16,2048]{1,0:T(8,128)S(1)} %shard_map.68.keep_ref, f32[16,2048]{1,0:T(8,128)S(1)} %collective-permute-done.1.got_ref, bf16[64,2048]{1,0:T(8,128)(2,1)S(1)} %bitcast.7), custom_call_target="tpu_custom_call" | custom-call | tf_op jit(solution)/shard_map/pallas_call | solution.py:309
Async XLA Ops:
  0.0 9.3 %collective-permute-start = (bf16[32,32768]{1,0:T(8,128)(2,1)}, bf16[32,32768]{1,0:T(8,128)(2,1)S(1)}, u32[]{:S(2)}, u32[]{:S(2)}) collective-permute-start(bf16[32,32768]{1,0:T(8,128)(2,1)} %bitcast.8), channel_id=1, source_target_pairs={{0,1},{1,0},{2,3},{3,2},{4,5},{5,4},{6,7},{7,6},{8,9},{9,8},{10,11... | collective-permute-start | bytes 6291464 | tf_op jit(solution)/shard_map/ppermute | solution.py:228
  1.9 12.7 %all-to-all-start = ((bf16[8,2,4096]{2,1,0:T(2,128)(2,1)}), bf16[8,2,4096]{2,1,0:T(2,128)(2,1)S(1)}, u32[]{:S(2)}, u32[]{:S(2)}) async-start(bf16[8,2,4096]{2,1,0:T(2,128)(2,1)} %broadcast_in_dim.2), calls=%async_computation | async-start | bytes 262144 | tf_op jit(solution)/shard_map/all_to_all | solution.py:231
  9.3 1.3 %copy-start.1 = (bf16[32,32768]{1,0:T(8,128)(2,1)}, bf16[32,32768]{1,0:T(8,128)(2,1)S(1)}, u32[]{:S(2)}) copy-start(bf16[32,32768]{1,0:T(8,128)(2,1)S(1)} %collective-permute-done.upo_ref) | copy-start | bytes 6291460
  14.6 1.6 %copy-start = (bf16[64,16384]{1,0:T(8,128)(2,1)S(1)}, bf16[64,16384]{1,0:T(8,128)(2,1)}, u32[]{:S(2)}) copy-start(bf16[64,16384]{1,0:T(8,128)(2,1)} %get-tuple-element.26.up_ref) | copy-start | bytes 6291460
  14.9 1.2 %collective-permute-start.2 = (f32[16,64]{1,0:T(8,128)S(1)}, f32[16,64]{1,0:T(8,128)S(1)}, u32[]{:S(2)}, u32[]{:S(2)}) collective-permute-start(f32[16,64]{1,0:T(8,128)S(1)} %get-tuple-element.23.x_ref), channel_id=1, source_target_pairs={{0,1},{1,0},{2,3},{3,2},{4,5},{5,4},{6,7},{7,6},{8,9},{9,8},{10,11... | collective-permute-start | bytes 12296 | tf_op jit(solution)/shard_map/ppermute | solution.py:270
  17.5 15.1 %all-to-all-start.1 = ((bf16[8,8,2048]{2,1,0:T(8,128)(2,1)}), bf16[8,8,2048]{2,1,0:T(8,128)(2,1)S(1)}, u32[]{:S(2)}, u32[]{:S(2)}) async-start(bf16[8,8,2048]{2,1,0:T(8,128)(2,1)} %shard_map.69), calls=%async_computation.1 | async-start | bytes 524288 | tf_op jit(solution)/shard_map/all_to_all | solution.py:286
  31.2 1.4 %collective-permute-start.1 = (f32[16,2048]{1,0:T(8,128)S(1)}, f32[16,2048]{1,0:T(8,128)S(1)}, u32[]{:S(2)}, u32[]{:S(2)}) collective-permute-start(f32[16,2048]{1,0:T(8,128)S(1)} %get-tuple-element.22), channel_id=1, source_target_pairs={{0,1},{1,0},{2,3},{3,2},{4,5},{5,4},{6,7},{7,6},{8,9},{9,8},{10,11... | collective-permute-start | bytes 393224 | tf_op jit(solution)/shard_map/ppermute | solution.py:302

commit v10 on v9

--- a/solution.py
+++ b/solution.py
@@ -35,14 +35,14 @@
 
 def ready_kernel(
     batches, ra_in, sr_in, down_ref, up_ref, upo_ref, w_ref,
-    keep_ref, place_ref, sel_ref, downv_ref, upv_ref, wv_ref, ra_ref, sr_ref, stage, sems, index_sems
+    keep_ref, place_ref, sel_ref, downv_ref, upv_ref, wv_ref, ra_ref, sr_ref, stage, down_buf, sems, index_sems
 ):
     me = lax.axis_index("batch")
     core = lax.axis_index("tensor")
     rows, hidden = up_ref.shape
     cols = hidden // (2 * batches)
     last = [
-        pltpu.make_async_copy(down_ref, downv_ref, sems.at[0]),
+        pltpu.make_async_copy(down_ref, down_buf, sems.at[0]),
         pltpu.make_async_copy(w_ref.at[: wv_ref.shape[0]], wv_ref, sems.at[2 * batches + 1]),
     ]
     copies = []
@@ -52,7 +52,10 @@
             copies.append(
                 pltpu.make_async_copy(
                     ref.at[:, span],
-                    stage.at[k * rows : (k + 1) * rows, d * cols : (d + 1) * cols],
+                    stage.at[
+                        pl.ds(pl.multiple_of((core if k == 0 else 1 - core) * rows, 16), rows),
+                        d * cols : (d + 1) * cols,
+                    ],
                     sems.at[1 + 2 * d + k],
                 )
             )
@@ -83,10 +86,11 @@
     rank = jnp.sum(counts * marks, axis=1, keepdims=True).astype(jnp.int32)
     owner = jnp.sum(jnp.where(hit, iota((requests, batches), 1), 0), axis=1, keepdims=True)
     wide = keep_ref.shape[1]
-    width = wide // here
-    low = (slot - me * here) * width
+    half = wide // here // 2
     column = iota((requests, wide), 1)
-    keep_ref[...] = jnp.where((column >= low) & (column < low + width), 1.0, 0.0)
+    within = jnp.where(column < wide // 2, column, column - wide // 2)
+    low = (slot - me * here) * half
+    keep_ref[...] = jnp.where((within >= low) & (within < low + half), 1.0, 0.0)
     mine = (owner == me) & (iota((requests, OWN_MOST), 1) == rank)
     place_ref[...] = jnp.where(mine, 1.0, 0.0).astype(BF16)
     sel_ref[...] = jnp.where(
@@ -96,7 +100,17 @@
         c.wait()
     back = pltpu.make_async_copy(stage, upv_ref, sems.at[2 * batches + 2])
     back.start()
-    for c in last + [back]:
+    last[0].wait()
+    row, column = iota((wide, wide), 0), iota((wide, wide), 1)
+    source = jnp.zeros_like(row)
+    for h in range(here):
+        for k in range(2):
+            start = (k * here + h) * half
+            inside = (row >= start) & (row < start + half)
+            source = jnp.where(inside, (2 * h + k) * half + row - start, source)
+    pick = jnp.where(column == source, 1.0, 0.0).astype(BF16)
+    downv_ref[...] = jnp.dot(pick, down_buf[...], preferred_element_type=F32).astype(BF16)
+    for c in [last[1], back]:
         c.wait()
 
 
@@ -110,27 +124,13 @@
     )
 
 
-def delta_kernel(here, x_ref, xo_ref, keep_ref, place_ref, up_ref, acc_ref, out_ref, d_ref, sems):
+def delta_kernel(x_ref, xo_ref, keep_ref, place_ref, up_ref, acc_ref, out_ref, d_ref, sems):
     batches, _, cols = d_ref.shape
-    core = lax.axis_index("tensor")
-    wide = x_ref.shape[1]
-    rank = wide // here
-    half = rank // 2
     shrunk = (x_ref[...] + xo_ref[...]).astype(BF16)
     kept = (shrunk.astype(F32) * keep_ref[...]).astype(BF16)
     rows = lax.dot_general(
         place_ref[...], kept, (((0,), (0,)), ((), ())), preferred_element_type=F32
     ).astype(BF16)
-    i = lax.broadcasted_iota(jnp.int32, (wide, wide), 0)
-    j = lax.broadcasted_iota(jnp.int32, (wide, wide), 1)
-    side = jnp.where(j < wide // 2, core, 1 - core)
-    k = jnp.where(j < wide // 2, j, j - wide // 2)
-    source = jnp.zeros_like(k)
-    for h in range(here):
-        within = (k >= h * half) & (k < (h + 1) * half)
-        source = jnp.where(within, h * rank + k - h * half, source)
-    pick = jnp.where(i == source + side * half, 1.0, 0.0).astype(BF16)
-    rows = jnp.dot(rows, pick, preferred_element_type=F32).astype(BF16)
     copies = []
     for d in range(batches):
         d_ref[d] = jnp.dot(
@@ -249,6 +249,7 @@
             VMEM((1, requests), jnp.int32),
             VMEM((1, storage_row.shape[0]), jnp.int32),
             VMEM((wide, hidden // 2), BF16),
+            VMEM(down.shape, BF16),
             dma((3 + 2 * batches,)),
             dma((2,)),
         ],
@@ -277,7 +278,7 @@
         moves(head * 4 * step * cols, head * flops),
     )(rows, in_vmem(first))
     (delta,) = call(
-        functools.partial(delta_kernel, here),
+        delta_kernel,
         [pltpu.HBM((batches, OWN_MOST, cols), BF16)],
         "vvvvva",
         scratch=[VMEM((batches, OWN_MOST, cols), BF16), dma((batches,))],

time: 33.8 us -> 33.7 us (level)
  no operation moved by 1% of the time
where the time goes in v10:
time: 33.7 us; the launch traced here: 33.3 us
  Pallas kernels  17.6 us (52%)
  starting transfers between devices  11.4 us (34%)
  local copies, waits for them, and re-layouts  2.86 us (8%)
  waiting for transfers between devices  1.46 us (4%)
    pallas_call x1, Pallas kernels, per_device(): call(functools.partial(base_kernel, step, head, count), [half, half, VMEM...  10.2 us
    all_to_all x1, starting transfers between devices, per_device(): lax.all_to_all(sent, 'batch', 0, 0, tiled=True, axis_index_groups=[order_...  7.36 us
    all_to_all x1, starting transfers between devices, per_device(): received = lax.all_to_all(delta, 'batch', 0, 0, tiled=True)  3.47 us
    pallas_call x1, Pallas kernels, per_device(): call(functools.partial(ready_kernel, batches), [shape((requests, wide), F...  3.46 us
    broadcast_in_dim x1, local copies, waits for them, and re-layouts, per_device(): sent = jnp.broadcast_to(features[None], (batches,) + features.shape)  1.44 us
    unnamed x4, local copies, waits for them, and re-layouts  1.43 us
    pallas_call x1, Pallas kernels, per_device(): call(delta_kernel, [pltpu.HBM((batches, OWN_MOST, cols), BF16)], 'vvvvva'...  1.23 us
    pallas_call x1, Pallas kernels, per_device(): call(functools.partial(rest_kernel, blocks - later), half, 'vvv', moves(l...  1.18 us
  transfers between devices with their start and end apart: 5, of which 3 were waited for; matrix products, arithmetic and copies ran while one was open for 4% of the time, Pallas kernels for 46%

profile of v10, /device:TPU:0, one launch (start us, length us, event | category | flops | bytes accessed | tf_op | source)
XLA Modules:
  0.0 33.3 jit_solution(7877469926597282927)
XLA Ops:
  0.0 0.5 %collective-permute-start = (bf16[32,32768]{1,0:T(8,128)(2,1)}, bf16[32,32768]{1,0:T(8,128)(2,1)S(1)}, u32[]{:S(2)}, u32[]{:S(2)}) collective-permute-start(bf16[32,32768]{1,0:T(8,128)(2,1)} %bitcast.8), channel_id=1, source_target_pairs={{0,1},{1,0},{2,3},{3,2},{4,5},{5,4},{6,7},{7,6},{8,9},{9,8},{10,11... | collective-permute-start | bytes 6291464 | tf_op jit(solution)/shard_map/ppermute | solution.py:228
  0.5 1.4 %broadcast_in_dim.2 = bf16[8,2,4096]{2,1,0:T(2,128)(2,1)} broadcast(bf16[2,4096]{1,0:T(2,128)(2,1)} %param.6), dimensions={1,2} | broadcast | bytes 147456 | tf_op jit(solution)/shard_map/broadcast_in_dim | solution.py:230
  1.9 7.4 %all-to-all-start = ((bf16[8,2,4096]{2,1,0:T(2,128)(2,1)}), bf16[8,2,4096]{2,1,0:T(2,128)(2,1)S(1)}, u32[]{:S(2)}, u32[]{:S(2)}) async-start(bf16[8,2,4096]{2,1,0:T(2,128)(2,1)} %broadcast_in_dim.2), calls=%async_computation | async-start | bytes 262144 | tf_op jit(solution)/shard_map/all_to_all | solution.py:231
  9.3 0.0 collective-permute-done.upo_ref
  9.3 0.0 copy-start.1
  9.3 1.3 %copy-done.1 = bf16[32,32768]{1,0:T(8,128)(2,1)} copy-done((bf16[32,32768]{1,0:T(8,128)(2,1)}, bf16[32,32768]{1,0:T(8,128)(2,1)S(1)}, u32[]{:S(2)}) %copy-start.1) | copy-done | bytes 2097176
  10.6 3.5 %shard_map.64 = (f32[16,64]{1,0:T(8,128)S(1)}, bf16[16,8]{1,0:T(8,128)(2,1)S(1)}, bf16[16,64]{1,0:T(8,128)(2,1)S(1)}, bf16[64,4096]{1,0:T(8,128)(2,1)S(1)}, bf16...) custom-call(s32[1,16]{1,0:T(1,128)} %bitcast.11, s32[1,32]{1,0:T(1,128)} %bitcast.12, bf16[64,4096]{1,0:T(8,128)(2,1)} %bitcast.10, ...), custom_call_target="tpu_custom_call" | custom-call | bytes 6291456 | tf_op jit(solution)/shard_map/pallas_call | solution.py:236
  14.0 0.5 %all-to-all-done.g_ref = bf16[8,2,4096]{2,1,0:T(2,128)(2,1)S(1)} async-done(((bf16[8,2,4096]{2,1,0:T(2,128)(2,1)}), bf16[8,2,4096]{2,1,0:T(2,128)(2,1)S(1)}, u32[]{:S(2)}, u32[]{:S(2)}) %all-to-all-start) | async-done | bytes 131104 | tf_op jit(solution)/shard_map/all_to_all | solution.py:231
  14.6 0.0 copy-start
  14.6 0.3 shard_map.65
  14.9 0.0 collective-permute-start.2
  14.9 0.4 %shard_map.66.head_ref.acc_ref = f32[16,4096]{1,0:T(8,128)S(1)} custom-call(bf16[16,4096]{1,0:T(8,128)(2,1)S(1)} %get-tuple-element.18.f_ref, bf16[256,4096]{1,0:T(8,128)(2,1)S(1)} %get-tuple-element.19.w_ref), custom_call_target="tpu_custom_call" | custom-call | flops 33554432 | bytes 2097152 | tf_op jit(solution)/shard_map/pallas_call | solution.py:274
  15.3 0.8 %collective-permute-done.2.xo_ref = f32[16,64]{1,0:T(8,128)S(1)} collective-permute-done((f32[16,64]{1,0:T(8,128)S(1)}, f32[16,64]{1,0:T(8,128)S(1)}, u32[]{:S(2)}, u32[]{:S(2)}) %collective-permute-start.2) | collective-permute-done | bytes 4128 | tf_op jit(solution)/shard_map/ppermute | solution.py:271
  16.1 0.1 copy-done
  16.2 1.2 %shard_map.69 = bf16[8,8,2048]{2,1,0:T(8,128)(2,1)} custom-call(f32[16,64]{1,0:T(8,128)S(1)} %get-tuple-element.23.x_ref, f32[16,64]{1,0:T(8,128)S(1)} %collective-permute-done.2.xo_ref, f32[16,64]{1,0:T(8,128)S(1)} %get-tuple-element.24.keep_ref, bf16[16,8]{1,0:T(8,128)(2,1)S(1)} %get-tuple-element.25.place_ref, bf16[64,16384]{1,0:T(8,128)(2,1)S(1)} %copy-done, ...), custom_call_target="tpu_custom_call" | custom-call | tf_op jit(solution)/shard_map/pallas_call | solution.py:280
  17.4 3.5 %all-to-all-start.1 = ((bf16[8,8,2048]{2,1,0:T(8,128)(2,1)}), bf16[8,8,2048]{2,1,0:T(8,128)(2,1)S(1)}, u32[]{:S(2)}, u32[]{:S(2)}) async-start(bf16[8,8,2048]{2,1,0:T(8,128)(2,1)} %shard_map.69), calls=%async_computation.1 | async-start | bytes 524288 | tf_op jit(solution)/shard_map/all_to_all | solution.py:287
  20.9 10.2 %shard_map.67 = (f32[16,2048]{1,0:T(8,128)S(1)}, f32[16,2048]{1,0:T(8,128)S(1)}, bf16[8,256,2048]{2,1,0:T(8,128)(2,1)S(1)}) custom-call(bf16[16,4096]{1,0:T(8,128)(2,1)S(1)} %get-tuple-element.18.f_ref, f32[16,4096]{1,0:T(8,128)S(1)} %shard_map.66.head_ref.acc_ref, bf16[4096,4096]{1,0:T(8,128)(2,1)} %w_ref.3), custom_call_target="tpu_custom_call" | custom-call | flops 503316480 | bytes 31457280 | tf_op jit(solution)/shard_map/pallas_call | solution.py:291
  31.1 0.1 collective-permute-start.1
  31.2 1.2 %shard_map.68.keep_ref = f32[16,2048]{1,0:T(8,128)S(1)} custom-call(bf16[16,4096]{1,0:T(8,128)(2,1)S(1)} %get-tuple-element.18.f_ref, f32[16,2048]{1,0:T(8,128)S(1)} %get-tuple-element.20.mine_ref, bf16[8,256,2048]{2,1,0:T(8,128)(2,1)S(1)} %get-tuple-element.21.w_ref), custom_call_target="tpu_custom_call" | custom-call | flops 268435456 | bytes 16777216 | tf_op jit(solution)/shard_map/pallas_call | solution.py:304
  32.4 0.1 collective-permute-done.1.got_ref
  32.5 0.0 all-to-all-done.1
  32.5 0.8 %shard_map.70 = bf16[16,2048]{1,0:T(8,128)(2,1)} custom-call(bf16[16,64]{1,0:T(8,128)(2,1)S(1)} %get-tuple-element.16.sel_ref, f32[16,2048]{1,0:T(8,128)S(1)} %shard_map.68.keep_ref, f32[16,2048]{1,0:T(8,128)S(1)} %collective-permute-done.1.got_ref, bf16[64,2048]{1,0:T(8,128)(2,1)S(1)} %bitcast.7), custom_call_target="tpu_custom_call" | custom-call | tf_op jit(solution)/shard_map/pallas_call | solution.py:310
Async XLA Ops:
  0.0 9.3 %collective-permute-start = (bf16[32,32768]{1,0:T(8,128)(2,1)}, bf16[32,32768]{1,0:T(8,128)(2,1)S(1)}, u32[]{:S(2)}, u32[]{:S(2)}) collective-permute-start(bf16[32,32768]{1,0:T(8,128)(2,1)} %bitcast.8), channel_id=1, source_target_pairs={{0,1},{1,0},{2,3},{3,2},{4,5},{5,4},{6,7},{7,6},{8,9},{9,8},{10,11... | collective-permute-start | bytes 6291464 | tf_op jit(solution)/shard_map/ppermute | solution.py:228
  1.9 12.7 %all-to-all-start = ((bf16[8,2,4096]{2,1,0:T(2,128)(2,1)}), bf16[8,2,4096]{2,1,0:T(2,128)(2,1)S(1)}, u32[]{:S(2)}, u32[]{:S(2)}) async-start(bf16[8,2,4096]{2,1,0:T(2,128)(2,1)} %broadcast_in_dim.2), calls=%async_computation | async-start | bytes 262144 | tf_op jit(solution)/shard_map/all_to_all | solution.py:231
  9.3 1.3 %copy-start.1 = (bf16[32,32768]{1,0:T(8,128)(2,1)}, bf16[32,32768]{1,0:T(8,128)(2,1)S(1)}, u32[]{:S(2)}) copy-start(bf16[32,32768]{1,0:T(8,128)(2,1)S(1)} %collective-permute-done.upo_ref) | copy-start | bytes 6291460
  14.6 1.6 %copy-start = (bf16[64,16384]{1,0:T(8,128)(2,1)S(1)}, bf16[64,16384]{1,0:T(8,128)(2,1)}, u32[]{:S(2)}) copy-start(bf16[64,16384]{1,0:T(8,128)(2,1)} %get-tuple-element.26.up_ref) | copy-start | bytes 6291460
  14.9 1.2 %collective-permute-start.2 = (f32[16,64]{1,0:T(8,128)S(1)}, f32[16,64]{1,0:T(8,128)S(1)}, u32[]{:S(2)}, u32[]{:S(2)}) collective-permute-start(f32[16,64]{1,0:T(8,128)S(1)} %get-tuple-element.23.x_ref), channel_id=1, source_target_pairs={{0,1},{1,0},{2,3},{3,2},{4,5},{5,4},{6,7},{7,6},{8,9},{9,8},{10,11... | collective-permute-start | bytes 12296 | tf_op jit(solution)/shard_map/ppermute | solution.py:271
  17.4 15.1 %all-to-all-start.1 = ((bf16[8,8,2048]{2,1,0:T(8,128)(2,1)}), bf16[8,8,2048]{2,1,0:T(8,128)(2,1)S(1)}, u32[]{:S(2)}, u32[]{:S(2)}) async-start(bf16[8,8,2048]{2,1,0:T(8,128)(2,1)} %shard_map.69), calls=%async_computation.1 | async-start | bytes 524288 | tf_op jit(solution)/shard_map/all_to_all | solution.py:287
  31.1 1.4 %collective-permute-start.1 = (f32[16,2048]{1,0:T(8,128)S(1)}, f32[16,2048]{1,0:T(8,128)S(1)}, u32[]{:S(2)}, u32[]{:S(2)}) collective-permute-start(f32[16,2048]{1,0:T(8,128)S(1)} %get-tuple-element.22), channel_id=1, source_target_pairs={{0,1},{1,0},{2,3},{3,2},{4,5},{5,4},{6,7},{7,6},{8,9},{9,8},{10,11... | collective-permute-start | bytes 393224 | tf_op jit(solution)/shard_map/ppermute | solution.py:303

commit v11 on v10

--- a/solution.py
+++ b/solution.py
@@ -124,22 +124,17 @@
     )
 
 
-def delta_kernel(x_ref, xo_ref, keep_ref, place_ref, up_ref, acc_ref, out_ref, d_ref, sems):
+def delta_kernel(x_ref, xo_ref, keep_ref, place_ref, up_ref, acc_ref, d_ref):
     batches, _, cols = d_ref.shape
     shrunk = (x_ref[...] + xo_ref[...]).astype(BF16)
     kept = (shrunk.astype(F32) * keep_ref[...]).astype(BF16)
     rows = lax.dot_general(
         place_ref[...], kept, (((0,), (0,)), ((), ())), preferred_element_type=F32
     ).astype(BF16)
-    copies = []
     for d in range(batches):
         d_ref[d] = jnp.dot(
             rows, up_ref[:, d * cols : (d + 1) * cols], preferred_element_type=F32
         ).astype(BF16)
-        copies.append(pltpu.make_async_copy(d_ref.at[d], out_ref.at[d], sems.at[d]))
-        copies[d].start()
-    for c in copies:
-        c.wait()
 
 
 def head_kernel(f_ref, w_ref, acc_ref):
@@ -281,8 +276,6 @@
         delta_kernel,
         [pltpu.HBM((batches, OWN_MOST, cols), BF16)],
         "vvvvva",
-        scratch=[VMEM((batches, OWN_MOST, cols), BF16), dma((batches,))],
-        outs="h",
     )(x, x_other, keep, place, up, acc)
     received = lax.all_to_all(delta, "batch", 0, 0, tiled=True)
     count = blocks - head

time: 33.7 us -> 33.7 us (level)
  no operation moved by 1% of the time
where the time goes in v11:
time: 33.7 us; the launch traced here: 33.3 us
  Pallas kernels  17.6 us (52%)
  starting transfers between devices  11.4 us (34%)
  local copies, waits for them, and re-layouts  2.86 us (8%)
  waiting for transfers between devices  1.46 us (4%)
    pallas_call x1, Pallas kernels, per_device(): call(functools.partial(base_kernel, step, head, count), [half, half, VMEM...  10.2 us
    all_to_all x1, starting transfers between devices, per_device(): lax.all_to_all(sent, 'batch', 0, 0, tiled=True, axis_index_groups=[order_...  7.36 us
    all_to_all x1, starting transfers between devices, per_device(): received = lax.all_to_all(delta, 'batch', 0, 0, tiled=True)  3.46 us
    pallas_call x1, Pallas kernels, per_device(): call(functools.partial(ready_kernel, batches), [shape((requests, wide), F...  3.46 us
    broadcast_in_dim x1, local copies, waits for them, and re-layouts, per_device(): sent = jnp.broadcast_to(features[None], (batches,) + features.shape)  1.44 us
    unnamed x4, local copies, waits for them, and re-layouts  1.43 us
    pallas_call x1, Pallas kernels, per_device(): call(delta_kernel, [pltpu.HBM((batches, OWN_MOST, cols), BF16)], 'vvvvva')  1.26 us
    pallas_call x1, Pallas kernels, per_device(): call(functools.partial(rest_kernel, blocks - later), half, 'vvv', moves(l...  1.18 us
  transfers between devices with their start and end apart: 5, of which 3 were waited for; matrix products, arithmetic and copies ran while one was open for 4% of the time, Pallas kernels for 46%

profile of v11, /device:TPU:0, one launch (start us, length us, event | category | flops | bytes accessed | tf_op | source)
XLA Modules:
  0.0 33.3 jit_solution(9784917474491872134)
XLA Ops:
  0.0 0.5 %collective-permute-start = (bf16[32,32768]{1,0:T(8,128)(2,1)}, bf16[32,32768]{1,0:T(8,128)(2,1)S(1)}, u32[]{:S(2)}, u32[]{:S(2)}) collective-permute-start(bf16[32,32768]{1,0:T(8,128)(2,1)} %bitcast.8), channel_id=1, source_target_pairs={{0,1},{1,0},{2,3},{3,2},{4,5},{5,4},{6,7},{7,6},{8,9},{9,8},{10,11... | collective-permute-start | bytes 6291464 | tf_op jit(solution)/shard_map/ppermute | solution.py:223
  0.5 1.4 %broadcast_in_dim.2 = bf16[8,2,4096]{2,1,0:T(2,128)(2,1)} broadcast(bf16[2,4096]{1,0:T(2,128)(2,1)} %param.6), dimensions={1,2} | broadcast | bytes 147456 | tf_op jit(solution)/shard_map/broadcast_in_dim | solution.py:225
  1.9 7.4 %all-to-all-start = ((bf16[8,2,4096]{2,1,0:T(2,128)(2,1)}), bf16[8,2,4096]{2,1,0:T(2,128)(2,1)S(1)}, u32[]{:S(2)}, u32[]{:S(2)}) async-start(bf16[8,2,4096]{2,1,0:T(2,128)(2,1)} %broadcast_in_dim.2), calls=%async_computation | async-start | bytes 262144 | tf_op jit(solution)/shard_map/all_to_all | solution.py:226
  9.3 0.0 collective-permute-done.upo_ref
  9.3 0.0 copy-start.1
  9.3 1.3 %copy-done.1 = bf16[32,32768]{1,0:T(8,128)(2,1)} copy-done((bf16[32,32768]{1,0:T(8,128)(2,1)}, bf16[32,32768]{1,0:T(8,128)(2,1)S(1)}, u32[]{:S(2)}) %copy-start.1) | copy-done | bytes 2097176
  10.6 3.5 %shard_map.64 = (f32[16,64]{1,0:T(8,128)S(1)}, bf16[16,8]{1,0:T(8,128)(2,1)S(1)}, bf16[16,64]{1,0:T(8,128)(2,1)S(1)}, bf16[64,4096]{1,0:T(8,128)(2,1)S(1)}, bf16...) custom-call(s32[1,16]{1,0:T(1,128)} %bitcast.11, s32[1,32]{1,0:T(1,128)} %bitcast.12, bf16[64,4096]{1,0:T(8,128)(2,1)} %bitcast.10, ...), custom_call_target="tpu_custom_call" | custom-call | bytes 6291456 | tf_op jit(solution)/shard_map/pallas_call | solution.py:231
  14.0 0.5 %all-to-all-done.g_ref = bf16[8,2,4096]{2,1,0:T(2,128)(2,1)S(1)} async-done(((bf16[8,2,4096]{2,1,0:T(2,128)(2,1)}), bf16[8,2,4096]{2,1,0:T(2,128)(2,1)S(1)}, u32[]{:S(2)}, u32[]{:S(2)}) %all-to-all-start) | async-done | bytes 131104 | tf_op jit(solution)/shard_map/all_to_all | solution.py:226
  14.6 0.0 copy-start
  14.6 0.3 shard_map.65
  14.9 0.0 collective-permute-start.2
  14.9 0.4 %shard_map.66.head_ref.acc_ref = f32[16,4096]{1,0:T(8,128)S(1)} custom-call(bf16[16,4096]{1,0:T(8,128)(2,1)S(1)} %get-tuple-element.18.f_ref, bf16[256,4096]{1,0:T(8,128)(2,1)S(1)} %get-tuple-element.19.w_ref), custom_call_target="tpu_custom_call" | custom-call | flops 33554432 | bytes 2097152 | tf_op jit(solution)/shard_map/pallas_call | solution.py:269
  15.3 0.8 %collective-permute-done.2.xo_ref = f32[16,64]{1,0:T(8,128)S(1)} collective-permute-done((f32[16,64]{1,0:T(8,128)S(1)}, f32[16,64]{1,0:T(8,128)S(1)}, u32[]{:S(2)}, u32[]{:S(2)}) %collective-permute-start.2) | collective-permute-done | bytes 4128 | tf_op jit(solution)/shard_map/ppermute | solution.py:266
  16.1 0.1 copy-done
  16.2 1.3 %shard_map.69 = bf16[8,8,2048]{2,1,0:T(8,128)(2,1)} custom-call(f32[16,64]{1,0:T(8,128)S(1)} %get-tuple-element.23.x_ref, f32[16,64]{1,0:T(8,128)S(1)} %collective-permute-done.2.xo_ref, f32[16,64]{1,0:T(8,128)S(1)} %get-tuple-element.24.keep_ref, bf16[16,8]{1,0:T(8,128)(2,1)S(1)} %get-tuple-element.25.place_ref, bf16[64,16384]{1,0:T(8,128)(2,1)S(1)} %copy-done, ...), custom_call_target="tpu_custom_call" | custom-call | tf_op jit(solution)/shard_map/pallas_call | solution.py:275
  17.4 3.5 %all-to-all-start.1 = ((bf16[8,8,2048]{2,1,0:T(8,128)(2,1)}), bf16[8,8,2048]{2,1,0:T(8,128)(2,1)S(1)}, u32[]{:S(2)}, u32[]{:S(2)}) async-start(bf16[8,8,2048]{2,1,0:T(8,128)(2,1)} %shard_map.69), calls=%async_computation.1 | async-start | bytes 524288 | tf_op jit(solution)/shard_map/all_to_all | solution.py:280
  20.9 10.2 %shard_map.67 = (f32[16,2048]{1,0:T(8,128)S(1)}, f32[16,2048]{1,0:T(8,128)S(1)}, bf16[8,256,2048]{2,1,0:T(8,128)(2,1)S(1)}) custom-call(bf16[16,4096]{1,0:T(8,128)(2,1)S(1)} %get-tuple-element.18.f_ref, f32[16,4096]{1,0:T(8,128)S(1)} %shard_map.66.head_ref.acc_ref, bf16[4096,4096]{1,0:T(8,128)(2,1)} %w_ref.3), custom_call_target="tpu_custom_call" | custom-call | flops 503316480 | bytes 31457280 | tf_op jit(solution)/shard_map/pallas_call | solution.py:284
  31.1 0.1 collective-permute-start.1
  31.2 1.2 %shard_map.68.keep_ref = f32[16,2048]{1,0:T(8,128)S(1)} custom-call(bf16[16,4096]{1,0:T(8,128)(2,1)S(1)} %get-tuple-element.18.f_ref, f32[16,2048]{1,0:T(8,128)S(1)} %get-tuple-element.20.mine_ref, bf16[8,256,2048]{2,1,0:T(8,128)(2,1)S(1)} %get-tuple-element.21.w_ref), custom_call_target="tpu_custom_call" | custom-call | flops 268435456 | bytes 16777216 | tf_op jit(solution)/shard_map/pallas_call | solution.py:297
  32.4 0.1 collective-permute-done.1.got_ref
  32.5 0.0 all-to-all-done.1
  32.5 0.8 %shard_map.70 = bf16[16,2048]{1,0:T(8,128)(2,1)} custom-call(bf16[16,64]{1,0:T(8,128)(2,1)S(1)} %get-tuple-element.16.sel_ref, f32[16,2048]{1,0:T(8,128)S(1)} %shard_map.68.keep_ref, f32[16,2048]{1,0:T(8,128)S(1)} %collective-permute-done.1.got_ref, bf16[64,2048]{1,0:T(8,128)(2,1)S(1)} %bitcast.7), custom_call_target="tpu_custom_call" | custom-call | tf_op jit(solution)/shard_map/pallas_call | solution.py:303
Async XLA Ops:
  0.0 9.3 %collective-permute-start = (bf16[32,32768]{1,0:T(8,128)(2,1)}, bf16[32,32768]{1,0:T(8,128)(2,1)S(1)}, u32[]{:S(2)}, u32[]{:S(2)}) collective-permute-start(bf16[32,32768]{1,0:T(8,128)(2,1)} %bitcast.8), channel_id=1, source_target_pairs={{0,1},{1,0},{2,3},{3,2},{4,5},{5,4},{6,7},{7,6},{8,9},{9,8},{10,11... | collective-permute-start | bytes 6291464 | tf_op jit(solution)/shard_map/ppermute | solution.py:223
  1.9 12.7 %all-to-all-start = ((bf16[8,2,4096]{2,1,0:T(2,128)(2,1)}), bf16[8,2,4096]{2,1,0:T(2,128)(2,1)S(1)}, u32[]{:S(2)}, u32[]{:S(2)}) async-start(bf16[8,2,4096]{2,1,0:T(2,128)(2,1)} %broadcast_in_dim.2), calls=%async_computation | async-start | bytes 262144 | tf_op jit(solution)/shard_map/all_to_all | solution.py:226
  9.3 1.3 %copy-start.1 = (bf16[32,32768]{1,0:T(8,128)(2,1)}, bf16[32,32768]{1,0:T(8,128)(2,1)S(1)}, u32[]{:S(2)}) copy-start(bf16[32,32768]{1,0:T(8,128)(2,1)S(1)} %collective-permute-done.upo_ref) | copy-start | bytes 6291460
  14.6 1.6 %copy-start = (bf16[64,16384]{1,0:T(8,128)(2,1)S(1)}, bf16[64,16384]{1,0:T(8,128)(2,1)}, u32[]{:S(2)}) copy-start(bf16[64,16384]{1,0:T(8,128)(2,1)} %get-tuple-element.26.up_ref) | copy-start | bytes 6291460
  14.9 1.2 %collective-permute-start.2 = (f32[16,64]{1,0:T(8,128)S(1)}, f32[16,64]{1,0:T(8,128)S(1)}, u32[]{:S(2)}, u32[]{:S(2)}) collective-permute-start(f32[16,64]{1,0:T(8,128)S(1)} %get-tuple-element.23.x_ref), channel_id=1, source_target_pairs={{0,1},{1,0},{2,3},{3,2},{4,5},{5,4},{6,7},{7,6},{8,9},{9,8},{10,11... | collective-permute-start | bytes 12296 | tf_op jit(solution)/shard_map/ppermute | solution.py:266
  17.4 15.1 %all-to-all-start.1 = ((bf16[8,8,2048]{2,1,0:T(8,128)(2,1)}), bf16[8,8,2048]{2,1,0:T(8,128)(2,1)S(1)}, u32[]{:S(2)}, u32[]{:S(2)}) async-start(bf16[8,8,2048]{2,1,0:T(8,128)(2,1)} %shard_map.69), calls=%async_computation.1 | async-start | bytes 524288 | tf_op jit(solution)/shard_map/all_to_all | solution.py:280
  31.1 1.4 %collective-permute-start.1 = (f32[16,2048]{1,0:T(8,128)S(1)}, f32[16,2048]{1,0:T(8,128)S(1)}, u32[]{:S(2)}, u32[]{:S(2)}) collective-permute-start(f32[16,2048]{1,0:T(8,128)S(1)} %get-tuple-element.22), channel_id=1, source_target_pairs={{0,1},{1,0},{2,3},{3,2},{4,5},{5,4},{6,7},{7,6},{8,9},{9,8},{10,11... | collective-permute-start | bytes 393224 | tf_op jit(solution)/shard_map/ppermute | solution.py:296
